TPU v7x, 32 devices: a whole 2x2x4 slice. The times are simulated.
32 devices in a mesh: gx: 4 (over z), gy: 8 (over y, x, core).
Axes of the slice: x: 2, y: 2, z: 4, core: 2. Of those that a mesh axis runs over, the one named last changes fastest.
Arguments:
- positions: bfloat16 [32, 64, 3, 128], P('gx', 'gy'), may hold values from 0 to 1
- features: bfloat16 [32, 64, 256, 128], P('gx', 'gy'), may hold values from -6 to 6
- lever: float32 [32, 64, 3, 128], P('gx', 'gy'), may hold values from -4 to 4
- partner: int32 [32, 64, 6], P('gx', 'gy'), may hold values from 0 to 8, as said below
- body_slot: int32 [32, 64, 128], P('gx', 'gy'), may hold values from 0 to 127
- owner_dir: int32 [32, 64, 128], P('gx', 'gy'), may hold values from 0 to 8, as said below
- body_pose: float32 [4, 8, 7, 128], P('gx', 'gy'), as said below
- body_motion: float32 [4, 8, 6, 128], P('gx', 'gy'), may hold values from -5 to 5
- body_inverse: float32 [4, 8, 4, 128], P('gx', 'gy'), may hold values from 0.1 to 1
- weight_u: bfloat16 [512, 256], replicated, may hold values from -0.375 to 0.375
- weight_v: bfloat16 [128, 256], replicated, may hold values from -0.375 to 0.375
- radial_rate: float32 [4], replicated, may hold values from 0.5 to 4
Outputs:
- moved: float32 [32, 64, 3, 128], P('gx', 'gy')
- body_next: float32 [4, 8, 13, 128], P('gx', 'gy')
Inputs may be any that keep to these rules, and one draw needn't show every extreme that they name: `partner`: each tile's 6 codes are distinct; code 3 (a + 1) + (b + 1) names the tile a tiles along the first and b along the second dimension, a, b in -1, 0, 1. `owner_dir`: code 3 (a + 1) + (b + 1) names the domain a, b domains away; a is -1 only in a domain's first row of 8 tiles and 1 only in its last, b likewise for its 8 columns. `body_pose`: rows 3 to 6 are unit quaternions with a positive first entry.
All inputs are finite; a program needn't handle non-finite values.
Results may differ from a plain program's by a relative error of at most 0.0023.
Values may be sent and summed in bfloat16 or wider, within the bound.
No kernel may reach another device: no remote copies, remote signals or barrier semaphores. Data moves between devices by JAX's collectives and lax.ppermute only.
A program may use at most 128 MiB of HBM per device.

v0:
```python
import jax
import jax.numpy as jnp
from jax import lax
from jax.sharding import PartitionSpec as P

STEP_DT = 0.25
CUT_SQUARE = 4.0


def from_behind(block, axis, distance):
    devices = range(lax.axis_size(axis))
    route = [((i - distance) % len(devices), i) for i in devices]
    return lax.ppermute(block, axis, route)


def padded_2(value, sides, width):
    for axis, dim in sides:
        devices, length = (lax.axis_size(axis), value.shape[dim])
        up = [(i, (i + 1) % devices) for i in range(devices)]
        down = [(j, i) for i, j in up]
        last = lax.slice_in_dim(value, length - width, length, axis=dim)
        leading = lax.slice_in_dim(value, 0, width, axis=dim)
        before = lax.ppermute(last, axis, up)
        after = lax.ppermute(leading, axis, down)
        value = jnp.concatenate([before, value, after], axis=dim)
    return value


def rotation(quat):
    qw, qa, qb, qc = (quat[0], quat[1], quat[2], quat[3])
    first = jnp.stack(
        [1 - 2 * (qb * qb + qc * qc), 2 * (qa * qb - qw * qc), 2 * (qa * qc + qw * qb)]
    )
    second = jnp.stack(
        [2 * (qa * qb + qw * qc), 1 - 2 * (qa * qa + qc * qc), 2 * (qb * qc - qw * qa)]
    )
    third = jnp.stack(
        [2 * (qa * qc - qw * qb), 2 * (qb * qc + qw * qa), 1 - 2 * (qa * qa + qb * qb)]
    )
    return jnp.stack([first, second, third])


def integrate(pose, motion, inverse, totals):
    centre = pose[0:3]
    quat = pose[3:7]
    new_vel = motion[0:3] + STEP_DT * inverse[0] * totals[0:3]
    new_centre = centre + STEP_DT * new_vel
    new_ang = motion[3:6] + STEP_DT * totals[3:6]
    rot_old = rotation(quat)
    body_frame = jnp.sum(rot_old * new_ang[:, None], axis=0) * inverse[1:4]
    omega = jnp.sum(rot_old * body_frame[None, :], axis=1)
    scalar = -jnp.sum(omega * quat[1:4], axis=0)
    vector = quat[0] * omega + jnp.cross(omega, quat[1:4], axis=0)
    stepped = quat + 0.5 * STEP_DT * jnp.concatenate([scalar[None], vector], axis=0)
    new_quat = stepped / jnp.sqrt(jnp.sum(stepped * stepped, axis=0))
    rot_new = rotation(new_quat)
    relative = jnp.sum(rot_new[:, None, :] * rot_old[None, :, :], axis=2)
    next_state = jnp.concatenate([new_centre, new_quat, new_vel, new_ang], axis=0)
    packed = jnp.concatenate(
        [STEP_DT * new_vel, relative.reshape((9,) + relative.shape[2:])], axis=0
    )
    return (next_state, packed)


def tile_forces(u_row, p_row, v_part, p_part, offset, radial_rate):
    differ = p_row[:, :, :, None] - p_part[:, :, None, :] - offset[:, :, None, None]
    radius_sq = jnp.sum(differ * differ, axis=1)
    envelope = jnp.square(jnp.maximum(1.0 - radius_sq / CUT_SQUARE, 0.0))
    scores = jnp.einsum("mkha,mhb->mkab", u_row, v_part, preferred_element_type=jnp.float32)
    radial = jnp.exp(-radial_rate[None, :, None, None] * radius_sq[:, None])
    couple = envelope * jnp.sum(radial * scores, axis=1) / v_part.shape[1]
    weight_sum = jnp.sum(couple, axis=2)
    pulled = jnp.einsum("mab,mcb->mca", couple, p_part, precision=lax.Precision.HIGHEST)
    return (p_row - offset[:, :, None]) * weight_sum[:, None, :] - pulled


def pick_partner(three_rows, off_x, off_y, tiles_y):
    shape_mask = (-1,) + (1,) * (three_rows.ndim - 2)
    sel_left = (off_y == -1).reshape(shape_mask)
    sel_mid = (off_y == 0).reshape(shape_mask)
    per_row = []
    for row in range(3):
        left = three_rows[row, 0:tiles_y]
        middle = three_rows[row, 1 : tiles_y + 1]
        right = three_rows[row, 2 : tiles_y + 2]
        per_row.append(jnp.where(sel_left, left, jnp.where(sel_mid, middle, right)))
    sel_up = (off_x == -1).reshape(shape_mask)
    sel_same = (off_x == 0).reshape(shape_mask)
    return jnp.where(sel_up, per_row[0], jnp.where(sel_same, per_row[1], per_row[2]))


def along_gy(partial_sums, offset_by):
    return from_behind(partial_sums, "gy", offset_by)


def along_gx(partial_sums, offset_by):
    return from_behind(partial_sums, "gx", offset_by)


def local(
    positions,
    features,
    lever,
    partner,
    body_slot,
    owner_dir,
    body_pose,
    body_motion,
    body_inverse,
    weight_u,
    weight_v,
    radial_rate,
):
    tiles_x, tiles_y = (positions.shape[0], positions.shape[1])
    tile_len = positions.shape[3]
    width_h = weight_v.shape[0]
    channels = weight_u.shape[0] // width_h
    slots = body_pose.shape[3]
    u_all = jnp.einsum(
        "gf,xyfb->xygb", weight_u, features, preferred_element_type=jnp.float32
    ).astype(jnp.bfloat16)
    proj_v = jnp.einsum(
        "hf,xyfb->xyhb", weight_v, features, preferred_element_type=jnp.float32
    ).astype(jnp.bfloat16)
    state = jnp.concatenate([positions, proj_v], axis=2)
    padded = padded_2(state, (("gx", 0), ("gy", 1)), 1)
    pad_v = padded[:, :, 3:]
    pad_pos = padded[:, :, 0:3].astype(jnp.float32)

    def row_forces(inputs):
        row_index, u_row, p_row, codes = inputs
        rows_v = lax.dynamic_slice_in_dim(pad_v, row_index, 3, 0)
        rows_p = lax.dynamic_slice_in_dim(pad_pos, row_index, 3, 0)
        total = jnp.zeros((tiles_y, 3, tile_len), jnp.float32)
        for which in range(codes.shape[1]):
            code = codes[:, which]
            off_x = code // 3 - 1
            off_y = code % 3 - 1
            v_part = pick_partner(rows_v, off_x, off_y, tiles_y)
            p_part = pick_partner(rows_p, off_x, off_y, tiles_y)
            offset = jnp.stack([off_x, off_y, jnp.zeros_like(off_x)], axis=1).astype(jnp.float32)
            total = total + tile_forces(u_row, p_row, v_part, p_part, offset, radial_rate)
        return total

    forces = lax.map(
        row_forces,
        (
            jnp.arange(tiles_x, dtype=jnp.int32),
            u_all.reshape(tiles_x, tiles_y, channels, width_h, tile_len),
            positions.astype(jnp.float32),
            partner,
        ),
    )
    torque = jnp.cross(lever, forces, axis=2)
    terms = jnp.concatenate([forces, torque], axis=2)
    body_key = (owner_dir * slots + body_slot).reshape(tiles_x, tiles_y * tile_len)
    term_rows = jnp.moveaxis(terms, 2, 1).reshape(tiles_x, 6, tiles_y * tile_len)
    segment_ids = jnp.arange(9 * slots, dtype=jnp.int32)

    def row_sums(inputs):
        keys, term_row = inputs
        onehot = (keys[:, None] == segment_ids[None, :]).astype(jnp.float32)
        return jnp.dot(term_row, onehot, precision=lax.Precision.HIGHEST)

    sums = jnp.sum(lax.map(row_sums, (body_key, term_rows)), axis=0)
    parts = jnp.transpose(sums.reshape(6, 3, 3, slots), (1, 2, 0, 3))
    section_one = parts[:, 1] + along_gy(parts[:, 2], 1) + along_gy(parts[:, 0], -1)
    totals = section_one[1] + along_gx(section_one[2], 1) + along_gx(section_one[0], -1)
    next_state, packed = integrate(body_pose[0, 0], body_motion[0, 0], body_inverse[0, 0], totals)
    beside_all = padded_2(packed[None, None], (("gx", 0), ("gy", 1)), 1)
    table = jnp.transpose(beside_all, (2, 0, 1, 3)).reshape(12, 9 * slots)

    def row_lookup(keys):
        onehot = (keys[:, None] == segment_ids[None, :]).astype(jnp.float32)
        picked = jnp.einsum("gs,bs->gb", table, onehot, precision=lax.Precision.HIGHEST)
        return jnp.moveaxis(picked.reshape(12, tiles_y, tile_len), 0, 1)

    looked = lax.map(row_lookup, body_key)
    rotated = jnp.stack(
        [jnp.sum(looked[:, :, 3 + 3 * row : 6 + 3 * row] * lever, axis=2) for row in range(3)],
        axis=2,
    )
    moved = positions.astype(jnp.float32) + looked[:, :, 0:3] + rotated - lever
    return (moved, next_state[None, None])


def solution(mesh):
    placed = (
        P("gx", "gy", None, None),
        P("gx", "gy", None, None),
        P("gx", "gy", None, None),
        P("gx", "gy", None),
        P("gx", "gy", None),
        P("gx", "gy", None),
        P("gx", "gy", None, None),
        P("gx", "gy", None, None),
        P("gx", "gy", None, None),
        P(),
        P(),
        P(),
    )
    return jax.shard_map(
        local,
        mesh=mesh,
        in_specs=placed,
        out_specs=(P("gx", "gy", None, None), P("gx", "gy", None, None)),
        check_vma=False,
    )
```

profile of v0, /device:TPU:0, one launch (start us, length us, event | category | flops | bytes accessed | tf_op | source)
XLA Modules:
  0.0 285.6 jit_solution(9166484531618088728)
XLA Ops:
  1.5 3.1 %convert_bitcast_fusion.1 = bf16[8,8,128,128]{3,2,1,0:T(8,128)(2,1)S(1)} fusion(bf16[8,8,256,128]{3,2,1,0:T(8,128)(2,1)} %param.19, bf16[128,256]{1,0:T(8,128)(2,1)} %param.28), kind=kOutput, calls=%fused_computation.311 | convolution fusion | flops 537919488 | bytes 6356992 | tf_op jit(solution)/shard_map/hf,xyfb->xyhb/dot_general | solution.py:122
  4.8 3.1 %collective-permute-start = (bf16[1,8,131,128]{3,2,1,0:T(8,128)(2,1)S(1)}, bf16[1,8,131,128]{3,2,1,0:T(8,128)(2,1)S(1)}, u32[]{:S(2)}, u32[]{:S(2)}) collective-permute-start(bf16[1,8,131,128]{3,2,1,0:T(8,128)(2,1)S(1)} %get-tuple-element.430), channel_id=1, source_target_pairs={{0,8},{8,16},{16,24},{24,0},{1,9},{9,17},{17,25},{25,1},{2,10},{10... | collective-permute-start | bytes 804872 | tf_op jit(solution)/shard_map/ppermute | solution.py:23
  10.0 5.6 %convert_bitcast_fusion = bf16[8,8,512,128]{2,3,1,0:T(8,128)(2,1)} fusion(bf16[8,8,256,128]{3,2,1,0:T(8,128)(2,1)S(1)} %copy-done.1, bf16[512,256]{1,0:T(8,128)(2,1)S(1)} %copy-done), kind=kOutput, calls=%fused_computation.305 | convolution fusion | flops 2151677952 | bytes 12845056 | tf_op jit(solution)/shard_map/gf,xyfb->xygb/dot_general | solution.py:119
  18.1 3.9 %collective-permute-done.1 = bf16[1,8,131,128]{3,2,1,0:T(8,128)(2,1)S(1)} collective-permute-done((bf16[1,8,131,128]{3,2,1,0:T(8,128)(2,1)S(1)}, bf16[1,8,131,128]{3,2,1,0:T(8,128)(2,1)S(1)}, u32[]{:S(2)}, u32[]{:S(2)}) %collective-permute-start.1) | collective-permute-done | bytes 268320 | tf_op jit(solution)/shard_map/ppermute | solution.py:24
  23.0 2.6 collective-permute-start.3
  26.9 12.6 %reshape.1800 = bf16[8,8,4,128,128]{3,2,4,1,0:T(4,128)(2,1)} reshape(bf16[8,8,512,128]{2,3,1,0:T(8,128)(2,1)} %convert_bitcast_fusion) | data formatting | bytes 16777216 | tf_op jit(solution)/shard_map/reshape | solution.py:149
  40.1 3.7 %pad_maximum_fusion = bf16[10,10,128,128]{3,2,1,0:T(8,128)(2,1)} fusion(bf16[10,1,131,128]{3,2,1,0:T(8,128)(2,1)} %collective-permute-done.3, bf16[10,1,131,128]{3,2,1,0:T(8,128)(2,1)S(1)} %collective-permute-done.2, bf16[1,8,131,128]{3,2,1,0:T(8,128)(2,1)S(1)} %collective-permute-done.1, bf16[1,8,131,128]{3,2,1,0:T(8,128)(2,1)S(1)} %collective-permute-done, ...), kind=kLoop, calls=%fused_computation.306 | loop fusion | flops 19660800 | bytes 6630400 | tf_op jit(solution)/shard_map/concatenate | solution.py:25
  44.6 174.6 %while.35 = (s32[]{:T(128)}, f32[8,8,3,128]{3,2,1,0:T(4,128)}, f32[8,8,3,128]{3,1,2,0:T(8,128)}, s32[8,8,6]{1,0,2:T(8,128)}, s32[8]{0:T(128)S(1)}, /*index=5*/f3...) while((s32[]{:T(128)}, f32[8,8,3,128]{3,2,1,0:T(4,128)}, ...), condition=%wide.region_19.20_spmd, body=%wide.region_0.19_spmd.sunk | while | flops 867648384 | bytes 58460052 | solution.py:145
  50.2 2.3 multiply_reduce_fusion.26
  72.0 2.3 multiply_reduce_fusion.26
  93.8 2.3 multiply_reduce_fusion.26
  115.6 2.3 multiply_reduce_fusion.26
  137.4 2.3 multiply_reduce_fusion.26
  159.2 2.3 multiply_reduce_fusion.26
  181.0 2.3 multiply_reduce_fusion.26
  202.8 2.3 multiply_reduce_fusion.26
  221.3 19.0 %while.36 = (s32[]{:T(128)}, f32[8,6,1152]{2,1,0:T(8,128)S(1)}, f32[8,6,1024]{2,1,0:T(8,128)S(1)}, s32[8,1024]{1,0:T(8,128)}, s32[]{:T(128)}) while((s32[]{:T(128)}, f32[8,6,1152]{2,1,0:T(8,128)S(1)}, f32[8,6,1024]{2,1,0:T(8,128)S(1)}, s32[8,1024]{1,0:T(8,128)}, s32[]{:T(128)}) %tuple.224), condition=%wide.region_21.22_spmd.clone, body=%wide.region_20.21_spmd.clone.sunk | while | flops 86114304 | bytes 83009 | solution.py:165
  240.4 2.6 collective-permute-start.5
  245.6 2.7 collective-permute-start.7
  250.4 3.8 %collective-permute-start.9 = (f32[1,1,12,128]{3,2,1,0:T(8,128)S(1)}, f32[1,1,12,128]{3,2,1,0:T(8,128)S(1)}, u32[]{:S(2)}, u32[]{:S(2)}) collective-permute-start(f32[1,1,12,128]{3,2,1,0:T(8,128)S(1)} %maximum_bitcast_fusion.3), channel_id=1, source_target_pairs={{8,0},{16,8},{24,16},{0,24},{9,1},{17,9},{25,17},{1,25},{10,2},{18... | collective-permute-start | bytes 18440 | tf_op jit(solution)/shard_map/ppermute | solution.py:24
  255.9 2.6 collective-permute-start.11
  260.3 24.6 %while.37 = (s32[]{:T(128)}, f32[8,8,12,128]{3,1,2,0:T(8,128)S(1)}, s32[8,1024]{1,0:T(8,128)}, f32[12,1152]{1,0:T(8,128)S(1)}, s32[]{:T(128)}) while((s32[]{:T(128)}, f32[8,8,12,128]{3,1,2,0:T(8,128)S(1)}, s32[8,1024]{1,0:T(8,128)}, f32[12,1152]{1,0:T(8,128)S(1)}, s32[]{:T(128)}) %tuple.225), condition=%wide.region_29.30_spmd.clone, body=%wide.region_28.29_spmd.clone.sunk | while | flops 171048960 | bytes 346181 | solution.py:178
  270.3 2.2 fusion.275
  273.4 2.2 fusion.275
  (582 shorter events, 199.2 us)
Async XLA Ops:
  4.8 13.3 %collective-permute-start = (bf16[1,8,131,128]{3,2,1,0:T(8,128)(2,1)S(1)}, bf16[1,8,131,128]{3,2,1,0:T(8,128)(2,1)S(1)}, u32[]{:S(2)}, u32[]{:S(2)}) collective-permute-start(bf16[1,8,131,128]{3,2,1,0:T(8,128)(2,1)S(1)} %get-tuple-element.430), channel_id=1, source_target_pairs={{0,8},{8,16},{16,24},{24,0},{1,9},{9,17},{17,25},{25,1},{2,10},{10... | collective-permute-start | bytes 804872 | tf_op jit(solution)/shard_map/ppermute | solution.py:23
  7.9 14.1 %collective-permute-start.1 = (bf16[1,8,131,128]{3,2,1,0:T(8,128)(2,1)S(1)}, bf16[1,8,131,128]{3,2,1,0:T(8,128)(2,1)S(1)}, u32[]{:S(2)}, u32[]{:S(2)}) collective-permute-start(bf16[1,8,131,128]{3,2,1,0:T(8,128)(2,1)S(1)} %get-tuple-element.431), channel_id=1, source_target_pairs={{8,0},{16,8},{24,16},{0,24},{9,1},{17,9},{25,17},{1,25},{10,2},{18... | collective-permute-start | bytes 804872 | tf_op jit(solution)/shard_map/ppermute | solution.py:24
  23.0 17.0 %collective-permute-start.2 = (bf16[10,1,131,128]{3,2,1,0:T(8,128)(2,1)}, bf16[10,1,131,128]{3,2,1,0:T(8,128)(2,1)S(1)}, u32[]{:S(2)}, u32[]{:S(2)}) collective-permute-start(bf16[10,1,131,128]{3,2,1,0:T(8,128)(2,1)} %get-tuple-element.428), channel_id=1, source_target_pairs={{0,1},{1,2},{2,3},{3,4},{4,5},{5,6},{6,7},{7,0},{8,9},{9,10},{10,1... | collective-permute-start | bytes 1006088 | tf_op jit(solution)/shard_map/ppermute | solution.py:23
  23.0 17.1 %collective-permute-start.3 = (bf16[10,1,131,128]{3,2,1,0:T(8,128)(2,1)}, bf16[10,1,131,128]{3,2,1,0:T(8,128)(2,1)}, u32[]{:S(2)}, u32[]{:S(2)}) collective-permute-start(bf16[10,1,131,128]{3,2,1,0:T(8,128)(2,1)} %get-tuple-element.429), channel_id=1, source_target_pairs={{1,0},{2,1},{3,2},{4,3},{5,4},{6,5},{7,6},{0,7},{9,8},{10,9},{11,1... | collective-permute-start | bytes 1006088 | tf_op jit(solution)/shard_map/ppermute | solution.py:24
  44.5 174.6 %copy-start.3 = (f32[8,8,3,128]{3,1,2,0:T(8,128)S(1)}, f32[8,8,3,128]{3,1,2,0:T(8,128)}, u32[]{:S(2)}) copy-start(f32[8,8,3,128]{3,1,2,0:T(8,128)} %param.20) | copy-start | bytes 294916
  44.5 176.6 %copy-start.6 = (f32[8,6,1152]{2,1,0:T(8,128)S(1)}, f32[8,6,1152]{2,1,0:T(8,128)}, u32[]{:S(2)}) copy-start(f32[8,6,1152]{2,1,0:T(8,128)} %custom-call.1) | copy-start | bytes 663556
  221.2 21.9 %copy-start.11 = (f32[1,128]{1,0:T(1,128)S(1)}, f32[1,128]{1,0:T(1,128)}, u32[]{:S(2)}) copy-start(f32[1,128]{1,0:T(1,128)} %get-tuple-element.448) | copy-start | bytes 1540
  221.2 21.9 %copy-start.12 = (f32[1,128]{1,0:T(1,128)S(1)}, f32[1,128]{1,0:T(1,128)}, u32[]{:S(2)}) copy-start(f32[1,128]{1,0:T(1,128)} %get-tuple-element.449) | copy-start | bytes 1540
  221.2 21.9 %copy-start.13 = (f32[1,128]{1,0:T(1,128)S(1)}, f32[1,128]{1,0:T(1,128)}, u32[]{:S(2)}) copy-start(f32[1,128]{1,0:T(1,128)} %get-tuple-element.452) | copy-start | bytes 1540
  221.2 27.1 %copy-start.16 = (f32[1,128]{1,0:T(1,128)S(1)}, f32[1,128]{1,0:T(1,128)}, u32[]{:S(2)}) copy-start(f32[1,128]{1,0:T(1,128)} %get-tuple-element.450) | copy-start | bytes 1540
  221.3 27.1 %copy-start.17 = (f32[1,128]{1,0:T(1,128)S(1)}, f32[1,128]{1,0:T(1,128)}, u32[]{:S(2)}) copy-start(f32[1,128]{1,0:T(1,128)} %get-tuple-element.451) | copy-start | bytes 1540
  221.3 27.1 %copy-start.21 = (f32[1,128]{1,0:T(1,128)S(1)}, f32[1,128]{1,0:T(1,128)}, u32[]{:S(2)}) copy-start(f32[1,128]{1,0:T(1,128)} %get-tuple-element.455) | copy-start | bytes 1540
  221.3 28.6 %copy-start.22 = (f32[128]{0:T(128)S(1)}, f32[128]{0:T(128)}, u32[]{:S(2)}) copy-start(f32[128]{0:T(128)} %multiply_bitcast_fusion.6) | copy-start | bytes 1540
  221.3 28.7 %copy-start.14 = (f32[1,1,4,128]{3,2,1,0:T(4,128)S(1)}, f32[1,1,4,128]{3,2,1,0:T(4,128)}, u32[]{:S(2)}) copy-start(f32[1,1,4,128]{3,2,1,0:T(4,128)} %param.26) | copy-start | bytes 6148
  221.3 28.7 %copy-start.15 = (f32[128]{0:T(128)S(1)}, f32[128]{0:T(128)}, u32[]{:S(2)}) copy-start(f32[128]{0:T(128)} %get-tuple-element.447) | copy-start | bytes 1540
  240.4 4.1 %collective-permute-start.4 = (f32[3,6,128]{2,1,0:T(8,128)S(1)}, f32[3,6,128]{2,1,0:T(8,128)S(1)}, u32[]{:S(2)}, u32[]{:S(2)}) collective-permute-start(f32[3,6,128]{2,1,0:T(8,128)S(1)} %get-tuple-element.435), channel_id=1, source_target_pairs={{7,0},{0,1},{1,2},{2,3},{3,4},{4,5},{5,6},{6,7},{15,8},{8,9},{9,10... | collective-permute-start | bytes 27656 | tf_op jit(solution)/shard_map/ppermute | solution.py:13
  240.4 4.0 %collective-permute-start.5 = (f32[3,6,128]{2,1,0:T(8,128)S(1)}, f32[3,6,128]{2,1,0:T(8,128)S(1)}, u32[]{:S(2)}, u32[]{:S(2)}) collective-permute-start(f32[3,6,128]{2,1,0:T(8,128)S(1)} %get-tuple-element.436), channel_id=1, source_target_pairs={{1,0},{2,1},{3,2},{4,3},{5,4},{6,5},{7,6},{0,7},{9,8},{10,9},{11,1... | collective-permute-start | bytes 27656 | tf_op jit(solution)/shard_map/ppermute | solution.py:13
  244.5 5.4 %collective-permute-start.6 = (f32[6,128]{1,0:T(8,128)S(1)}, f32[6,128]{1,0:T(8,128)S(1)}, u32[]{:S(2)}, u32[]{:S(2)}) collective-permute-start(f32[6,128]{1,0:T(8,128)S(1)} %get-tuple-element.437), channel_id=1, source_target_pairs={{24,0},{0,8},{8,16},{16,24},{25,1},{1,9},{9,17},{17,25},{26,2},{2,... | collective-permute-start | bytes 9224 | tf_op jit(solution)/shard_map/ppermute | solution.py:13
  245.6 4.3 %collective-permute-start.7 = (f32[6,128]{1,0:T(8,128)S(1)}, f32[6,128]{1,0:T(8,128)S(1)}, u32[]{:S(2)}, u32[]{:S(2)}) collective-permute-start(f32[6,128]{1,0:T(8,128)S(1)} %get-tuple-element.438), channel_id=1, source_target_pairs={{8,0},{16,8},{24,16},{0,24},{9,1},{17,9},{25,17},{1,25},{10,2},{18... | collective-permute-start | bytes 9224 | tf_op jit(solution)/shard_map/ppermute | solution.py:13
  250.3 5.5 %collective-permute-start.8 = (f32[1,1,12,128]{3,2,1,0:T(8,128)S(1)}, f32[1,1,12,128]{3,2,1,0:T(8,128)S(1)}, u32[]{:S(2)}, u32[]{:S(2)}) collective-permute-start(f32[1,1,12,128]{3,2,1,0:T(8,128)S(1)} %maximum_bitcast_fusion.3), channel_id=1, source_target_pairs={{0,8},{8,16},{16,24},{24,0},{1,9},{9,17},{17,25},{25,1},{2,10},{10... | collective-permute-start | bytes 18440 | tf_op jit(solution)/shard_map/ppermute | solution.py:23
  250.4 5.4 %collective-permute-start.9 = (f32[1,1,12,128]{3,2,1,0:T(8,128)S(1)}, f32[1,1,12,128]{3,2,1,0:T(8,128)S(1)}, u32[]{:S(2)}, u32[]{:S(2)}) collective-permute-start(f32[1,1,12,128]{3,2,1,0:T(8,128)S(1)} %maximum_bitcast_fusion.3), channel_id=1, source_target_pairs={{8,0},{16,8},{24,16},{0,24},{9,1},{17,9},{25,17},{1,25},{10,2},{18... | collective-permute-start | bytes 18440 | tf_op jit(solution)/shard_map/ppermute | solution.py:24
  255.8 4.4 %collective-permute-start.10 = (f32[3,1,12,128]{3,2,1,0:T(8,128)S(1)}, f32[3,1,12,128]{3,2,1,0:T(8,128)S(1)}, u32[]{:S(2)}, u32[]{:S(2)}) collective-permute-start(f32[3,1,12,128]{3,2,1,0:T(8,128)S(1)} %pad_maximum_fusion.11), channel_id=1, source_target_pairs={{0,1},{1,2},{2,3},{3,4},{4,5},{5,6},{6,7},{7,0},{8,9},{9,10},{10,1... | collective-permute-start | bytes 55304 | tf_op jit(solution)/shard_map/ppermute | solution.py:23
  255.9 4.3 %collective-permute-start.11 = (f32[3,1,12,128]{3,2,1,0:T(8,128)S(1)}, f32[3,1,12,128]{3,2,1,0:T(8,128)S(1)}, u32[]{:S(2)}, u32[]{:S(2)}) collective-permute-start(f32[3,1,12,128]{3,2,1,0:T(8,128)S(1)} %pad_maximum_fusion.11), channel_id=1, source_target_pairs={{1,0},{2,1},{3,2},{4,3},{5,4},{6,5},{7,6},{0,7},{9,8},{10,9},{11,1... | collective-permute-start | bytes 55304 | tf_op jit(solution)/shard_map/ppermute | solution.py:24
  260.3 24.7 %copy-start.5 = (bf16[8,8,3,128]{3,1,2,0:T(8,128)(2,1)S(1)}, bf16[8,8,3,128]{3,1,2,0:T(8,128)(2,1)}, u32[]{:S(2)}) copy-start(bf16[8,8,3,128]{3,1,2,0:T(8,128)(2,1)} %param.18) | copy-start | bytes 147460
  (27 other events, 209.1 us)
where the time goes:
time: 289 us; the launch traced here: 286 us
  matrix products  128 us (44%)
  local copies, waits for them, and re-layouts  58.2 us (20%)
  other arithmetic  51.7 us (18%)
  starting transfers between devices  21 us (7%)
  loops' own time  16.2 us (6%)
  waiting for transfers between devices  9.45 us (3%)
    dot_general x48, matrix products, tile_forces(): jnp.einsum('mab,mcb->mca', couple, p_part, precision=lax.Precision.HIGHEST)  50.3 us
    dot_general x48, matrix products, tile_forces(): jnp.einsum('mkha,mhb->mkab', u_row, v_part, preferred_element_type=jnp.fl...  38.2 us
    dynamic_slice x48, local copies, waits for them, and re-layouts, local(): lax.map(row_forces, (jnp.arange(tiles_x, dtype=jnp.int32), u_all.reshape(...  29.8 us
    reduce_sum x8, other arithmetic, tile_forces(): radius_sq = jnp.sum(differ * differ, axis=1)  18.3 us
    dot_general x8, matrix products, row_lookup(): jnp.einsum('gs,bs->gb', table, onehot, precision=lax.Precision.HIGHEST)  17.9 us
    another operation x1, loops' own time, local(): lax.map(row_forces, (jnp.arange(tiles_x, dtype=jnp.int32), u_all.reshape(...  15.9 us
    dot_general x8, matrix products, row_sums(): return jnp.dot(term_row, onehot, precision=lax.Precision.HIGHEST)  12.8 us
    reshape x1, local copies, waits for them, and re-layouts, local(): u_all.reshape(tiles_x, tiles_y, channels, width_h, tile_len)  12.6 us
  transfers between devices with their start and end apart: 12, of which 5 were waited for; matrix products, arithmetic and copies ran while one was open for 8% of the time, Pallas kernels for 0%

commit v1 on v0

v1 whole, which is shorter than its diff:
```python
import math
import jax
import jax.numpy as jnp
from jax import lax
from jax.experimental import pallas as pl
from jax.experimental.pallas import tpu as pltpu
from jax.sharding import PartitionSpec as P

STEP_DT = 0.25
CUT_SQUARE = 4.0
F32 = jnp.float32
BF16 = jnp.bfloat16
VMEM = pl.BlockSpec(memory_space=pltpu.VMEM)
SMEM = pl.BlockSpec(memory_space=pltpu.SMEM)
HBM = pl.BlockSpec(memory_space=pl.ANY)
LIMIT = 56 * 2**20
DIRS = [(-1, -1), (-1, 0), (-1, 1), (0, -1), (0, 1), (1, -1), (1, 0), (1, 1)]
EXTRA = 16


def rows_iota(rows, lanes):
    return lax.broadcasted_iota(jnp.int32, (rows, lanes), 0)


def split_two(value):
    high = value.astype(BF16)
    return high, (value - high.astype(F32)).astype(BF16)


def one_hot(keys, slots, base):
    hit = rows_iota(slots, keys.shape[-1]) == keys - base
    return jnp.where(hit, 1.0, 0.0).astype(BF16)


def project_kernel(feat, pos, weight_v, own, top, bottom, left, right, c0, c1, c2, c3):
    x = pl.program_id(0)
    last_x = pl.num_programs(0) - 1
    tiles_y, beads = feat.shape[1], feat.shape[3]
    row = rows_iota(8, beads)
    for y in range(0, tiles_y, 2):
        both = jnp.concatenate([feat[0, y], feat[0, y + 1]], axis=1)
        v = jnp.dot(weight_v[...], both, preferred_element_type=F32).astype(BF16)
        for e in range(2):
            own[0, y + e, 0:beads, :] = v[:, e * beads : (e + 1) * beads].T
            p = pos[0, y + e].astype(F32)
            px, py, pz = (jnp.broadcast_to(p[c : c + 1], (8, beads)) for c in range(3))
            norm = -0.25 * (px * px + py * py + pz * pz)
            n1 = norm.astype(BF16).astype(F32)
            n2 = (norm - n1).astype(BF16).astype(F32)
            n3 = norm - n1 - n2
            first = px
            for r, val in ((1, py), (2, pz), (3, px), (4, py), (5, n1), (6, n2), (7, n3)):
                first = jnp.where(row == r, val, first)
            second = jnp.where(row < 3, 1.0, 0.0)
            own[0, y + e, beads : beads + EXTRA, :] = jnp.concatenate(
                [first, second], axis=0
            ).astype(BF16)
    left[0] = own[0, 0]
    right[0] = own[0, tiles_y - 1]

    @pl.when(x == 0)
    def _():
        top[...] = own[0]
        c0[...] = own[0, 0]
        c1[...] = own[0, tiles_y - 1]

    @pl.when(x == last_x)
    def _():
        bottom[...] = own[0]
        c2[...] = own[0, 0]
        c3[...] = own[0, tiles_y - 1]


def project(features, positions, weight_v):
    tx, ty, f, beads = features.shape
    rows = beads + EXTRA
    fixed3 = lambda s: pl.BlockSpec(s, lambda i: (0, 0, 0))
    fixed2 = lambda s: pl.BlockSpec(s, lambda i: (0, 0))
    sds = lambda *s: jax.ShapeDtypeStruct(s, BF16)
    return pl.pallas_call(
        project_kernel,
        grid=(tx,),
        out_shape=[sds(tx, ty, rows, beads), sds(ty, rows, beads), sds(ty, rows, beads),
                   sds(tx, rows, beads), sds(tx, rows, beads)] + [sds(rows, beads)] * 4,
        in_specs=[
            pl.BlockSpec((1, ty, f, beads), lambda i: (i, 0, 0, 0)),
            pl.BlockSpec((1, ty, 3, beads), lambda i: (i, 0, 0, 0)),
            fixed2(weight_v.shape),
        ],
        out_specs=[
            pl.BlockSpec((1, ty, rows, beads), lambda i: (i, 0, 0, 0)),
            fixed3((ty, rows, beads)), fixed3((ty, rows, beads)),
            pl.BlockSpec((1, rows, beads), lambda i: (i, 0, 0)),
            pl.BlockSpec((1, rows, beads), lambda i: (i, 0, 0)),
        ] + [fixed2((rows, beads))] * 4,
        compiler_params=pltpu.CompilerParams(vmem_limit_bytes=LIMIT),
    )(features, positions, weight_v)


def pairs_kernel(tiles, halo, shape, *refs):
    n = len(tiles)
    tx, ty, beads, width_h, chans, nb, slots = shape
    refs = list(refs)
    take = lambda k: [refs.pop(0) for _ in range(k)]
    ids, partner, rate, features, weight_u, lever, slot, owner, own = take(9)
    around = take(8) if halo else []
    sums = refs.pop(0)
    sent = take(8) if halo else []
    feat, ub, sa, sb, za, zb, ca, cb, wz, fsem = take(10)
    terms, vp, vsem = take(3) if halo else (None, own, None)
    org = 1 if halo else 0
    side = chans * width_h

    for q, (i, j) in enumerate(tiles):
        pltpu.make_async_copy(features.at[i, j], feat.at[q], fsem.at[q]).start()
    if halo:
        places = [vp.at[0, 0], vp.at[0, 1 : ty + 1], vp.at[0, ty + 1], vp.at[1 : tx + 1, 0],
                  vp.at[1 : tx + 1, ty + 1], vp.at[tx + 1, 0], vp.at[tx + 1, 1 : ty + 1],
                  vp.at[tx + 1, ty + 1], vp.at[1 : tx + 1, 1 : ty + 1]]
        copies = [pltpu.make_async_copy(src, dst, vsem.at[q])
                  for q, (src, dst) in enumerate(zip(around + [own], places))]
        for copy in copies:
            copy.start()
    wz[...] = jnp.zeros_like(wz)
    sums[...] = jnp.zeros_like(sums)
    row8 = rows_iota(8, beads)
    row16 = rows_iota(16, beads)

    def wait_feat(t):
        pltpu.make_async_copy(features.at[0, 0], feat.at[t], fsem.at[t]).wait()

    def where_is(t):
        return ids[t] // ty, ids[t] % ty

    def codes(i, j, m):
        code = partner[i, j, m]
        a = lax.shift_right_logical(code * 11, 5)
        return a - 1, code - 3 * a - 1

    def make_u(s):
        both = jnp.concatenate([feat[2 * s], feat[2 * s + 1]], axis=1)
        u = jnp.dot(weight_u[...], both, preferred_element_type=F32).astype(BF16)
        for e in range(2):
            for k in range(chans):
                ub[e, :, k * beads : (k + 1) * beads] = u[
                    k * width_h : (k + 1) * width_h, e * beads : (e + 1) * beads]

    def scores(t, e, buf, zbuf):
        i, j = where_is(t)
        lhs, feats = [], []
        mine = vp[i + org, j + org, beads : beads + EXTRA, :].astype(F32)
        up = mine[0:8]
        bx, by = (jnp.broadcast_to(up[c : c + 1], (8, beads)) for c in (0, 1))
        bn = jnp.broadcast_to(up[5:6] + up[6:7] + up[7:8], (8, beads))
        fixed = jnp.where(row8 < 3, 0.5 * up, jnp.where(row8 >= 5, 1.0, 0.0))
        for m in range(nb):
            a, b = codes(i, j, m)
            lhs.append(vp[i + a + org, j + b + org, 0:beads, :])
            feats.append(vp[i + a + org, j + b + org, beads : beads + EXTRA, :])
            af, bf = a.astype(F32), b.astype(F32)
            high = jnp.where(row8 == 3, -0.5 * af, jnp.where(row8 == 4, -0.5 * bf, fixed))
            norm = bn + bx * (0.5 * af) + by * (0.5 * bf) - 0.25 * (af * af + bf * bf)
            n1 = norm.astype(BF16).astype(F32)
            rest = norm - n1
            n2 = rest.astype(BF16).astype(F32)
            low = jnp.where(row8 == 0, n1, jnp.where(row8 == 1, n2, jnp.where(row8 == 2, rest - n2, 0.0)))
            wz[m // 2, EXTRA * (m % 2) : EXTRA * (m % 2 + 1), (m % 2) * beads : (m % 2 + 1) * beads] = (
                jnp.concatenate([high, low], axis=0).astype(BF16))
        for h in range(nb // 2):
            left = jnp.concatenate([feats[2 * h], feats[2 * h + 1]], axis=0)
            zbuf[h] = lax.dot_general(left, wz[h], (((0,), (0,)), ((), ())), preferred_element_type=F32)
        buf[...] = jnp.dot(jnp.concatenate(lhs, axis=0), ub[e], preferred_element_type=F32)

    def couples(buf, zbuf, cbuf):
        step = 16
        for m in range(nb):
            for r in range(0, beads, step):
                z = zbuf[m // 2, r : r + step, (m % 2) * beads : (m % 2 + 1) * beads]
                env = jnp.maximum(1.0 + z, 0.0)
                total = None
                for k in range(chans):
                    part = jnp.exp2(z * (rate[k] * (CUT_SQUARE / math.log(2.0)))) * buf[
                        m * beads + r : m * beads + r + step, k * beads : (k + 1) * beads]
                    total = part if total is None else total + part
                cbuf[m * beads + r : m * beads + r + step, :] = ((env * env) * total).astype(BF16)

    def gather(t, cbuf):
        i, j = where_is(t)
        lhs = []
        for m in range(nb):
            a, b = codes(i, j, m)
            base = vp[i + a + org, j + b + org, beads : beads + EXTRA, :]
            extra = jnp.where(row16 == 11, a.astype(F32), jnp.where(row16 == 12, b.astype(F32), 0.0))
            lhs.append(base + extra.astype(BF16))
        out = jnp.dot(jnp.concatenate(lhs, axis=1), cbuf[...], preferred_element_type=F32)
        out = out * (1.0 / width_h)
        mine = vp[i + org, j + org, beads : beads + EXTRA, :].astype(F32)
        w = out[8:9]
        fx = mine[0:1] * w - out[0:1] - out[11:12]
        fy = mine[1:2] * w - out[1:2] - out[12:13]
        fz = mine[2:3] * w - out[2:3]
        lev = lever[i, j]
        lx, ly, lz = lev[0:1], lev[1:2], lev[2:3]
        value = jnp.concatenate(
            [fx, fy, fz, ly * fz - lz * fy, lz * fx - lx * fz, lx * fy - ly * fx,
             jnp.zeros((2, beads), F32)], axis=0)
        term = jnp.concatenate(split_two(value), axis=0)
        if halo:
            terms[t] = term
        key = owner[i, pl.ds(j, 1), :] * slots + slot[i, pl.ds(j, 1), :]
        got = lax.dot_general(term, one_hot(key, slots, 4 * slots), (((1,), (1,)), ((), ())),
                              preferred_element_type=F32)
        return got[0:8] + got[8:16]

    wait_feat(0)
    wait_feat(1)
    make_u(0)
    if halo:
        for copy in copies:
            copy.wait()
    scores(0, 0, sa, za)

    def body(s, carry):
        before = jnp.maximum(2 * s - 2, 0)
        later = jnp.minimum(s + 1, n // 2 - 1)

        @pl.when(s < n // 2 - 1)
        def _():
            wait_feat(2 * s + 2)
            wait_feat(2 * s + 3)

        old = gather(before, ca) + gather(before + 1, cb)
        sums[...] = jnp.where(s == 0, 0.0, sums[...] + old)
        scores(2 * s + 1, 1, sb, zb)
        couples(sa, za, ca)
        make_u(later)
        scores(2 * later, 0, sa, za)
        couples(sb, zb, cb)
        return carry

    lax.fori_loop(0, n // 2, body, 0)
    sums[...] = sums[...] + gather(n - 2, ca) + gather(n - 1, cb)
    if halo:
        for q, (a, b) in enumerate(DIRS):
            keep = [t for t, (i, j) in enumerate(tiles)
                    if (a == 0 or i == (0 if a < 0 else tx - 1)) and (b == 0 or j == (0 if b < 0 else ty - 1))]
            left, right = [], []
            for t in keep:
                i, j = tiles[t]
                key = owner[i, j : j + 1, :] * slots + slot[i, j : j + 1, :]
                left.append(terms[t])
                right.append(one_hot(key, slots, (3 * a + b + 4) * slots))
            got = lax.dot_general(jnp.concatenate(left, axis=1), jnp.concatenate(right, axis=1),
                                  (((1,), (1,)), ((), ())), preferred_element_type=F32)
            sent[q][...] = got[0:8] + got[8:16]


def pairs(tiles, halo, args, own, around):
    partner, rate, features, weight_u, lever, slot, owner, slots = args
    tx, ty, f, beads = features.shape
    nb = partner.shape[2]
    chans = rate.shape[0]
    width_h = weight_u.shape[0] // chans
    rows = beads + EXTRA
    n = len(tiles)
    total = jax.ShapeDtypeStruct((8, slots), F32)
    scratch = [
        pltpu.VMEM((n, f, beads), BF16),
        pltpu.VMEM((2, width_h, chans * beads), BF16),
        pltpu.VMEM((nb * beads, chans * beads), F32),
        pltpu.VMEM((nb * beads, chans * beads), F32),
        pltpu.VMEM((nb // 2, beads, 2 * beads), F32),
        pltpu.VMEM((nb // 2, beads, 2 * beads), F32),
        pltpu.VMEM((nb * beads, beads), BF16),
        pltpu.VMEM((nb * beads, beads), BF16),
        pltpu.VMEM((nb // 2, 2 * EXTRA, 2 * beads), BF16),
        pltpu.SemaphoreType.DMA((n,)),
    ]
    if halo:
        scratch += [pltpu.VMEM((n, 16, beads), BF16), pltpu.VMEM((tx + 2, ty + 2, rows, beads), BF16),
                    pltpu.SemaphoreType.DMA((9,))]
    ids = jnp.asarray([i * ty + j for i, j in tiles], jnp.int32)
    shape = (tx, ty, beads, width_h, chans, nb, slots)
    return pl.pallas_call(
        lambda *refs: pairs_kernel(tiles, halo, shape, *refs),
        out_shape=[total] * (9 if halo else 1),
        in_specs=[SMEM, SMEM, SMEM, HBM, VMEM, VMEM, VMEM, VMEM, HBM if halo else VMEM]
        + [HBM] * (8 if halo else 0),
        out_specs=[VMEM] * (9 if halo else 1),
        scratch_shapes=scratch,
        compiler_params=pltpu.CompilerParams(vmem_limit_bytes=LIMIT),
        cost_estimate=pl.CostEstimate(flops=n * 150_000_000, bytes_accessed=n * 100_000, transcendentals=0),
    )(ids, partner, rate, features, weight_u, lever, slot, owner, own, *(around if halo else []))


def rotation_rows(q):
    w, a, b, c = q
    return [
        [1 - 2 * (b * b + c * c), 2 * (a * b - w * c), 2 * (a * c + w * b)],
        [2 * (a * b + w * c), 1 - 2 * (a * a + c * c), 2 * (b * c - w * a)],
        [2 * (a * c - w * b), 2 * (b * c + w * a), 1 - 2 * (a * a + b * b)],
    ]


def integrate_kernel(*refs):
    sums, (pose, motion, inverse, state, packed) = refs[:-5], refs[-5:]
    total = sums[0][...]
    for other in sums[1:]:
        total = total + other[...]
    row = lambda ref, r: ref[0, 0, r : r + 1, :]
    f = [total[r : r + 1] for r in range(6)]
    q = [row(pose, 3 + r) for r in range(4)]
    vel = [row(motion, r) + STEP_DT * row(inverse, 0) * f[r] for r in range(3)]
    centre = [row(pose, r) + STEP_DT * vel[r] for r in range(3)]
    ang = [row(motion, 3 + r) + STEP_DT * f[3 + r] for r in range(3)]
    old = rotation_rows(q)
    frame = [sum(old[r][c] * ang[r] for r in range(3)) * row(inverse, 1 + c) for c in range(3)]
    om = [sum(old[r][c] * frame[c] for c in range(3)) for r in range(3)]
    w, x, y, z = q
    rate = [
        -(om[0] * x + om[1] * y + om[2] * z),
        w * om[0] + om[1] * z - om[2] * y,
        w * om[1] + om[2] * x - om[0] * z,
        w * om[2] + om[0] * y - om[1] * x,
    ]
    step = [q[r] + 0.5 * STEP_DT * rate[r] for r in range(4)]
    size = jnp.sqrt(sum(s * s for s in step))
    new = [s / size for s in step]
    turned = rotation_rows(new)
    rel = [sum(turned[r][k] * old[c][k] for k in range(3)) for r in range(3) for c in range(3)]
    for r, val in enumerate(centre + new + vel + ang):
        state[0, 0, r : r + 1, :] = val
    for r, val in enumerate([STEP_DT * v for v in vel] + rel):
        packed[r : r + 1, :] = val
    packed[12:16, :] = jnp.zeros((4, packed.shape[1]), F32)


def integrate(sums, pose, motion, inverse):
    slots = pose.shape[3]
    return pl.pallas_call(
        integrate_kernel,
        out_shape=[jax.ShapeDtypeStruct((1, 1, 13, slots), F32), jax.ShapeDtypeStruct((16, slots), F32)],
        in_specs=[VMEM] * (len(sums) + 3),
        out_specs=[VMEM] * 2,
    )(*sums, pose, motion, inverse)


def place(table, key, base, lev):
    slots = table.shape[1]
    got = jnp.dot(table, one_hot(key, slots, base), preferred_element_type=F32)
    got = got[0:16] + got[16:32]
    out = got[0:3]
    turned = [
        sum(got[3 + 3 * r + c : 4 + 3 * r + c] * lev[c : c + 1] for c in range(3)) for r in range(3)
    ]
    return out + jnp.concatenate(turned, axis=0)


def move_own_kernel(packed, pos, lever, slot, owner, moved):
    tx, ty = pos.shape[0], pos.shape[1]
    slots = packed.shape[1]
    table = jnp.concatenate(split_two(packed[...]), axis=0)

    def line(i, carry):
        for j in range(ty):
            key = owner[i, j : j + 1, :] * slots + slot[i, j : j + 1, :]
            lev = lever[i, j]
            moved[i, j] = pos[i, j].astype(F32) + place(table, key, 4 * slots, lev) - lev
        return carry

    lax.fori_loop(0, tx, line, 0)


def move_own(packed, pos, lever, slot, owner):
    return pl.pallas_call(
        move_own_kernel,
        out_shape=jax.ShapeDtypeStruct(lever.shape, F32),
        in_specs=[VMEM] * 5,
        out_specs=VMEM,
        compiler_params=pltpu.CompilerParams(vmem_limit_bytes=LIMIT),
    )(packed, pos, lever, slot, owner)


def move_rim_kernel(*refs):
    tables, (part, lever, slot, owner, moved) = refs[:8], refs[8:]
    tx, ty = part.shape[0], part.shape[1]
    slots = tables[0].shape[1]
    moved[...] = part[...]
    for q, (a, b) in enumerate(DIRS):
        table = jnp.concatenate(split_two(tables[q][...]), axis=0)
        for i in range(tx) if a == 0 else [0 if a < 0 else tx - 1]:
            for j in range(ty) if b == 0 else [0 if b < 0 else ty - 1]:
                key = owner[i, j : j + 1, :] * slots + slot[i, j : j + 1, :]
                moved[i, j] = moved[i, j] + place(table, key, (3 * a + b + 4) * slots, lever[i, j])


def move_rim(tables, part, lever, slot, owner):
    return pl.pallas_call(
        move_rim_kernel,
        out_shape=jax.ShapeDtypeStruct(lever.shape, F32),
        in_specs=[VMEM] * 12,
        out_specs=VMEM,
        compiler_params=pltpu.CompilerParams(vmem_limit_bytes=LIMIT),
    )(*tables, part, lever, slot, owner)


def shifted(value, a, b):
    nx, ny = lax.axis_size("gx"), lax.axis_size("gy")
    if a == 0:
        return lax.ppermute(value, "gy", [(y, (y + b) % ny) for y in range(ny)])
    if b == 0:
        return lax.ppermute(value, "gx", [(x, (x + a) % nx) for x in range(nx)])
    route = [(x * ny + y, (x + a) % nx * ny + (y + b) % ny) for x in range(nx) for y in range(ny)]
    return lax.ppermute(value, ("gx", "gy"), route)


def local(positions, features, lever, partner, body_slot, owner_dir, body_pose, body_motion,
          body_inverse, weight_u, weight_v, radial_rate):
    tx, ty = positions.shape[0], positions.shape[1]
    slots = body_pose.shape[3]
    own, top, bottom, left, right, c0, c1, c2, c3 = project(features, positions, weight_v)
    edge = {(-1, -1): c3, (-1, 0): bottom, (-1, 1): c2, (0, -1): right, (0, 1): left,
            (1, -1): c1, (1, 0): top, (1, 1): c0}
    around = [shifted(edge[d], -d[0], -d[1]) for d in DIRS]
    args = (partner, radial_rate, features, weight_u, lever, body_slot, owner_dir, slots)
    inner = [(i, j) for i in range(1, tx - 1) for j in range(1, ty - 1)]
    rim = [(i, j) for i in range(tx) for j in range(ty) if i in (0, tx - 1) or j in (0, ty - 1)]
    cut = 24
    (first,) = pairs(inner[:cut], False, args, own, None)
    second, *out = pairs(rim, True, args, own, around)
    got = [shifted(value, a, b) for value, (a, b) in zip(out, DIRS)]
    (third,) = pairs(inner[cut:], False, args, own, None)
    state, packed = integrate([first, second, third] + got, body_pose, body_motion, body_inverse)
    tables = [shifted(packed, -a, -b) for a, b in DIRS]
    part = move_own(packed, positions, lever, body_slot, owner_dir)
    moved = move_rim(tables, part, lever, body_slot, owner_dir)
    return (moved, state)


def solution(mesh):
    placed = (
        P("gx", "gy", None, None),
        P("gx", "gy", None, None),
        P("gx", "gy", None, None),
        P("gx", "gy", None),
        P("gx", "gy", None),
        P("gx", "gy", None),
        P("gx", "gy", None, None),
        P("gx", "gy", None, None),
        P("gx", "gy", None, None),
        P(),
        P(),
        P(),
    )
    return jax.shard_map(
        local,
        mesh=mesh,
        in_specs=placed,
        out_specs=(P("gx", "gy", None, None), P("gx", "gy", None, None)),
        check_vma=False,
    )
```

time: 289 us -> 143 us (0.49); the launches traced: 286 us -> 143 us
  matrix products: 128 us -> 0 us
  Pallas kernels: 0 us -> 68.8 us
  other arithmetic: 51.7 us -> 0 us
  local copies, waits for them, and re-layouts: 58.2 us -> 9.67 us
  starting transfers between devices: 21 us -> 39.7 us
  loops' own time: 16.2 us -> 0 us
  waiting for transfers between devices: 9.45 us -> 23.5 us
    dot_general x114 -> x0, matrix products: 128 us -> none  [the longest x48 50.3 us: tile_forces(): jnp.einsum('mab,mcb->mca', couple, p_part, precision=lax.Precision.HIGHEST)]
    pallas_call x0 -> x7, Pallas kernels: none -> 68.8 us  [the longest x3 54 us: pairs(): pl.pallas_call(lambda *refs: pairs_kernel(tiles, halo, shape, *refs), out...]
    dynamic_slice x64 -> x0, local copies, waits for them, and re-layouts: 42.1 us -> none  [the longest x48 29.8 us: local(): lax.map(row_forces, (jnp.arange(tiles_x, dtype=jnp.int32), u_all.reshape(...]
    reduce_sum x63 -> x0, other arithmetic: 28.7 us -> none  [the longest x8 18.3 us: tile_forces(): radius_sq = jnp.sum(differ * differ, axis=1)]
    ppermute x12 -> x24, starting transfers between devices: 21 us -> 39.7 us  [the longest x12 19 us: shifted(): return lax.ppermute(value, ('gx', 'gy'), route)]
    another operation x3 -> x0, loops' own time: 16.2 us -> none  [the longest x1 15.9 us: local(): lax.map(row_forces, (jnp.arange(tiles_x, dtype=jnp.int32), u_all.reshape(...]
    ppermute x12 -> x24, waiting for transfers between devices: 9.45 us -> 23.5 us  [the longest x12 23.4 us: shifted(): return lax.ppermute(value, ('gx', 'gy'), route)]
    reshape x3 -> x0, local copies, waits for them, and re-layouts: 12.6 us -> none  [the longest x1 12.6 us: local(): u_all.reshape(tiles_x, tiles_y, channels, width_h, tile_len)]
  transfers between devices with their start and end apart: 12 -> 24, of which waited for: 5 -> 4; matrix products, arithmetic and copies ran while one was open for 8% -> 3% of each run, Pallas kernels for 0% -> 24%
where the time goes in v1:
time: 143 us
  Pallas kernels  68.8 us (48%)
  starting transfers between devices  39.7 us (28%)
  waiting for transfers between devices  23.5 us (16%)
  local copies, waits for them, and re-layouts  9.67 us (7%)
    pallas_call x3, Pallas kernels, pairs(): pl.pallas_call(lambda *refs: pairs_kernel(tiles, halo, shape, *refs), out...  54 us
    ppermute x12, waiting for transfers between devices, shifted(): return lax.ppermute(value, ('gx', 'gy'), route)  23.4 us
    ppermute x12, starting transfers between devices, shifted(): return lax.ppermute(value, ('gx', 'gy'), route)  19 us
    ppermute x6, starting transfers between devices, shifted(): return lax.ppermute(value, 'gx', [(x, (x + a) % nx) for x in range(nx)])  10.9 us
    ppermute x6, starting transfers between devices, shifted(): return lax.ppermute(value, 'gy', [(y, (y + b) % ny) for y in range(ny)])  9.72 us
    unnamed x73, local copies, waits for them, and re-layouts  9.67 us
    pallas_call x1, Pallas kernels, project(): pl.pallas_call(project_kernel, grid=(tx,), out_shape=[sds(tx, ty, rows, b...  7.73 us
    pallas_call x1, Pallas kernels, move_own(): pl.pallas_call(move_own_kernel, out_shape=jax.ShapeDtypeStruct(lever.shap...  3.44 us
  transfers between devices with their start and end apart: 24, of which 4 were waited for; matrix products, arithmetic and copies ran while one was open for 3% of the time, Pallas kernels for 24%

profile of v1, /device:TPU:0, one launch (start us, length us, event | category | flops | bytes accessed | tf_op | source)
XLA Modules:
  0.0 142.6 jit_solution(11494216994598896590)
XLA Ops:
  0.6 1.5 %copy.17.pos = bf16[8,8,3,128]{3,2,1,0:T(4,128)(2,1)} copy(bf16[8,8,3,128]{3,1,2,0:T(8,128)(2,1)} %param.15) | data formatting | bytes 98304 | tf_op args[0]
  2.1 7.7 %shard_map.158 = (bf16[8,8,144,128]{3,2,1,0:T(8,128)(2,1)}, bf16[8,144,128]{2,1,0:T(8,128)(2,1)}, bf16[8,144,128]{2,1,0:T(8,128)(2,1)}, bf16[8,144,128]{2,1,0:T(...) custom-call(bf16[8,8,256,128]{3,2,1,0:T(8,128)(2,1)} %refs_3_.5, ...), custom_call_target="tpu_custom_call" | custom-call | tf_op jit(solution)/shard_map/pallas_call | solution.py:80
  9.9 3.1 %collective-permute-start.1 = (bf16[8,144,128]{2,1,0:T(8,128)(2,1)}, bf16[8,144,128]{2,1,0:T(8,128)(2,1)S(1)}, u32[]{:S(2)}, u32[]{:S(2)}) collective-permute-start(bf16[8,144,128]{2,1,0:T(8,128)(2,1)} %get-tuple-element.24), channel_id=1, source_target_pairs={{0,8},{8,16},{16,24},{24,0},{1,9},{9,17},{17,25},{25,1},{2,10},{10... | collective-permute-start | bytes 884744 | tf_op jit(solution)/shard_map/ppermute | solution.py:412
  13.0 2.6 %collective-permute-start.4 = (bf16[8,144,128]{2,1,0:T(8,128)(2,1)}, bf16[8,144,128]{2,1,0:T(8,128)(2,1)S(1)}, u32[]{:S(2)}, u32[]{:S(2)}) collective-permute-start(bf16[8,144,128]{2,1,0:T(8,128)(2,1)} %get-tuple-element.27), channel_id=1, source_target_pairs={{0,7},{1,0},{2,1},{3,2},{4,3},{5,4},{6,5},{7,6},{8,15},{9,8},{10,9... | collective-permute-start | bytes 884744 | tf_op jit(solution)/shard_map/ppermute | solution.py:410
  15.6 2.1 %collective-permute-start.6 = (bf16[8,144,128]{2,1,0:T(8,128)(2,1)}, bf16[8,144,128]{2,1,0:T(8,128)(2,1)S(1)}, u32[]{:S(2)}, u32[]{:S(2)}) collective-permute-start(bf16[8,144,128]{2,1,0:T(8,128)(2,1)} %get-tuple-element.29), channel_id=1, source_target_pairs={{0,24},{8,0},{16,8},{24,16},{1,25},{9,1},{17,9},{25,17},{2,26},{10... | collective-permute-start | bytes 884744 | tf_op jit(solution)/shard_map/ppermute | solution.py:412
  17.7 12.5 %collective-permute-done.refs_9_ = bf16[144,128]{1,0:T(8,128)(2,1)S(1)} collective-permute-done((bf16[144,128]{1,0:T(8,128)(2,1)}, bf16[144,128]{1,0:T(8,128)(2,1)S(1)}, u32[]{:S(2)}, u32[]{:S(2)}) %collective-permute-start) | collective-permute-done | bytes 36896 | tf_op jit(solution)/shard_map/ppermute | solution.py:414
  30.7 4.9 %collective-permute-done.2.refs_11_ = bf16[144,128]{1,0:T(8,128)(2,1)S(1)} collective-permute-done((bf16[144,128]{1,0:T(8,128)(2,1)}, bf16[144,128]{1,0:T(8,128)(2,1)S(1)}, u32[]{:S(2)}, u32[]{:S(2)}) %collective-permute-start.2) | collective-permute-done | bytes 36896 | tf_op jit(solution)/shard_map/ppermute | solution.py:414
  35.6 5.4 %collective-permute-done.5.refs_14_ = bf16[144,128]{1,0:T(8,128)(2,1)S(1)} collective-permute-done((bf16[144,128]{1,0:T(8,128)(2,1)}, bf16[144,128]{1,0:T(8,128)(2,1)S(1)}, u32[]{:S(2)}, u32[]{:S(2)}) %collective-permute-start.5) | collective-permute-done | bytes 36896 | tf_op jit(solution)/shard_map/ppermute | solution.py:414
  40.9 2.5 %collective-permute-start.7 = (bf16[144,128]{1,0:T(8,128)(2,1)}, bf16[144,128]{1,0:T(8,128)(2,1)S(1)}, u32[]{:S(2)}, u32[]{:S(2)}) collective-permute-start(bf16[144,128]{1,0:T(8,128)(2,1)} %get-tuple-element.30), channel_id=1, source_target_pairs={{0,31},{1,24},{2,25},{3,26},{4,27},{5,28},{6,29},{7,30},{8,7},{9,0... | collective-permute-start | bytes 110600 | tf_op jit(solution)/shard_map/ppermute | solution.py:414
  46.6 23.2 %shard_map.160 = (f32[8,128]{1,0:T(8,128)}, f32[8,128]{1,0:T(8,128)}, f32[8,128]{1,0:T(8,128)}, f32[8,128]{1,0:T(8,128)}, f32[8,128]{1,0:T(8,128)}, /*index=5*/f...) custom-call(s32[28]{0:T(128)} %constant.7.clone.refs_0_, s32[8,8,6]{2,1,0:T(8,128)} %copy.18.refs_1_, ...), custom_call_target="tpu_custom_call" | custom-call | flops 4200000000 | bytes 2800000 | tf_op jit(solution)/shard_map/pallas_call | solution.py:284
  69.8 1.9 %collective-permute-start.10 = (f32[8,128]{1,0:T(8,128)}, f32[8,128]{1,0:T(8,128)S(1)}, u32[]{:S(2)}, u32[]{:S(2)}) collective-permute-start(f32[8,128]{1,0:T(8,128)} %get-tuple-element.34), channel_id=1, source_target_pairs={{0,25},{1,26},{2,27},{3,28},{4,29},{5,30},{6,31},{7,24},{8,1},{9,2... | collective-permute-start | bytes 12296 | tf_op jit(solution)/shard_map/ppermute | solution.py:414
  71.7 4.4 %collective-permute-start.11 = (f32[8,128]{1,0:T(8,128)}, f32[8,128]{1,0:T(8,128)S(1)}, u32[]{:S(2)}, u32[]{:S(2)}) collective-permute-start(f32[8,128]{1,0:T(8,128)} %get-tuple-element.35), channel_id=1, source_target_pairs={{0,7},{1,0},{2,1},{3,2},{4,3},{5,4},{6,5},{7,6},{8,15},{9,8},{10,9... | collective-permute-start | bytes 12296 | tf_op jit(solution)/shard_map/ppermute | solution.py:410
  76.1 19.1 %shard_map.159.refs_0_ = f32[8,128]{1,0:T(8,128)} custom-call(s32[24]{0:T(128)} %constant.6.clone.refs_0_, s32[8,8,6]{2,1,0:T(8,128)} %copy.18.refs_1_, f32[4]{0:T(128)} %refs_2_.5, bf16[8,8,256,128]{3,2,1,0:T(8,128)(2,1)} %refs_3_.5, bf16[512,256]{1,0:T(8,128)(2,1)} %refs_4_.5, f32[8,8,3,128]{3,2,1,0:T(4,128)} %copy.19.refs_5_.lever.refs_9_, ...), custom_call_target="tpu_custom_call" | custom-call | flops 3600000000 | bytes 2400000 | tf_op jit(solution)/shard_map/pallas_call | solution.py:284
  95.8 5.3 %collective-permute-start.8 = (f32[8,128]{1,0:T(8,128)S(1)}, f32[8,128]{1,0:T(8,128)S(1)}, u32[]{:S(2)}, u32[]{:S(2)}) collective-permute-start(f32[8,128]{1,0:T(8,128)S(1)} %copy-done.29), channel_id=1, source_target_pairs={{0,31},{1,24},{2,25},{3,26},{4,27},{5,28},{6,29},{7,30},{8,7},{9,0... | collective-permute-start | bytes 12296 | tf_op jit(solution)/shard_map/ppermute | solution.py:414
  101.1 3.8 %collective-permute-start.9 = (f32[8,128]{1,0:T(8,128)S(1)}, f32[8,128]{1,0:T(8,128)S(1)}, u32[]{:S(2)}, u32[]{:S(2)}) collective-permute-start(f32[8,128]{1,0:T(8,128)S(1)} %copy-done.28), channel_id=1, source_target_pairs={{0,24},{8,0},{16,8},{24,16},{1,25},{9,1},{17,9},{25,17},{2,26},{10... | collective-permute-start | bytes 12296 | tf_op jit(solution)/shard_map/ppermute | solution.py:412
  104.9 11.7 %shard_map.161.refs_2_ = f32[8,128]{1,0:T(8,128)} custom-call(s32[12]{0:T(128)} %constant.8.clone.refs_0_, s32[8,8,6]{2,1,0:T(8,128)} %copy.18.refs_1_, f32[4]{0:T(128)} %refs_2_.5, bf16[8,8,256,128]{3,2,1,0:T(8,128)(2,1)} %refs_3_.5, bf16[512,256]{1,0:T(8,128)(2,1)} %refs_4_.5, f32[8,8,3,128]{3,2,1,0:T(4,128)} %copy.19.refs_5_.lever.refs_9_, ...), custom_call_target="tpu_custom_call" | custom-call | flops 1800000000 | bytes 1200000 | tf_op jit(solution)/shard_map/pallas_call | solution.py:284
  118.5 1.4 shard_map.162
  120.0 4.3 %collective-permute-start.18 = (f32[16,128]{1,0:T(8,128)}, f32[16,128]{1,0:T(8,128)S(1)}, u32[]{:S(2)}, u32[]{:S(2)}) collective-permute-start(f32[16,128]{1,0:T(8,128)} %get-tuple-element.40.packed), channel_id=1, source_target_pairs={{0,15},{1,8},{2,9},{3,10},{4,11},{5,12},{6,13},{7,14},{8,23},{9,16... | collective-permute-start | bytes 24584 | tf_op jit(solution)/shard_map/ppermute | solution.py:414
  124.3 2.6 %collective-permute-start.20 = (f32[16,128]{1,0:T(8,128)}, f32[16,128]{1,0:T(8,128)S(1)}, u32[]{:S(2)}, u32[]{:S(2)}) collective-permute-start(f32[16,128]{1,0:T(8,128)} %get-tuple-element.40.packed), channel_id=1, source_target_pairs={{0,7},{1,0},{2,1},{3,2},{4,3},{5,4},{6,5},{7,6},{8,15},{9,8},{10,9... | collective-permute-start | bytes 24584 | tf_op jit(solution)/shard_map/ppermute | solution.py:410
  127.0 1.9 %collective-permute-start.22 = (f32[16,128]{1,0:T(8,128)}, f32[16,128]{1,0:T(8,128)S(1)}, u32[]{:S(2)}, u32[]{:S(2)}) collective-permute-start(f32[16,128]{1,0:T(8,128)} %get-tuple-element.40.packed), channel_id=1, source_target_pairs={{0,24},{8,0},{16,8},{24,16},{1,25},{9,1},{17,9},{25,17},{2,26},{10... | collective-permute-start | bytes 24584 | tf_op jit(solution)/shard_map/ppermute | solution.py:412
  128.8 4.1 %collective-permute-start.23 = (f32[16,128]{1,0:T(8,128)}, f32[16,128]{1,0:T(8,128)S(1)}, u32[]{:S(2)}, u32[]{:S(2)}) collective-permute-start(f32[16,128]{1,0:T(8,128)} %get-tuple-element.40.packed), channel_id=1, source_target_pairs={{0,31},{1,24},{2,25},{3,26},{4,27},{5,28},{6,29},{7,30},{8,7},{9,0... | collective-permute-start | bytes 24584 | tf_op jit(solution)/shard_map/ppermute | solution.py:414
  132.9 3.4 %shard_map.163.refs_8_ = f32[8,8,3,128]{3,2,1,0:T(4,128)} custom-call(f32[16,128]{1,0:T(8,128)} %get-tuple-element.40.packed, bf16[8,8,3,128]{3,2,1,0:T(4,128)(2,1)} %copy.17.pos, f32[8,8,3,128]{3,2,1,0:T(4,128)} %copy.19.refs_5_.lever.refs_9_, s32[8,8,128]{2,1,0:T(8,128)} %refs_10_.1, s32[8,8,128]{2,1,0:T(8,128)} %refs_11_.2), custom_call_target="tpu_custom_call" | custom-call | tf_op jit(solution)/shard_map/pallas_call | solution.py:375
  138.9 2.2 %shard_map.164 = f32[8,8,3,128]{3,2,1,0:T(4,128)} custom-call(f32[16,128]{1,0:T(8,128)} %copy-done.2, f32[16,128]{1,0:T(8,128)} %copy-done.3, f32[16,128]{1,0:T(8,128)} %copy-done.4, f32[16,128]{1,0:T(8,128)} %copy-done.5, f32[16,128]{1,0:T(8,128)} %copy-done.6, f32[16,128]{1,0:T(8,128)} %copy-done.7, f32[16,128]{1,0:T(8,128)} %copy-done.8, ...), custom_call_target="tpu_custom_call" | custom-call | tf_op jit(solution)/shard_map/pallas_call | solution.py:398
  141.1 1.6 %copy.29 = f32[8,8,3,128]{3,1,2,0:T(8,128)} copy(f32[8,8,3,128]{3,2,1,0:T(4,128)} %shard_map.164) | data formatting | bytes 196608
  (104 shorter events, 8.5 us)
Async XLA Ops:
  9.9 35.7 %collective-permute-start.1 = (bf16[8,144,128]{2,1,0:T(8,128)(2,1)}, bf16[8,144,128]{2,1,0:T(8,128)(2,1)S(1)}, u32[]{:S(2)}, u32[]{:S(2)}) collective-permute-start(bf16[8,144,128]{2,1,0:T(8,128)(2,1)} %get-tuple-element.24), channel_id=1, source_target_pairs={{0,8},{8,16},{16,24},{24,0},{1,9},{9,17},{17,25},{25,1},{2,10},{10... | collective-permute-start | bytes 884744 | tf_op jit(solution)/shard_map/ppermute | solution.py:412
  13.0 32.6 %collective-permute-start.3 = (bf16[8,144,128]{2,1,0:T(8,128)(2,1)}, bf16[8,144,128]{2,1,0:T(8,128)(2,1)S(1)}, u32[]{:S(2)}, u32[]{:S(2)}) collective-permute-start(bf16[8,144,128]{2,1,0:T(8,128)(2,1)} %get-tuple-element.26), channel_id=1, source_target_pairs={{0,1},{1,2},{2,3},{3,4},{4,5},{5,6},{6,7},{7,0},{8,9},{9,10},{10,1... | collective-permute-start | bytes 884744 | tf_op jit(solution)/shard_map/ppermute | solution.py:410
  13.0 32.6 %collective-permute-start.4 = (bf16[8,144,128]{2,1,0:T(8,128)(2,1)}, bf16[8,144,128]{2,1,0:T(8,128)(2,1)S(1)}, u32[]{:S(2)}, u32[]{:S(2)}) collective-permute-start(bf16[8,144,128]{2,1,0:T(8,128)(2,1)} %get-tuple-element.27), channel_id=1, source_target_pairs={{0,7},{1,0},{2,1},{3,2},{4,3},{5,4},{6,5},{7,6},{8,15},{9,8},{10,9... | collective-permute-start | bytes 884744 | tf_op jit(solution)/shard_map/ppermute | solution.py:410
  15.6 30.0 %collective-permute-start.6 = (bf16[8,144,128]{2,1,0:T(8,128)(2,1)}, bf16[8,144,128]{2,1,0:T(8,128)(2,1)S(1)}, u32[]{:S(2)}, u32[]{:S(2)}) collective-permute-start(bf16[8,144,128]{2,1,0:T(8,128)(2,1)} %get-tuple-element.29), channel_id=1, source_target_pairs={{0,24},{8,0},{16,8},{24,16},{1,25},{9,1},{17,9},{25,17},{2,26},{10... | collective-permute-start | bytes 884744 | tf_op jit(solution)/shard_map/ppermute | solution.py:412
  17.7 12.5 %collective-permute-start = (bf16[144,128]{1,0:T(8,128)(2,1)}, bf16[144,128]{1,0:T(8,128)(2,1)S(1)}, u32[]{:S(2)}, u32[]{:S(2)}) collective-permute-start(bf16[144,128]{1,0:T(8,128)(2,1)} %get-tuple-element.23), channel_id=1, source_target_pairs={{0,9},{1,10},{2,11},{3,12},{4,13},{5,14},{6,15},{7,8},{8,17},{9,18... | collective-permute-start | bytes 110600 | tf_op jit(solution)/shard_map/ppermute | solution.py:414
  30.2 5.4 %collective-permute-start.2 = (bf16[144,128]{1,0:T(8,128)(2,1)}, bf16[144,128]{1,0:T(8,128)(2,1)S(1)}, u32[]{:S(2)}, u32[]{:S(2)}) collective-permute-start(bf16[144,128]{1,0:T(8,128)(2,1)} %get-tuple-element.25), channel_id=1, source_target_pairs={{0,15},{1,8},{2,9},{3,10},{4,11},{5,12},{6,13},{7,14},{8,23},{9,16... | collective-permute-start | bytes 110600 | tf_op jit(solution)/shard_map/ppermute | solution.py:414
  35.6 5.4 %collective-permute-start.5 = (bf16[144,128]{1,0:T(8,128)(2,1)}, bf16[144,128]{1,0:T(8,128)(2,1)S(1)}, u32[]{:S(2)}, u32[]{:S(2)}) collective-permute-start(bf16[144,128]{1,0:T(8,128)(2,1)} %get-tuple-element.28), channel_id=1, source_target_pairs={{0,25},{1,26},{2,27},{3,28},{4,29},{5,30},{6,31},{7,24},{8,1},{9,2... | collective-permute-start | bytes 110600 | tf_op jit(solution)/shard_map/ppermute | solution.py:414
  40.9 4.6 %collective-permute-start.7 = (bf16[144,128]{1,0:T(8,128)(2,1)}, bf16[144,128]{1,0:T(8,128)(2,1)S(1)}, u32[]{:S(2)}, u32[]{:S(2)}) collective-permute-start(bf16[144,128]{1,0:T(8,128)(2,1)} %get-tuple-element.30), channel_id=1, source_target_pairs={{0,31},{1,24},{2,25},{3,26},{4,27},{5,28},{6,29},{7,30},{8,7},{9,0... | collective-permute-start | bytes 110600 | tf_op jit(solution)/shard_map/ppermute | solution.py:414
  69.8 25.6 %collective-permute-start.10 = (f32[8,128]{1,0:T(8,128)}, f32[8,128]{1,0:T(8,128)S(1)}, u32[]{:S(2)}, u32[]{:S(2)}) collective-permute-start(f32[8,128]{1,0:T(8,128)} %get-tuple-element.34), channel_id=1, source_target_pairs={{0,25},{1,26},{2,27},{3,28},{4,29},{5,30},{6,31},{7,24},{8,1},{9,2... | collective-permute-start | bytes 12296 | tf_op jit(solution)/shard_map/ppermute | solution.py:414
  71.7 24.1 %collective-permute-start.11 = (f32[8,128]{1,0:T(8,128)}, f32[8,128]{1,0:T(8,128)S(1)}, u32[]{:S(2)}, u32[]{:S(2)}) collective-permute-start(f32[8,128]{1,0:T(8,128)} %get-tuple-element.35), channel_id=1, source_target_pairs={{0,7},{1,0},{2,1},{3,2},{4,3},{5,4},{6,5},{7,6},{8,15},{9,8},{10,9... | collective-permute-start | bytes 12296 | tf_op jit(solution)/shard_map/ppermute | solution.py:410
  76.1 25.1 %collective-permute-start.12 = (f32[8,128]{1,0:T(8,128)}, f32[8,128]{1,0:T(8,128)S(1)}, u32[]{:S(2)}, u32[]{:S(2)}) collective-permute-start(f32[8,128]{1,0:T(8,128)} %get-tuple-element.36), channel_id=1, source_target_pairs={{0,1},{1,2},{2,3},{3,4},{4,5},{5,6},{6,7},{7,0},{8,9},{9,10},{10,1... | collective-permute-start | bytes 12296 | tf_op jit(solution)/shard_map/ppermute | solution.py:410
  95.2 22.6 %collective-permute-start.13 = (f32[8,128]{1,0:T(8,128)S(1)}, f32[8,128]{1,0:T(8,128)S(1)}, u32[]{:S(2)}, u32[]{:S(2)}) collective-permute-start(f32[8,128]{1,0:T(8,128)S(1)} %copy-done.32), channel_id=1, source_target_pairs={{0,15},{1,8},{2,9},{3,10},{4,11},{5,12},{6,13},{7,14},{8,23},{9,16... | collective-permute-start | bytes 12296 | tf_op jit(solution)/shard_map/ppermute | solution.py:414
  95.3 22.5 %collective-permute-start.14 = (f32[8,128]{1,0:T(8,128)S(1)}, f32[8,128]{1,0:T(8,128)S(1)}, u32[]{:S(2)}, u32[]{:S(2)}) collective-permute-start(f32[8,128]{1,0:T(8,128)S(1)} %copy-done.31), channel_id=1, source_target_pairs={{0,8},{8,16},{16,24},{24,0},{1,9},{9,17},{17,25},{25,1},{2,10},{10... | collective-permute-start | bytes 12296 | tf_op jit(solution)/shard_map/ppermute | solution.py:412
  95.4 22.4 %collective-permute-start.15 = (f32[8,128]{1,0:T(8,128)S(1)}, f32[8,128]{1,0:T(8,128)S(1)}, u32[]{:S(2)}, u32[]{:S(2)}) collective-permute-start(f32[8,128]{1,0:T(8,128)S(1)} %copy-done.30), channel_id=1, source_target_pairs={{0,9},{1,10},{2,11},{3,12},{4,13},{5,14},{6,15},{7,8},{8,17},{9,18... | collective-permute-start | bytes 12296 | tf_op jit(solution)/shard_map/ppermute | solution.py:414
  95.8 22.1 %collective-permute-start.8 = (f32[8,128]{1,0:T(8,128)S(1)}, f32[8,128]{1,0:T(8,128)S(1)}, u32[]{:S(2)}, u32[]{:S(2)}) collective-permute-start(f32[8,128]{1,0:T(8,128)S(1)} %copy-done.29), channel_id=1, source_target_pairs={{0,31},{1,24},{2,25},{3,26},{4,27},{5,28},{6,29},{7,30},{8,7},{9,0... | collective-permute-start | bytes 12296 | tf_op jit(solution)/shard_map/ppermute | solution.py:414
  101.1 16.8 %collective-permute-start.9 = (f32[8,128]{1,0:T(8,128)S(1)}, f32[8,128]{1,0:T(8,128)S(1)}, u32[]{:S(2)}, u32[]{:S(2)}) collective-permute-start(f32[8,128]{1,0:T(8,128)S(1)} %copy-done.28), channel_id=1, source_target_pairs={{0,24},{8,0},{16,8},{24,16},{1,25},{9,1},{17,9},{25,17},{2,26},{10... | collective-permute-start | bytes 12296 | tf_op jit(solution)/shard_map/ppermute | solution.py:412
  119.9 7.0 %collective-permute-start.16 = (f32[16,128]{1,0:T(8,128)}, f32[16,128]{1,0:T(8,128)S(1)}, u32[]{:S(2)}, u32[]{:S(2)}) collective-permute-start(f32[16,128]{1,0:T(8,128)} %get-tuple-element.40.packed), channel_id=1, source_target_pairs={{0,9},{1,10},{2,11},{3,12},{4,13},{5,14},{6,15},{7,8},{8,17},{9,18... | collective-permute-start | bytes 24584 | tf_op jit(solution)/shard_map/ppermute | solution.py:414
  119.9 7.0 %collective-permute-start.17 = (f32[16,128]{1,0:T(8,128)}, f32[16,128]{1,0:T(8,128)S(1)}, u32[]{:S(2)}, u32[]{:S(2)}) collective-permute-start(f32[16,128]{1,0:T(8,128)} %get-tuple-element.40.packed), channel_id=1, source_target_pairs={{0,8},{8,16},{16,24},{24,0},{1,9},{9,17},{17,25},{25,1},{2,10},{10... | collective-permute-start | bytes 24584 | tf_op jit(solution)/shard_map/ppermute | solution.py:412
  120.0 8.9 %collective-permute-start.18 = (f32[16,128]{1,0:T(8,128)}, f32[16,128]{1,0:T(8,128)S(1)}, u32[]{:S(2)}, u32[]{:S(2)}) collective-permute-start(f32[16,128]{1,0:T(8,128)} %get-tuple-element.40.packed), channel_id=1, source_target_pairs={{0,15},{1,8},{2,9},{3,10},{4,11},{5,12},{6,13},{7,14},{8,23},{9,16... | collective-permute-start | bytes 24584 | tf_op jit(solution)/shard_map/ppermute | solution.py:414
  124.3 13.4 %collective-permute-start.19 = (f32[16,128]{1,0:T(8,128)}, f32[16,128]{1,0:T(8,128)S(1)}, u32[]{:S(2)}, u32[]{:S(2)}) collective-permute-start(f32[16,128]{1,0:T(8,128)} %get-tuple-element.40.packed), channel_id=1, source_target_pairs={{0,1},{1,2},{2,3},{3,4},{4,5},{5,6},{6,7},{7,0},{8,9},{9,10},{10,1... | collective-permute-start | bytes 24584 | tf_op jit(solution)/shard_map/ppermute | solution.py:410
  124.3 13.4 %collective-permute-start.20 = (f32[16,128]{1,0:T(8,128)}, f32[16,128]{1,0:T(8,128)S(1)}, u32[]{:S(2)}, u32[]{:S(2)}) collective-permute-start(f32[16,128]{1,0:T(8,128)} %get-tuple-element.40.packed), channel_id=1, source_target_pairs={{0,7},{1,0},{2,1},{3,2},{4,3},{5,4},{6,5},{7,6},{8,15},{9,8},{10,9... | collective-permute-start | bytes 24584 | tf_op jit(solution)/shard_map/ppermute | solution.py:410
  126.9 10.8 %collective-permute-start.21 = (f32[16,128]{1,0:T(8,128)}, f32[16,128]{1,0:T(8,128)S(1)}, u32[]{:S(2)}, u32[]{:S(2)}) collective-permute-start(f32[16,128]{1,0:T(8,128)} %get-tuple-element.40.packed), channel_id=1, source_target_pairs={{0,25},{1,26},{2,27},{3,28},{4,29},{5,30},{6,31},{7,24},{8,1},{9,2... | collective-permute-start | bytes 24584 | tf_op jit(solution)/shard_map/ppermute | solution.py:414
  127.0 10.8 %collective-permute-start.22 = (f32[16,128]{1,0:T(8,128)}, f32[16,128]{1,0:T(8,128)S(1)}, u32[]{:S(2)}, u32[]{:S(2)}) collective-permute-start(f32[16,128]{1,0:T(8,128)} %get-tuple-element.40.packed), channel_id=1, source_target_pairs={{0,24},{8,0},{16,8},{24,16},{1,25},{9,1},{17,9},{25,17},{2,26},{10... | collective-permute-start | bytes 24584 | tf_op jit(solution)/shard_map/ppermute | solution.py:412
  128.8 8.9 %collective-permute-start.23 = (f32[16,128]{1,0:T(8,128)}, f32[16,128]{1,0:T(8,128)S(1)}, u32[]{:S(2)}, u32[]{:S(2)}) collective-permute-start(f32[16,128]{1,0:T(8,128)} %get-tuple-element.40.packed), channel_id=1, source_target_pairs={{0,31},{1,24},{2,25},{3,26},{4,27},{5,28},{6,29},{7,30},{8,7},{9,0... | collective-permute-start | bytes 24584 | tf_op jit(solution)/shard_map/ppermute | solution.py:414
  (33 other events, 364.7 us)

commit v2 on v1

v2 whole, which is shorter than its diff:
```python
import math
import jax
import jax.numpy as jnp
from jax import lax
from jax.experimental import pallas as pl
from jax.experimental.pallas import tpu as pltpu
from jax.sharding import PartitionSpec as P

STEP_DT = 0.25
CUT_SQUARE = 4.0
F32 = jnp.float32
BF16 = jnp.bfloat16
VMEM = pl.BlockSpec(memory_space=pltpu.VMEM)
SMEM = pl.BlockSpec(memory_space=pltpu.SMEM)
HBM = pl.BlockSpec(memory_space=pl.ANY)
LIMIT = 56 * 2**20
DIRS = [(-1, -1), (-1, 0), (-1, 1), (0, -1), (0, 1), (1, -1), (1, 0), (1, 1)]
EXTRA = 16
BODY = 48


def rows_iota(rows, lanes):
    return lax.broadcasted_iota(jnp.int32, (rows, lanes), 0)


def split_two(value):
    high = value.astype(BF16)
    return high, (value - high.astype(F32)).astype(BF16)


def one_hot(keys, slots, base):
    hit = rows_iota(slots, keys.shape[-1]) == keys - base
    return jnp.where(hit, 1.0, 0.0).astype(BF16)


def outward(axis):
    return lax.rem(lax.axis_index(axis), 2) == 1


def split_three(value):
    first = value.astype(BF16)
    rest = value - first.astype(F32)
    second = rest.astype(BF16)
    return first, second, (rest - second.astype(F32)).astype(BF16)


def project_kernel(feat, pos, weight_v, pose, motion, inverse, own, col_in, col_out, row_in, row_out):
    x = pl.program_id(0)
    tiles_x, tiles_y, beads = pl.num_programs(0), feat.shape[1], feat.shape[3]
    rows = beads + EXTRA
    row = rows_iota(8, beads)
    high_x, high_y = outward("gx"), outward("gy")
    for y in range(0, tiles_y, 2):
        both = jnp.concatenate([feat[0, y], feat[0, y + 1]], axis=1)
        v = jnp.dot(weight_v[...], both, preferred_element_type=F32).astype(BF16)
        for e in range(2):
            own[0, y + e, 0:beads, :] = v[:, e * beads : (e + 1) * beads].T
            px, py, pz = (jnp.broadcast_to(pos[0, c, y + e : y + e + 1, :].astype(F32), (8, beads)) for c in range(3))
            norm = -0.25 * (px * px + py * py + pz * pz)
            n1, n2, n3 = (part.astype(F32) for part in split_three(norm))
            first = px
            for r, val in ((1, py), (2, pz), (3, px), (4, py), (5, n1), (6, n2), (7, n3)):
                first = jnp.where(row == r, val, first)
            second = jnp.where(row < 3, 1.0, 0.0)
            own[0, y + e, beads:rows, :] = jnp.concatenate([first, second], axis=0).astype(BF16)
    at = pl.ds(pl.multiple_of(x * rows, 16), rows)
    low, high = own[0, 0], own[0, tiles_y - 1]
    col_in[at, :] = jnp.where(high_y, low, high)
    col_out[at, :] = jnp.where(high_y, high, low)

    @pl.when(x == jnp.where(high_x, 0, tiles_x - 1))
    def _():
        row_in[...] = own[0]

    @pl.when(x == jnp.where(high_x, tiles_x - 1, 0))
    def _():
        row_out[...] = own[0]

    @pl.when(x == 0)
    def _():
        body = jnp.concatenate(
            [pose[0, r] for r in range(3, 7)] + [motion[0, r] for r in range(6)]
            + [inverse[0, 0, r : r + 1, :] for r in range(4)] + [jnp.zeros((2, beads), F32)], axis=0)
        body = jnp.concatenate(split_three(body), axis=0)
        end = col_in.shape[0] - BODY
        col_in[end:, :] = body
        col_out[end:, :] = body


def project(features, pos, weight_v, pose, motion, inverse):
    tx, ty, f, beads = features.shape
    rows = beads + EXTRA
    whole = lambda s: pl.BlockSpec(s, lambda i: (0,) * len(s))
    sds = lambda *s: jax.ShapeDtypeStruct(s, BF16)
    col = (tx * rows + BODY, beads)
    return pl.pallas_call(
        project_kernel,
        grid=(tx,),
        out_shape=[sds(tx, ty, rows, beads), sds(*col), sds(*col), sds(ty, rows, beads), sds(ty, rows, beads)],
        in_specs=[
            pl.BlockSpec((1, ty, f, beads), lambda i: (i, 0, 0, 0)),
            pl.BlockSpec((1, 3, ty, beads), lambda i: (i, 0, 0, 0)),
            whole(weight_v.shape), whole(pose.shape), whole(motion.shape), whole(inverse.shape),
        ],
        out_specs=[
            pl.BlockSpec((1, ty, rows, beads), lambda i: (i, 0, 0, 0)),
            whole(col), whole(col), whole((ty, rows, beads)), whole((ty, rows, beads)),
        ],
        compiler_params=pltpu.CompilerParams(vmem_limit_bytes=LIMIT),
    )(features, pos, weight_v, pose, motion, inverse)


def pairs_kernel(strips, halo, shape, *refs):
    tiles = [(i, j) for rows, cols in strips for i in rows for j in cols]
    n = len(tiles)
    tx, ty, beads, width_h, chans, nb, slots = shape
    refs = list(refs)
    take = lambda k: [refs.pop(0) for _ in range(k)]
    ids, partner, rate, features, weight_u, lever, slot, owner, own = take(9)
    around = take(7) if halo else []
    sums = refs.pop(0)
    where_to, code_of = take(2)
    feat, ub, sa, sb, za, zb, ca, cb, wa, wb, high_of, norm_of, extra_of, fsem = take(14)
    terms, vp, vsem, total = take(4) if halo else (None, own, None, sums)
    wide = ty + 2
    here = lambda i, j: (i + 1) * wide + j + 1 if halo else i * ty + j
    side = chans * width_h

    at = 0
    loads = []
    for q, (i, j) in enumerate(strips):
        size = max(len(i), len(j))
        src = features.at[i[0], j[0] : j[-1] + 1] if len(i) == 1 else features.at[i[0] : i[-1] + 1, j[0]]
        loads.append(pltpu.make_async_copy(src, feat.at[at : at + size], fsem.at[q]))
        loads[-1].start()
        at += size
    if halo:
        rows = beads + EXTRA
        high_x, high_y = outward("gx"), outward("gy")
        x_in, x_out = jnp.where(high_x, 0, tx + 1), jnp.where(high_x, tx + 1, 0)
        y_in, y_out = jnp.where(high_y, 0, ty + 1), jnp.where(high_y, ty + 1, 0)
        line = lambda i: vp.at[pl.ds(i * wide + 1, ty)]
        cols, lines, ends = around[0:2], around[2:4], around[4:6]
        pairs_of = []
        for i in range(tx):
            for col, y in zip(cols, (y_in, y_out)):
                pairs_of.append((col.at[pl.ds(i * rows, rows)], vp.at[(i + 1) * wide + y]))
            pairs_of.append((own.at[i * ty : (i + 1) * ty], line(i + 1)))
        for src, end, x in zip(lines, ends, (x_in, x_out)):
            pairs_of.append((src, line(x)))
            pairs_of.append((end.at[pl.ds(0, rows)], vp.at[x * wide + y_in]))
            pairs_of.append((end.at[pl.ds(rows, rows)], vp.at[x * wide + y_out]))
        copies = [pltpu.make_async_copy(src, dst, vsem.at[q]) for q, (src, dst) in enumerate(pairs_of)]
        for copy in copies:
            copy.start()
    wa[...] = jnp.zeros_like(wa)
    wb[...] = jnp.zeros_like(wb)
    total[...] = around[6][...] if halo else jnp.zeros_like(total)

    def where_is(t):
        return lax.div(ids[t], jnp.int32(ty)), lax.rem(ids[t], jnp.int32(ty))

    def prepare(t, carry):
        i, j = where_is(t)
        for m in range(nb):
            code = partner[m, i, j]
            a = lax.shift_right_logical(code * 11, 5)
            where_to[t * nb + m] = here(i + a - 1, j + code - 3 * a - 1)
            code_of[t * nb + m] = code
        return carry

    row8 = rows_iota(8, beads)
    row16 = rows_iota(16, beads)
    for c in range(9):
        a, b = c // 3 - 1, c % 3 - 1
        high_of[c] = jnp.where(row8 == 3, -0.5 * a, jnp.where(row8 == 4, -0.5 * b, 0.0))
        for q, val in enumerate((0.5 * a, 0.5 * b, -0.25 * (a * a + b * b))):
            norm_of[c, q] = jnp.full((8, beads), val, F32)
        extra_of[c] = jnp.where(row16 == 11, 1.0 * a, jnp.where(row16 == 12, 1.0 * b, 0.0)).astype(BF16)

    def make_u(s):
        both = jnp.concatenate([feat[2 * s], feat[2 * s + 1]], axis=1)
        u = jnp.dot(weight_u[...], both, preferred_element_type=F32).astype(BF16)
        for e in range(2):
            for k in range(chans):
                ub[e, :, k * beads : (k + 1) * beads] = u[
                    k * width_h : (k + 1) * width_h, e * beads : (e + 1) * beads]

    def scores(t, e, buf, zbuf, wz):
        i, j = where_is(t)
        lhs, feats = [], []
        mine = vp[here(i, j), beads : beads + EXTRA, :].astype(F32)
        up = mine[0:8]
        bx, by = (jnp.broadcast_to(up[c : c + 1], (8, beads)) for c in (0, 1))
        bn = jnp.broadcast_to(up[5:6] + up[6:7] + up[7:8], (8, beads))
        fixed = jnp.where(row8 < 3, 0.5 * up, jnp.where(row8 >= 5, 1.0, 0.0))
        for m in range(nb):
            there, code = where_to[t * nb + m], code_of[t * nb + m]
            lhs.append(vp[there, 0:beads, :])
            feats.append(vp[there, beads : beads + EXTRA, :])
            high = fixed + high_of[code]
            norm = bn + bx * norm_of[code, 0] + by * norm_of[code, 1] + norm_of[code, 2]
            n1 = norm.astype(BF16).astype(F32)
            rest = norm - n1
            n2 = rest.astype(BF16).astype(F32)
            low = jnp.where(row8 == 0, n1, jnp.where(row8 == 1, n2, jnp.where(row8 == 2, rest - n2, 0.0)))
            wz[m // 2, EXTRA * (m % 2) : EXTRA * (m % 2 + 1), (m % 2) * beads : (m % 2 + 1) * beads] = (
                jnp.concatenate([high, low], axis=0).astype(BF16))
        for h in range(nb // 2):
            left = jnp.concatenate([feats[2 * h], feats[2 * h + 1]], axis=0)
            zbuf[h] = lax.dot_general(left, wz[h], (((0,), (0,)), ((), ())), preferred_element_type=F32)
        buf[...] = jnp.dot(jnp.concatenate(lhs, axis=0), ub[e], preferred_element_type=F32)

    def couples(buf, zbuf, cbuf):
        step = 16
        for m in range(nb):
            for r in range(0, beads, step):
                z = zbuf[m // 2, r : r + step, (m % 2) * beads : (m % 2 + 1) * beads]
                env = jnp.maximum(1.0 + z, 0.0)
                total = None
                for k in range(chans):
                    part = jnp.exp2(z * (rate[k] * (CUT_SQUARE / math.log(2.0)))) * buf[
                        m * beads + r : m * beads + r + step, k * beads : (k + 1) * beads]
                    total = part if total is None else total + part
                cbuf[m * beads + r : m * beads + r + step, :] = ((env * env) * total).astype(BF16)

    def gather(t, cbuf):
        i, j = where_is(t)
        lhs = []
        for m in range(nb):
            lhs.append(vp[where_to[t * nb + m], beads : beads + EXTRA, :] + extra_of[code_of[t * nb + m]])
        out = jnp.dot(jnp.concatenate(lhs, axis=1), cbuf[...], preferred_element_type=F32)
        out = out * (1.0 / width_h)
        mine = vp[here(i, j), beads : beads + EXTRA, :].astype(F32)
        w = out[8:9]
        fx = mine[0:1] * w - out[0:1] - out[11:12]
        fy = mine[1:2] * w - out[1:2] - out[12:13]
        fz = mine[2:3] * w - out[2:3]
        lx, ly, lz = (lever[i, c, pl.ds(j, 1), :] for c in range(3))
        value = jnp.concatenate(
            [fx, fy, fz, ly * fz - lz * fy, lz * fx - lx * fz, lx * fy - ly * fx,
             jnp.zeros((2, beads), F32)], axis=0)
        term = jnp.concatenate(split_two(value), axis=0)
        if halo:
            terms[t] = term
        key = owner[i, pl.ds(j, 1), :] * slots + slot[i, pl.ds(j, 1), :]
        got = lax.dot_general(term, one_hot(key, slots, 4 * slots), (((1,), (1,)), ((), ())),
                              preferred_element_type=F32)
        return got[0:8] + got[8:16]

    lax.fori_loop(0, n, prepare, 0)
    for load in loads:
        load.wait()
    make_u(0)
    if halo:
        for copy in copies:
            copy.wait()
    scores(0, 0, sa, za, wa)

    def body(s, carry):
        before = jnp.maximum(2 * s - 1, 0)
        later = jnp.minimum(s + 1, n // 2 - 1)

        scores(2 * s + 1, 1, sb, zb, wb)
        old = gather(before, cb)
        couples(sa, za, ca)
        make_u(later)
        scores(2 * later, 0, sa, za, wa)
        new = gather(2 * s, ca)
        couples(sb, zb, cb)
        total[...] = total[...] + jnp.where(s == 0, 0.0, old) + new
        return carry

    lax.fori_loop(0, n // 2, body, 0)
    total[...] = total[...] + gather(n - 1, cb)
    if halo:
        turn = lambda d, high: 1 + jnp.where(high, d, -d)
        sums[1, 1] = total[...]
        for a, b in DIRS:
            keep = [t for t, (i, j) in enumerate(tiles)
                    if (a == 0 or i == (0 if a < 0 else tx - 1)) and (b == 0 or j == (0 if b < 0 else ty - 1))]
            left, right = [], []
            for t in keep:
                i, j = tiles[t]
                key = owner[i, j : j + 1, :] * slots + slot[i, j : j + 1, :]
                left.append(terms[t])
                right.append(one_hot(key, slots, (3 * a + b + 4) * slots))
            got = lax.dot_general(jnp.concatenate(left, axis=1), jnp.concatenate(right, axis=1),
                                  (((1,), (1,)), ((), ())), preferred_element_type=F32)
            sums[turn(b, high_y), turn(a, high_x)] = got[0:8] + got[8:16]


def pairs(strips, halo, args, own, around):
    tiles = [(i, j) for rows, cols in strips for i in rows for j in cols]
    partner, rate, features, weight_u, lever, slot, owner, slots = args
    tx, ty, f, beads = features.shape
    nb = partner.shape[0]
    chans = rate.shape[0]
    width_h = weight_u.shape[0] // chans
    rows = beads + EXTRA
    n = len(tiles)
    out = (3, 3, 8, slots) if halo else (8, slots)
    scratch = [
        pltpu.SMEM((n * nb,), jnp.int32),
        pltpu.SMEM((n * nb,), jnp.int32),
        pltpu.VMEM((n, f, beads), BF16),
        pltpu.VMEM((2, width_h, chans * beads), BF16),
        pltpu.VMEM((nb * beads, chans * beads), F32),
        pltpu.VMEM((nb * beads, chans * beads), F32),
        pltpu.VMEM((nb // 2, beads, 2 * beads), F32),
        pltpu.VMEM((nb // 2, beads, 2 * beads), F32),
        pltpu.VMEM((nb * beads, beads), BF16),
        pltpu.VMEM((nb * beads, beads), BF16),
        pltpu.VMEM((nb // 2, 2 * EXTRA, 2 * beads), BF16),
        pltpu.VMEM((nb // 2, 2 * EXTRA, 2 * beads), BF16),
        pltpu.VMEM((9, 8, beads), F32),
        pltpu.VMEM((9, 3, 8, beads), F32),
        pltpu.VMEM((9, 16, beads), BF16),
        pltpu.SemaphoreType.DMA((len(strips),)),
    ]
    if halo:
        scratch += [pltpu.VMEM((n, 16, beads), BF16), pltpu.VMEM(((tx + 2) * (ty + 2), rows, beads), BF16),
                    pltpu.SemaphoreType.DMA((3 * tx + 6,)), pltpu.VMEM((8, slots), F32)]
    ids = jnp.asarray([i * ty + j for i, j in tiles], jnp.int32)
    shape = (tx, ty, beads, width_h, chans, nb, slots)
    return pl.pallas_call(
        lambda *refs: pairs_kernel(strips, halo, shape, *refs),
        out_shape=jax.ShapeDtypeStruct(out, F32),
        in_specs=[SMEM, SMEM, SMEM, HBM, VMEM, VMEM, VMEM, VMEM, HBM if halo else VMEM]
        + ([HBM] * 6 + [VMEM] if halo else []),
        out_specs=VMEM,
        scratch_shapes=scratch,
        compiler_params=pltpu.CompilerParams(vmem_limit_bytes=LIMIT),
        cost_estimate=pl.CostEstimate(flops=n * 150_000_000, bytes_accessed=n * 100_000, transcendentals=0),
    )(ids, partner, rate, features, weight_u, lever, slot, owner, own.reshape((tx * ty, rows, beads)), *(around if halo else []))


def rotation_rows(q):
    w, a, b, c = q
    return [
        [1 - 2 * (b * b + c * c), 2 * (a * b - w * c), 2 * (a * c + w * b)],
        [2 * (a * b + w * c), 1 - 2 * (a * a + c * c), 2 * (b * c - w * a)],
        [2 * (a * c - w * b), 2 * (b * c + w * a), 1 - 2 * (a * a + b * b)],
    ]


def integrate(q, motion, inverse, f):
    vel = [motion[r] + STEP_DT * inverse[0] * f[r] for r in range(3)]
    ang = [motion[3 + r] + STEP_DT * f[3 + r] for r in range(3)]
    old = rotation_rows(q)
    frame = [sum(old[r][c] * ang[r] for r in range(3)) * inverse[1 + c] for c in range(3)]
    om = [sum(old[r][c] * frame[c] for c in range(3)) for r in range(3)]
    w, x, y, z = q
    rate = [
        -(om[0] * x + om[1] * y + om[2] * z),
        w * om[0] + om[1] * z - om[2] * y,
        w * om[1] + om[2] * x - om[0] * z,
        w * om[2] + om[0] * y - om[1] * x,
    ]
    step = [q[r] + 0.5 * STEP_DT * rate[r] for r in range(4)]
    size = jnp.sqrt(sum(s * s for s in step))
    new = [s / size for s in step]
    turned = rotation_rows(new)
    rel = [sum(turned[r][k] * old[c][k] for k in range(3)) for r in range(3) for c in range(3)]
    return new, vel, ang, [STEP_DT * v for v in vel] + rel


def finish_kernel(totals, pose, motion, inverse, col_a, col_b, end_a, end_b, pos, lever, slot, owner,
                  moved, state, table):
    tx, ty = pos.shape[0], pos.shape[2]
    slots = totals.shape[3]
    high_x, high_y = outward("gx"), outward("gy")
    turn = lambda d, high: 1 + jnp.where(high, d, -d)
    rows_a, rows_b = end_a.shape[0] - 3 * BODY, col_a.shape[0] - BODY
    bodies = {(1, 0): (col_a, rows_b), (1, 2): (col_b, rows_b)}
    for a, end in ((0, end_a), (2, end_b)):
        for q, b in enumerate((1, 0, 2)):
            bodies[a, b] = (end, rows_a + q * BODY)
    for a in range(3):
        for b in range(3):
            f = totals[b, a]
            f = [f[r : r + 1] for r in range(6)]
            if (a, b) == (1, 1):
                q = [pose[0, 3 + r] for r in range(4)]
                mot = [motion[0, r] for r in range(6)]
                inv = [inverse[0, 0, r : r + 1, :] for r in range(4)]
            else:
                ref, at = bodies[a, b]
                third = BODY // 3
                body = sum(ref[at + k * third : at + (k + 1) * third, :].astype(F32) for k in range(3))
                body = [body[r : r + 1] for r in range(14)]
                q, mot, inv = body[0:4], body[4:10], body[10:14]
            new, vel, ang, packed = integrate(q, mot, inv, f)
            if (a, b) == (1, 1):
                centre = [pose[0, r] + STEP_DT * vel[r] for r in range(3)]
                for r, val in enumerate(centre + new + vel + ang):
                    state[0, r] = val
            packed = jnp.concatenate(packed + [jnp.zeros((4, slots), F32)], axis=0)
            table[a, b] = jnp.concatenate(split_two(packed), axis=0)

    def place(i, j, a, b):
        key = owner[i, pl.ds(j, 1), :] * slots + slot[i, pl.ds(j, 1), :]
        rows = table[1, 1] if a == 0 and b == 0 else table[turn(a, high_x), turn(b, high_y)]
        got = jnp.dot(rows, one_hot(key, slots, (3 * a + b + 4) * slots), preferred_element_type=F32)
        got = got[0:16] + got[16:32]
        lev = [lever[i, c, pl.ds(j, 1), :] for c in range(3)]
        return [got[r : r + 1] + sum(got[3 + 3 * r + c : 4 + 3 * r + c] * lev[c] for c in range(3)) for r in range(3)]

    def line(i, carry):
        for j in range(ty):
            for r, val in enumerate(place(i, j, 0, 0)):
                moved[i, r, j : j + 1, :] = pos[i, r, j : j + 1, :].astype(F32) + val - lever[i, r, j : j + 1, :]
        return carry

    lax.fori_loop(0, tx, line, 0)
    for a, b in DIRS:
        for i in range(tx) if a == 0 else [0 if a < 0 else tx - 1]:
            for j in range(ty) if b == 0 else [0 if b < 0 else ty - 1]:
                for r, val in enumerate(place(i, j, a, b)):
                    moved[i, r, j : j + 1, :] = moved[i, r, j : j + 1, :] + val


def finish(totals, pose, motion, inverse, cols, ends, pos, lever, slot, owner):
    slots = totals.shape[3]
    return pl.pallas_call(
        finish_kernel,
        out_shape=[jax.ShapeDtypeStruct(lever.shape, F32), jax.ShapeDtypeStruct((1, 13, 1, slots), F32)],
        in_specs=[VMEM] * 12,
        out_specs=[VMEM] * 2,
        scratch_shapes=[pltpu.VMEM((3, 3, 32, slots), BF16)],
        compiler_params=pltpu.CompilerParams(vmem_limit_bytes=LIMIT),
    )(totals, pose, motion, inverse, *cols, *ends, pos, lever, slot, owner)


def swap(value, axis, start):
    n = lax.axis_size(axis)
    route = []
    for c in range(start, n + start, 2):
        route += [(c % n, (c + 1) % n), ((c + 1) % n, c % n)]
    return lax.ppermute(value, axis, route)


def inside(value, axis):
    return swap(value, axis, 0)


def outside(value, axis):
    return swap(value, axis, 1)


def local(positions, features, lever, partner, body_slot, owner_dir, body_pose, body_motion,
          body_inverse, weight_u, weight_v, radial_rate):
    tx, ty = positions.shape[0], positions.shape[1]
    slots = body_pose.shape[3]
    rows = positions.shape[3] + EXTRA
    pos, lever = (jnp.transpose(v, (0, 2, 1, 3)) for v in (positions, lever))
    pose, motion = (jnp.transpose(v, (0, 2, 1, 3)) for v in (body_pose, body_motion))
    codes = jnp.transpose(partner, (2, 0, 1))
    own, col_in, col_out, row_in, row_out = project(features, pos, weight_v, pose, motion, body_inverse)
    line_a, line_b = inside(row_in, "gx"), outside(row_out, "gx")
    col_a, col_b = inside(col_in, "gy"), outside(col_out, "gy")
    high_x = outward("gx")
    bodies = [v[tx * rows :] for v in (col_in, col_a, col_b)]
    corner = lambda high: jnp.concatenate(
        [jnp.where(high, v[(tx - 1) * rows : tx * rows], v[:rows]) for v in (col_a, col_b)] + bodies, axis=0)
    end_a, end_b = inside(corner(~high_x), "gx"), outside(corner(high_x), "gx")
    args = (codes, radial_rate, features, weight_u, lever, body_slot, owner_dir, slots)
    inner = [((i,), range(1, ty - 1)) for i in range(1, tx - 1)]
    rim = [((0,), range(ty)), ((tx - 1,), range(ty)), (range(1, tx - 1), (0,)), (range(1, tx - 1), (ty - 1,))]
    first = pairs(inner, False, args, own, None)
    parts = pairs(rim, True, args, own, [col_a, col_b, line_a, line_b, end_a, end_b, first])
    mine = parts[1] + inside(parts[0], "gy")
    got = outside(jnp.stack([parts[2], mine]), "gy")
    mine = mine + got[0]
    cols = jnp.stack([inside(mine, "gy"), mine, got[1] + parts[2]])
    if lax.axis_size("gx") == 4:
        other = inside(cols, "gx")
        mine = cols[:, 1] + other[:, 0]
        got = outside(jnp.stack([cols[:, 2], mine, other[:, 2]]), "gx")
        mine = mine + got[0]
        beside = other[:, 1] + cols[:, 0] + got[2]
    else:
        mine = cols[:, 1] + inside(cols[:, 0], "gx")
        got = outside(jnp.stack([cols[:, 2], mine]), "gx")
        mine = mine + got[0]
        beside = inside(mine, "gx")
    totals = jnp.stack([beside, mine, got[1] + cols[:, 2]], axis=1)
    moved, state = finish(totals, pose, motion, body_inverse, (col_a, col_b), (end_a, end_b),
                          pos, lever, body_slot, owner_dir)
    return (jnp.transpose(moved, (0, 2, 1, 3)), jnp.transpose(state, (0, 2, 1, 3)))


def solution(mesh):
    placed = (
        P("gx", "gy", None, None),
        P("gx", "gy", None, None),
        P("gx", "gy", None, None),
        P("gx", "gy", None),
        P("gx", "gy", None),
        P("gx", "gy", None),
        P("gx", "gy", None, None),
        P("gx", "gy", None, None),
        P("gx", "gy", None, None),
        P(),
        P(),
        P(),
    )
    return jax.shard_map(
        local,
        mesh=mesh,
        in_specs=placed,
        out_specs=(P("gx", "gy", None, None), P("gx", "gy", None, None)),
        check_vma=False,
    )
```

time: 143 us -> 98.9 us (0.69)
  starting transfers between devices: 39.7 us -> 16.1 us
  Pallas kernels: 68.8 us -> 60.4 us
  waiting for transfers between devices: 23.5 us -> 15.2 us
  local copies, waits for them, and re-layouts: 9.67 us -> 2.97 us
  other arithmetic: 0 us -> 2.84 us
    ppermute x24 -> x11, starting transfers between devices: 39.7 us -> 16.1 us  [swap(): return lax.ppermute(value, axis, route)]
    pallas_call x6 -> x3, Pallas kernels: 61 us -> 52.6 us  [the longest x2 48 us: pairs(): pl.pallas_call(lambda *refs: pairs_kernel(strips, halo, shape, *refs), ou...]
    ppermute x24 -> x11, waiting for transfers between devices: 23.5 us -> 15.2 us  [swap(): return lax.ppermute(value, axis, route)]
    unnamed x73 -> x15, local copies, waits for them, and re-layouts: 9.67 us -> 2.96 us
    add x0 -> x4, other arithmetic: none -> 1.44 us  [the longest x1 0.72 us: local(): cols = jnp.stack([inside(mine, 'gy'), mine, got[1] + parts[2]])]
  transfers between devices with their start and end apart: 24 -> 11, of which waited for: 4 -> 6; matrix products, arithmetic and copies ran while one was open for 3% -> 2% of each run, Pallas kernels for 24% -> 26%
where the time goes in v2:
time: 98.9 us; the launch traced here: 98.3 us
  Pallas kernels  60.4 us (61%)
  starting transfers between devices  16.1 us (16%)
  waiting for transfers between devices  15.2 us (15%)
  local copies, waits for them, and re-layouts  2.97 us (3%)
  other arithmetic  2.84 us (3%)
    pallas_call x2, Pallas kernels, pairs(): pl.pallas_call(lambda *refs: pairs_kernel(strips, halo, shape, *refs), ou...  48 us
    ppermute x11, starting transfers between devices, swap(): return lax.ppermute(value, axis, route)  16.1 us
    ppermute x11, waiting for transfers between devices, swap(): return lax.ppermute(value, axis, route)  15.2 us
    pallas_call x1, Pallas kernels, project(): pl.pallas_call(project_kernel, grid=(tx,), out_shape=[sds(tx, ty, rows, b...  7.78 us
    pallas_call x1, Pallas kernels, finish(): pl.pallas_call(finish_kernel, out_shape=[jax.ShapeDtypeStruct(lever.shape...  4.61 us
    unnamed x15, local copies, waits for them, and re-layouts  2.96 us
  transfers between devices with their start and end apart: 11, of which 6 were waited for; matrix products, arithmetic and copies ran while one was open for 2% of the time, Pallas kernels for 26%

profile of v2, /device:TPU:0, one launch (start us, length us, event | category | flops | bytes accessed | tf_op | source)
XLA Modules:
  0.0 98.3 jit_solution(16014007019362375246)
XLA Ops:
  0.6 7.8 %shard_map.149 = (bf16[8,8,144,128]{3,2,1,0:T(8,128)(2,1)}, bf16[1200,128]{1,0:T(8,128)(2,1)}, bf16[1200,128]{1,0:T(8,128)(2,1)}, bf16[8,144,128]{2,1,0:T(8,128)(2,1)}, bf16[8,144,128]{2,1,0:T(8,128)(2,1)}) custom-call(bf16[8,8,256,128]{3,2,1,0:T(8,128)(2,1)} %refs_3_.3, bf16[8,3,8,128]{3,2,1,0:T(8,128)(2,1)} %bitcast.69, bf16[128,256]{1,0:T(8,128)(2,1)} %weight_v.1, ...), custom_call_target="tpu_custom_call" | custom-call | tf_op jit(solution)/shard_map/pallas_call | solution.py:96
  8.9 3.6 %collective-permute-start.1 = (bf16[1200,128]{1,0:T(8,128)(2,1)}, bf16[1200,128]{1,0:T(8,128)(2,1)S(1)}, u32[]{:S(2)}, u32[]{:S(2)}) collective-permute-start(bf16[1200,128]{1,0:T(8,128)(2,1)} %get-tuple-element.11), channel_id=1, source_target_pairs={{1,2},{2,1},{3,4},{4,3},{5,6},{6,5},{7,0},{0,7},{9,10},{10,9},{11,... | collective-permute-start | bytes 921608 | tf_op jit(solution)/shard_map/ppermute | solution.py:440
  12.5 1.6 %collective-permute-start.2 = (bf16[8,144,128]{2,1,0:T(8,128)(2,1)}, bf16[8,144,128]{2,1,0:T(8,128)(2,1)S(1)}, u32[]{:S(2)}, u32[]{:S(2)}) collective-permute-start(bf16[8,144,128]{2,1,0:T(8,128)(2,1)} %get-tuple-element.12), channel_id=1, source_target_pairs={{0,8},{8,0},{16,24},{24,16},{1,9},{9,1},{17,25},{25,17},{2,10},{10... | collective-permute-start | bytes 884744 | tf_op jit(solution)/shard_map/ppermute | solution.py:440
  14.1 2.5 %collective-permute-start.3 = (bf16[8,144,128]{2,1,0:T(8,128)(2,1)}, bf16[8,144,128]{2,1,0:T(8,128)(2,1)S(1)}, u32[]{:S(2)}, u32[]{:S(2)}) collective-permute-start(bf16[8,144,128]{2,1,0:T(8,128)(2,1)} %get-tuple-element.13), channel_id=1, source_target_pairs={{8,16},{16,8},{24,0},{0,24},{9,17},{17,9},{25,1},{1,25},{10,18},{1... | collective-permute-start | bytes 884744 | tf_op jit(solution)/shard_map/ppermute | solution.py:440
  16.6 3.2 %collective-permute-done.1.refs_10_.col_b = bf16[1200,128]{1,0:T(8,128)(2,1)S(1)} collective-permute-done((bf16[1200,128]{1,0:T(8,128)(2,1)}, bf16[1200,128]{1,0:T(8,128)(2,1)S(1)}, u32[]{:S(2)}, u32[]{:S(2)}) %collective-permute-start.1) | collective-permute-done | bytes 307232 | tf_op jit(solution)/shard_map/ppermute | solution.py:440
  19.8 0.8 constant_dynamic-update-slice_fusion.5
  20.5 2.0 %collective-permute-start.4 = (bf16[432,128]{1,0:T(8,128)(2,1)S(1)}, bf16[432,128]{1,0:T(8,128)(2,1)S(1)}, u32[]{:S(2)}, u32[]{:S(2)}) collective-permute-start(bf16[432,128]{1,0:T(8,128)(2,1)S(1)} %get-tuple-element.19), channel_id=1, source_target_pairs={{0,8},{8,0},{16,24},{24,16},{1,9},{9,1},{17,25},{25,17},{2,10},{10... | collective-permute-start | bytes 331784 | tf_op jit(solution)/shard_map/ppermute | solution.py:440
  22.5 2.5 %collective-permute-start.5 = (bf16[432,128]{1,0:T(8,128)(2,1)S(1)}, bf16[432,128]{1,0:T(8,128)(2,1)S(1)}, u32[]{:S(2)}, u32[]{:S(2)}) collective-permute-start(bf16[432,128]{1,0:T(8,128)(2,1)S(1)} %get-tuple-element.18), channel_id=1, source_target_pairs={{8,16},{16,8},{24,0},{0,24},{9,17},{17,9},{25,1},{1,25},{10,18},{1... | collective-permute-start | bytes 331784 | tf_op jit(solution)/shard_map/ppermute | solution.py:440
  25.0 25.7 %shard_map.150.refs_15_ = f32[8,128]{1,0:T(8,128)} custom-call(s32[36]{0:T(128)} %constant.15.clone.refs_0_, s32[6,8,8]{2,1,0:T(8,128)} %bitcast.83, f32[4]{0:T(128)} %refs_2_.3, bf16[8,8,256,128]{3,2,1,0:T(8,128)(2,1)} %refs_3_.3, bf16[512,256]{1,0:T(8,128)(2,1)} %refs_4_.3, f32[8,3,8,128]{3,2,1,0:T(8,128)} %bitcast.71, s32[8,8,128]{2,1,0:T(8,128)} %slot.1, ...), custom_call_target="tpu_custom_call" | custom-call | flops 5400000000 | bytes 3600000 | tf_op jit(solution)/shard_map/pallas_call | solution.py:326
  50.8 0.7 copy-done.4
  51.6 0.7 copy-done.3
  52.3 22.2 %shard_map.151 = f32[3,3,8,128]{3,2,1,0:T(8,128)} custom-call(s32[28]{0:T(128)} %constant.16.clone.refs_0_, s32[6,8,8]{2,1,0:T(8,128)} %bitcast.84, f32[4]{0:T(128)} %refs_2_.3, bf16[8,8,256,128]{3,2,1,0:T(8,128)(2,1)} %refs_3_.3, bf16[512,256]{1,0:T(8,128)(2,1)} %refs_4_.3, f32[8,3,8,128]{3,2,1,0:T(8,128)} %bitcast.72, s32[8,8,128]{2,1,0:T(8,128)} %slot.1, ...), custom_call_target="tpu_custom_call" | custom-call | flops 4200000000 | bytes 2800000 | tf_op jit(solution)/shard_map/pallas_call | solution.py:326
  74.5 0.7 slice_bitcast_fusion.5
  75.3 1.2 %collective-permute-done.6 = f32[3,8,128]{2,1,0:T(8,128)S(1)} collective-permute-done((f32[3,8,128]{2,1,0:T(8,128)S(1)}, f32[3,8,128]{2,1,0:T(8,128)S(1)}, u32[]{:S(2)}, u32[]{:S(2)}) %collective-permute-start.6) | collective-permute-done | bytes 12320 | tf_op jit(solution)/shard_map/ppermute | solution.py:440
  76.5 0.7 fusion.7
  77.2 1.5 %collective-permute-start.7 = (f32[2,3,8,128]{3,2,0,1:T(8,128)S(1)}, f32[2,3,8,128]{3,2,0,1:T(8,128)S(1)}, u32[]{:S(2)}, u32[]{:S(2)}) collective-permute-start(f32[2,3,8,128]{3,2,0,1:T(8,128)S(1)} %pad_maximum_fusion.3), channel_id=1, source_target_pairs={{1,2},{2,1},{3,4},{4,3},{5,6},{6,5},{7,0},{0,7},{9,10},{10,9},{11,... | collective-permute-start | bytes 73736 | tf_op jit(solution)/shard_map/ppermute | solution.py:440
  78.6 2.7 %collective-permute-done.7 = f32[2,3,8,128]{3,2,0,1:T(8,128)S(1)} collective-permute-done((f32[2,3,8,128]{3,2,0,1:T(8,128)S(1)}, f32[2,3,8,128]{3,2,0,1:T(8,128)S(1)}, u32[]{:S(2)}, u32[]{:S(2)}) %collective-permute-start.7) | collective-permute-done | bytes 24608 | tf_op jit(solution)/shard_map/ppermute | solution.py:440
  81.3 0.7 fusion.5
  82.0 0.7 slice_add_fusion.2
  83.2 0.6 collective-permute-start.9
  83.8 3.3 %collective-permute-done.9 = f32[3,3,8,128]{3,2,0,1:T(8,128)S(1)} collective-permute-done((f32[3,3,8,128]{3,2,0,1:T(8,128)S(1)}, f32[3,3,8,128]{3,2,0,1:T(8,128)S(1)}, u32[]{:S(2)}, u32[]{:S(2)}) %collective-permute-start.9) | collective-permute-done | bytes 36896 | tf_op jit(solution)/shard_map/ppermute | solution.py:440
  87.2 1.4 %collective-permute-start.10 = (f32[3,3,8,128]{3,2,1,0:T(8,128)S(1)}, f32[3,3,8,128]{3,2,1,0:T(8,128)S(1)}, u32[]{:S(2)}, u32[]{:S(2)}) collective-permute-start(f32[3,3,8,128]{3,2,1,0:T(8,128)S(1)} %pad_maximum_fusion.1), channel_id=1, source_target_pairs={{8,16},{16,8},{24,0},{0,24},{9,17},{17,9},{25,1},{1,25},{10,18},{1... | collective-permute-start | bytes 110600 | tf_op jit(solution)/shard_map/ppermute | solution.py:440
  88.6 4.4 %collective-permute-done.10 = f32[3,3,8,128]{3,2,1,0:T(8,128)S(1)} collective-permute-done((f32[3,3,8,128]{3,2,1,0:T(8,128)S(1)}, f32[3,3,8,128]{3,2,1,0:T(8,128)S(1)}, u32[]{:S(2)}, u32[]{:S(2)}) %collective-permute-start.10) | collective-permute-done | bytes 36896 | tf_op jit(solution)/shard_map/ppermute | solution.py:440
  93.6 4.6 %shard_map.152 = (f32[8,3,8,128]{3,2,1,0:T(8,128)}, f32[1,13,1,128]{3,2,1,0:T(1,128)}) custom-call(f32[3,3,8,128]{3,2,1,0:T(8,128)} %pad_maximum_fusion.2.totals, f32[1,7,1,128]{3,2,1,0:T(1,128)} %bitcast.76, f32[1,6,1,128]{3,2,1,0:T(1,128)} %bitcast.79, f32[1,1,4,128]{3,2,1,0:T(4,128)} %inverse.3, bf16[1200,128]{1,0:T(8,128)(2,1)} %copy-done, ...), custom_call_target="tpu_custom_call" | custom-call | tf_op jit(solution)/shard_map/pallas_call | solution.py:425
  (30 shorter events, 1.9 us)
Async XLA Ops:
  8.4 8.1 %collective-permute-start = (bf16[1200,128]{1,0:T(8,128)(2,1)}, bf16[1200,128]{1,0:T(8,128)(2,1)S(1)}, u32[]{:S(2)}, u32[]{:S(2)}) collective-permute-start(bf16[1200,128]{1,0:T(8,128)(2,1)} %get-tuple-element.10), channel_id=1, source_target_pairs={{0,1},{1,0},{2,3},{3,2},{4,5},{5,4},{6,7},{7,6},{8,9},{9,8},{10,11... | collective-permute-start | bytes 921608 | tf_op jit(solution)/shard_map/ppermute | solution.py:440
  8.9 10.8 %collective-permute-start.1 = (bf16[1200,128]{1,0:T(8,128)(2,1)}, bf16[1200,128]{1,0:T(8,128)(2,1)S(1)}, u32[]{:S(2)}, u32[]{:S(2)}) collective-permute-start(bf16[1200,128]{1,0:T(8,128)(2,1)} %get-tuple-element.11), channel_id=1, source_target_pairs={{1,2},{2,1},{3,4},{4,3},{5,6},{6,5},{7,0},{0,7},{9,10},{10,9},{11,... | collective-permute-start | bytes 921608 | tf_op jit(solution)/shard_map/ppermute | solution.py:440
  12.5 38.3 %collective-permute-start.2 = (bf16[8,144,128]{2,1,0:T(8,128)(2,1)}, bf16[8,144,128]{2,1,0:T(8,128)(2,1)S(1)}, u32[]{:S(2)}, u32[]{:S(2)}) collective-permute-start(bf16[8,144,128]{2,1,0:T(8,128)(2,1)} %get-tuple-element.12), channel_id=1, source_target_pairs={{0,8},{8,0},{16,24},{24,16},{1,9},{9,1},{17,25},{25,17},{2,10},{10... | collective-permute-start | bytes 884744 | tf_op jit(solution)/shard_map/ppermute | solution.py:440
  14.1 36.7 %collective-permute-start.3 = (bf16[8,144,128]{2,1,0:T(8,128)(2,1)}, bf16[8,144,128]{2,1,0:T(8,128)(2,1)S(1)}, u32[]{:S(2)}, u32[]{:S(2)}) collective-permute-start(bf16[8,144,128]{2,1,0:T(8,128)(2,1)} %get-tuple-element.13), channel_id=1, source_target_pairs={{8,16},{16,8},{24,0},{0,24},{9,17},{17,9},{25,1},{1,25},{10,18},{1... | collective-permute-start | bytes 884744 | tf_op jit(solution)/shard_map/ppermute | solution.py:440
  16.5 34.2 %copy-start = (bf16[1200,128]{1,0:T(8,128)(2,1)}, bf16[1200,128]{1,0:T(8,128)(2,1)S(1)}, u32[]{:S(2)}) copy-start(bf16[1200,128]{1,0:T(8,128)(2,1)S(1)} %collective-permute-done.refs_9_.col_a) | copy-start | bytes 921604
  19.7 31.0 %copy-start.1 = (bf16[1200,128]{1,0:T(8,128)(2,1)}, bf16[1200,128]{1,0:T(8,128)(2,1)S(1)}, u32[]{:S(2)}) copy-start(bf16[1200,128]{1,0:T(8,128)(2,1)S(1)} %collective-permute-done.1.refs_10_.col_b) | copy-start | bytes 921604
  20.5 30.3 %collective-permute-start.4 = (bf16[432,128]{1,0:T(8,128)(2,1)S(1)}, bf16[432,128]{1,0:T(8,128)(2,1)S(1)}, u32[]{:S(2)}, u32[]{:S(2)}) collective-permute-start(bf16[432,128]{1,0:T(8,128)(2,1)S(1)} %get-tuple-element.19), channel_id=1, source_target_pairs={{0,8},{8,0},{16,24},{24,16},{1,9},{9,1},{17,25},{25,17},{2,10},{10... | collective-permute-start | bytes 331784 | tf_op jit(solution)/shard_map/ppermute | solution.py:440
  22.5 28.3 %collective-permute-start.5 = (bf16[432,128]{1,0:T(8,128)(2,1)S(1)}, bf16[432,128]{1,0:T(8,128)(2,1)S(1)}, u32[]{:S(2)}, u32[]{:S(2)}) collective-permute-start(bf16[432,128]{1,0:T(8,128)(2,1)S(1)} %get-tuple-element.18), channel_id=1, source_target_pairs={{8,16},{16,8},{24,0},{0,24},{9,17},{17,9},{25,1},{1,25},{10,18},{1... | collective-permute-start | bytes 331784 | tf_op jit(solution)/shard_map/ppermute | solution.py:440
  50.8 0.7 copy-start.4
  50.8 0.8 copy-start.5
  50.8 0.8 copy-start.2
  51.6 0.7 copy-start.3
  75.3 1.2 %collective-permute-start.6 = (f32[3,8,128]{2,1,0:T(8,128)S(1)}, f32[3,8,128]{2,1,0:T(8,128)S(1)}, u32[]{:S(2)}, u32[]{:S(2)}) collective-permute-start(f32[3,8,128]{2,1,0:T(8,128)S(1)} %get-tuple-element.34), channel_id=1, source_target_pairs={{0,1},{1,0},{2,3},{3,2},{4,5},{5,4},{6,7},{7,6},{8,9},{9,8},{10,11... | collective-permute-start | bytes 36872 | tf_op jit(solution)/shard_map/ppermute | solution.py:440
  77.2 4.2 %collective-permute-start.7 = (f32[2,3,8,128]{3,2,0,1:T(8,128)S(1)}, f32[2,3,8,128]{3,2,0,1:T(8,128)S(1)}, u32[]{:S(2)}, u32[]{:S(2)}) collective-permute-start(f32[2,3,8,128]{3,2,0,1:T(8,128)S(1)} %pad_maximum_fusion.3), channel_id=1, source_target_pairs={{1,2},{2,1},{3,4},{4,3},{5,6},{6,5},{7,0},{0,7},{9,10},{10,9},{11,... | collective-permute-start | bytes 73736 | tf_op jit(solution)/shard_map/ppermute | solution.py:440
  82.0 1.2 %collective-permute-start.8 = (f32[3,8,128]{2,1,0:T(8,128)S(1)}, f32[3,8,128]{2,1,0:T(8,128)S(1)}, u32[]{:S(2)}, u32[]{:S(2)}) collective-permute-start(f32[3,8,128]{2,1,0:T(8,128)S(1)} %fusion.5), channel_id=1, source_target_pairs={{0,1},{1,0},{2,3},{3,2},{4,5},{5,4},{6,7},{7,6},{8,9},{9,8},{10,11... | collective-permute-start | bytes 36872 | tf_op jit(solution)/shard_map/ppermute | solution.py:440
  83.2 4.0 %collective-permute-start.9 = (f32[3,3,8,128]{3,2,0,1:T(8,128)S(1)}, f32[3,3,8,128]{3,2,0,1:T(8,128)S(1)}, u32[]{:S(2)}, u32[]{:S(2)}) collective-permute-start(f32[3,3,8,128]{3,2,0,1:T(8,128)S(1)} %pad_maximum_fusion), channel_id=1, source_target_pairs={{0,8},{8,0},{16,24},{24,16},{1,9},{9,1},{17,25},{25,17},{2,10},{10... | collective-permute-start | bytes 110600 | tf_op jit(solution)/shard_map/ppermute | solution.py:440
  87.2 5.8 %collective-permute-start.10 = (f32[3,3,8,128]{3,2,1,0:T(8,128)S(1)}, f32[3,3,8,128]{3,2,1,0:T(8,128)S(1)}, u32[]{:S(2)}, u32[]{:S(2)}) collective-permute-start(f32[3,3,8,128]{3,2,1,0:T(8,128)S(1)} %pad_maximum_fusion.1), channel_id=1, source_target_pairs={{8,16},{16,8},{24,0},{0,24},{9,17},{17,9},{25,1},{1,25},{10,18},{1... | collective-permute-start | bytes 110600 | tf_op jit(solution)/shard_map/ppermute | solution.py:440

commit v3 on v2

--- a/solution.py
+++ b/solution.py
@@ -13,10 +13,12 @@
 VMEM = pl.BlockSpec(memory_space=pltpu.VMEM)
 SMEM = pl.BlockSpec(memory_space=pltpu.SMEM)
 HBM = pl.BlockSpec(memory_space=pl.ANY)
-LIMIT = 56 * 2**20
+LIMIT = 24 * 2**20
 DIRS = [(-1, -1), (-1, 0), (-1, 1), (0, -1), (0, 1), (1, -1), (1, 0), (1, 1)]
 EXTRA = 16
 BODY = 48
+UNROLL = 4
+STEP = 4
 
 
 def rows_iota(rows, lanes):
@@ -48,33 +50,46 @@
     x = pl.program_id(0)
     tiles_x, tiles_y, beads = pl.num_programs(0), feat.shape[1], feat.shape[3]
     rows = beads + EXTRA
-    row = rows_iota(8, beads)
+    step = feat.shape[0]
+    second = jnp.where(rows_iota(8, beads) < 3, 1.0, 0.0)
     high_x, high_y = outward("gx"), outward("gy")
-    for y in range(0, tiles_y, 2):
-        both = jnp.concatenate([feat[0, y], feat[0, y + 1]], axis=1)
-        v = jnp.dot(weight_v[...], both, preferred_element_type=F32).astype(BF16)
-        for e in range(2):
-            own[0, y + e, 0:beads, :] = v[:, e * beads : (e + 1) * beads].T
-            px, py, pz = (jnp.broadcast_to(pos[0, c, y + e : y + e + 1, :].astype(F32), (8, beads)) for c in range(3))
-            norm = -0.25 * (px * px + py * py + pz * pz)
-            n1, n2, n3 = (part.astype(F32) for part in split_three(norm))
-            first = px
-            for r, val in ((1, py), (2, pz), (3, px), (4, py), (5, n1), (6, n2), (7, n3)):
-                first = jnp.where(row == r, val, first)
-            second = jnp.where(row < 3, 1.0, 0.0)
-            own[0, y + e, beads:rows, :] = jnp.concatenate([first, second], axis=0).astype(BF16)
-    at = pl.ds(pl.multiple_of(x * rows, 16), rows)
-    low, high = own[0, 0], own[0, tiles_y - 1]
-    col_in[at, :] = jnp.where(high_y, low, high)
-    col_out[at, :] = jnp.where(high_y, high, low)
-
-    @pl.when(x == jnp.where(high_x, 0, tiles_x - 1))
+    for z in range(step):
+        for y in range(0, tiles_y, 2):
+            both = jnp.concatenate([feat[z, y], feat[z, y + 1]], axis=1)
+            v = jnp.dot(weight_v[...], both, preferred_element_type=F32).astype(BF16)
+            for e in range(2):
+                own[z, y + e, 0:beads, :] = v[:, e * beads : (e + 1) * beads].T
+        px, py, pz = (pos[z, c].astype(F32) for c in range(3))
+        norm = -0.25 * (px * px + py * py + pz * pz)
+        none = jnp.zeros_like(px)
+        parts = [px, py, pz, none, none] + [part.astype(F32) for part in split_three(norm)]
+        for y in range(tiles_y):
+            first = jnp.concatenate([part[y : y + 1] for part in parts], axis=0)
+            own[z, y, beads:rows, :] = jnp.concatenate([first, second], axis=0).astype(BF16)
+        at = pl.ds(pl.multiple_of((x * step + z) * rows, 16), rows)
+        low, high = own[z, 0], own[z, tiles_y - 1]
+        col_in[at, :] = jnp.where(high_y, low, high)
+        col_out[at, :] = jnp.where(high_y, high, low)
+
+    @pl.when(x == 0)
     def _():
-        row_in[...] = own[0]
-
-    @pl.when(x == jnp.where(high_x, tiles_x - 1, 0))
+        @pl.when(high_x)
+        def _():
+            row_in[...] = own[0]
+
+        @pl.when(~high_x)
+        def _():
+            row_out[...] = own[0]
+
+    @pl.when(x == tiles_x - 1)
     def _():
-        row_out[...] = own[0]
+        @pl.when(high_x)
+        def _():
+            row_out[...] = own[step - 1]
+
+        @pl.when(~high_x)
+        def _():
+            row_in[...] = own[step - 1]
 
     @pl.when(x == 0)
     def _():
@@ -95,15 +110,15 @@
     col = (tx * rows + BODY, beads)
     return pl.pallas_call(
         project_kernel,
-        grid=(tx,),
+        grid=(tx // STEP,),
         out_shape=[sds(tx, ty, rows, beads), sds(*col), sds(*col), sds(ty, rows, beads), sds(ty, rows, beads)],
         in_specs=[
-            pl.BlockSpec((1, ty, f, beads), lambda i: (i, 0, 0, 0)),
-            pl.BlockSpec((1, 3, ty, beads), lambda i: (i, 0, 0, 0)),
+            pl.BlockSpec((STEP, ty, f, beads), lambda i: (i, 0, 0, 0)),
+            pl.BlockSpec((STEP, 3, ty, beads), lambda i: (i, 0, 0, 0)),
             whole(weight_v.shape), whole(pose.shape), whole(motion.shape), whole(inverse.shape),
         ],
         out_specs=[
-            pl.BlockSpec((1, ty, rows, beads), lambda i: (i, 0, 0, 0)),
+            pl.BlockSpec((STEP, ty, rows, beads), lambda i: (i, 0, 0, 0)),
             whole(col), whole(col), whole((ty, rows, beads)), whole((ty, rows, beads)),
         ],
         compiler_params=pltpu.CompilerParams(vmem_limit_bytes=LIMIT),
@@ -118,10 +133,11 @@
     take = lambda k: [refs.pop(0) for _ in range(k)]
     ids, partner, rate, features, weight_u, lever, slot, owner, own = take(9)
     around = take(7) if halo else []
-    sums = refs.pop(0)
+    sums = take(3 if halo else 1)
     where_to, code_of = take(2)
-    feat, ub, sa, sb, za, zb, ca, cb, wa, wb, high_of, norm_of, extra_of, fsem = take(14)
-    terms, vp, vsem, total = take(4) if halo else (None, own, None, sums)
+    feat, shift_of, norm_of, terms, fsem = take(5)
+    sets = [take(7), take(7)]
+    vp, vsem, total, parts = take(4) if halo else (own, None, sums[0], None)
     wide = ty + 2
     here = lambda i, j: (i + 1) * wide + j + 1 if halo else i * ty + j
     side = chans * width_h
@@ -153,8 +169,6 @@
         copies = [pltpu.make_async_copy(src, dst, vsem.at[q]) for q, (src, dst) in enumerate(pairs_of)]
         for copy in copies:
             copy.start()
-    wa[...] = jnp.zeros_like(wa)
-    wb[...] = jnp.zeros_like(wb)
     total[...] = around[6][...] if halo else jnp.zeros_like(total)
 
     def where_is(t):
@@ -170,15 +184,14 @@
         return carry
 
     row8 = rows_iota(8, beads)
-    row16 = rows_iota(16, beads)
+    row16 = rows_iota(EXTRA, beads)
     for c in range(9):
         a, b = c // 3 - 1, c % 3 - 1
-        high_of[c] = jnp.where(row8 == 3, -0.5 * a, jnp.where(row8 == 4, -0.5 * b, 0.0))
-        for q, val in enumerate((0.5 * a, 0.5 * b, -0.25 * (a * a + b * b))):
+        shift_of[c] = jnp.where(row16 == 3, 1.0 * a, jnp.where(row16 == 4, 1.0 * b, 0.0)).astype(BF16)
+        for q, val in enumerate((-0.5 * a, -0.5 * b, -0.25 * (a * a + b * b))):
             norm_of[c, q] = jnp.full((8, beads), val, F32)
-        extra_of[c] = jnp.where(row16 == 11, 1.0 * a, jnp.where(row16 == 12, 1.0 * b, 0.0)).astype(BF16)
-
-    def make_u(s):
+
+    def make_u(s, ub):
         both = jnp.concatenate([feat[2 * s], feat[2 * s + 1]], axis=1)
         u = jnp.dot(weight_u[...], both, preferred_element_type=F32).astype(BF16)
         for e in range(2):
@@ -186,36 +199,44 @@
                 ub[e, :, k * beads : (k + 1) * beads] = u[
                     k * width_h : (k + 1) * width_h, e * beads : (e + 1) * beads]
 
-    def scores(t, e, buf, zbuf, wz):
+    def moved_block(t, m):
+        return vp[where_to[t * nb + m], beads : beads + EXTRA, :] + shift_of[code_of[t * nb + m]]
+
+    def products(t, ub, e, buf, g):
+        cols = slice(2 * g * beads, 2 * (g + 1) * beads)
+        lhs = jnp.concatenate([vp[where_to[t * nb + m], 0:beads, :] for m in range(nb)], axis=0)
+        buf[:, cols] = jnp.dot(lhs, ub[e, :, cols], preferred_element_type=F32)
+
+    def scores(t, ub, e, buf, zbuf):
         i, j = where_is(t)
-        lhs, feats = [], []
-        mine = vp[here(i, j), beads : beads + EXTRA, :].astype(F32)
-        up = mine[0:8]
-        bx, by = (jnp.broadcast_to(up[c : c + 1], (8, beads)) for c in (0, 1))
-        bn = jnp.broadcast_to(up[5:6] + up[6:7] + up[7:8], (8, beads))
-        fixed = jnp.where(row8 < 3, 0.5 * up, jnp.where(row8 >= 5, 1.0, 0.0))
+        up = vp[here(i, j), beads : beads + EXTRA, :].astype(F32)[0:8]
+        px, py = (jnp.broadcast_to(0.5 * up[c : c + 1], (8, beads)) for c in (0, 1))
+        high = jnp.where(row8 < 3, 0.5 * up, jnp.where(row8 == 3, px, jnp.where(row8 == 4, py, 1.0)))
+        low = jnp.where(row8 < 3, pltpu.roll(up, 3, 0), 0.0)
+        mine = jnp.concatenate([high, low], axis=0).astype(BF16)
+        none = jnp.zeros_like(mine)
+        mine = jnp.concatenate([jnp.concatenate([mine, none], axis=1), jnp.concatenate([none, mine], axis=1)], axis=0)
+        feats = []
         for m in range(nb):
-            there, code = where_to[t * nb + m], code_of[t * nb + m]
-            lhs.append(vp[there, 0:beads, :])
-            feats.append(vp[there, beads : beads + EXTRA, :])
-            high = fixed + high_of[code]
-            norm = bn + bx * norm_of[code, 0] + by * norm_of[code, 1] + norm_of[code, 2]
+            code = code_of[t * nb + m]
+            block = moved_block(t, m).astype(F32)
+            up = block[0:8]
+            qx, qy = (jnp.broadcast_to(up[c : c + 1], (8, beads)) for c in (0, 1))
+            norm = jnp.broadcast_to(up[5:6] + up[6:7] + up[7:8], (8, beads)) + norm_of[code, 2]
+            norm = norm + qx * norm_of[code, 0] + qy * norm_of[code, 1]
             n1 = norm.astype(BF16).astype(F32)
             rest = norm - n1
             n2 = rest.astype(BF16).astype(F32)
-            low = jnp.where(row8 == 0, n1, jnp.where(row8 == 1, n2, jnp.where(row8 == 2, rest - n2, 0.0)))
-            wz[m // 2, EXTRA * (m % 2) : EXTRA * (m % 2 + 1), (m % 2) * beads : (m % 2 + 1) * beads] = (
-                jnp.concatenate([high, low], axis=0).astype(BF16))
-        for h in range(nb // 2):
-            left = jnp.concatenate([feats[2 * h], feats[2 * h + 1]], axis=0)
-            zbuf[h] = lax.dot_general(left, wz[h], (((0,), (0,)), ((), ())), preferred_element_type=F32)
-        buf[...] = jnp.dot(jnp.concatenate(lhs, axis=0), ub[e], preferred_element_type=F32)
-
-    def couples(buf, zbuf, cbuf):
+            high = jnp.where(row8 < 5, up, jnp.where(row8 == 5, n1, jnp.where(row8 == 6, n2, rest - n2)))
+            feats.append(jnp.concatenate([high, block[8:16]], axis=0).astype(BF16))
+        left = jnp.concatenate([jnp.concatenate(feats[h::2], axis=1) for h in range(2)], axis=0)
+        zbuf[...] = lax.dot_general(left, mine, (((0,), (0,)), ((), ())), preferred_element_type=F32)
+
+    def couples(buf, zbuf, cbuf, which):
         step = 16
-        for m in range(nb):
+        for m in which:
             for r in range(0, beads, step):
-                z = zbuf[m // 2, r : r + step, (m % 2) * beads : (m % 2 + 1) * beads]
+                z = zbuf[m // 2 * beads + r : m // 2 * beads + r + step, (m % 2) * beads : (m % 2 + 1) * beads]
                 env = jnp.maximum(1.0 + z, 0.0)
                 total = None
                 for k in range(chans):
@@ -226,56 +247,82 @@
 
     def gather(t, cbuf):
         i, j = where_is(t)
-        lhs = []
-        for m in range(nb):
-            lhs.append(vp[where_to[t * nb + m], beads : beads + EXTRA, :] + extra_of[code_of[t * nb + m]])
-        out = jnp.dot(jnp.concatenate(lhs, axis=1), cbuf[...], preferred_element_type=F32)
-        out = out * (1.0 / width_h)
+        lhs = jnp.concatenate([moved_block(t, m) for m in range(nb)], axis=1)
+        out = jnp.dot(lhs, cbuf[...], preferred_element_type=F32) * (1.0 / width_h)
         mine = vp[here(i, j), beads : beads + EXTRA, :].astype(F32)
         w = out[8:9]
-        fx = mine[0:1] * w - out[0:1] - out[11:12]
-        fy = mine[1:2] * w - out[1:2] - out[12:13]
+        fx = mine[0:1] * w - out[0:1] - out[3:4]
+        fy = mine[1:2] * w - out[1:2] - out[4:5]
         fz = mine[2:3] * w - out[2:3]
         lx, ly, lz = (lever[i, c, pl.ds(j, 1), :] for c in range(3))
         value = jnp.concatenate(
             [fx, fy, fz, ly * fz - lz * fy, lz * fx - lx * fz, lx * fy - ly * fx,
              jnp.zeros((2, beads), F32)], axis=0)
         term = jnp.concatenate(split_two(value), axis=0)
-        if halo:
-            terms[t] = term
-        key = owner[i, pl.ds(j, 1), :] * slots + slot[i, pl.ds(j, 1), :]
-        got = lax.dot_general(term, one_hot(key, slots, 4 * slots), (((1,), (1,)), ((), ())),
-                              preferred_element_type=F32)
+        terms[t] = term
+
+    def add_up(s):
+        left, right = [], []
+        for t in (2 * s, 2 * s + 1):
+            i, j = where_is(t)
+            key = owner[i, pl.ds(j, 1), :] * slots + slot[i, pl.ds(j, 1), :]
+            left.append(terms[t])
+            right.append(one_hot(key, slots, 4 * slots))
+        got = lax.dot_general(jnp.concatenate(left, axis=1), jnp.concatenate(right, axis=1),
+                              (((1,), (1,)), ((), ())), preferred_element_type=F32)
         return got[0:8] + got[8:16]
 
     lax.fori_loop(0, n, prepare, 0)
     for load in loads:
         load.wait()
-    make_u(0)
+    last = n // 2 - 1
+
+    def fill(s, into):
+        ub, sa, sb, za, zb, _, _ = into
+        scores(2 * s, ub, 0, sa, za)
+        scores(2 * s + 1, ub, 1, sb, zb)
+        for g in range(chans // 2):
+            products(2 * s, ub, 0, sa, g)
+            products(2 * s + 1, ub, 1, sb, g)
+
+    def half(s, now, later):
+        _, sa, sb, za, zb, ca, cb = now
+        before = jnp.maximum(s - 1, 0)
+        nxt = jnp.minimum(s + 1, last)
+        scores(2 * nxt + 0, later[0], 0, later[1], later[3])
+        products(2 * nxt + 0, later[0], 0, later[1], 0)
+        couples(sa, za, ca, range(0, 3))
+        products(2 * nxt + 0, later[0], 0, later[1], 1)
+        couples(sa, za, ca, range(3, 6))
+        scores(2 * nxt + 1, later[0], 1, later[2], later[4])
+        products(2 * nxt + 1, later[0], 1, later[2], 0)
+        couples(sb, zb, cb, range(0, 3))
+        products(2 * nxt + 1, later[0], 1, later[2], 1)
+        couples(sb, zb, cb, range(3, 6))
+        make_u(jnp.minimum(s + 2, last), now[0])
+        gather(2 * before, later[5])
+        gather(2 * before + 1, later[6])
+        total[...] = total[...] + jnp.where(s == 0, 0.0, add_up(before))
+
+    make_u(0, sets[0][0])
+    make_u(min(1, last), sets[1][0])
     if halo:
         for copy in copies:
             copy.wait()
-    scores(0, 0, sa, za, wa)
-
-    def body(s, carry):
-        before = jnp.maximum(2 * s - 1, 0)
-        later = jnp.minimum(s + 1, n // 2 - 1)
-
-        scores(2 * s + 1, 1, sb, zb, wb)
-        old = gather(before, cb)
-        couples(sa, za, ca)
-        make_u(later)
-        scores(2 * later, 0, sa, za, wa)
-        new = gather(2 * s, ca)
-        couples(sb, zb, cb)
-        total[...] = total[...] + jnp.where(s == 0, 0.0, old) + new
+    fill(0, sets[0])
+
+    def body(g, carry):
+        half(2 * g, sets[0], sets[1])
+        half(2 * g + 1, sets[1], sets[0])
         return carry
 
-    lax.fori_loop(0, n // 2, body, 0)
-    total[...] = total[...] + gather(n - 1, cb)
+    lax.fori_loop(0, n // 4, body, 0)
+    gather(n - 2, sets[1][5])
+    gather(n - 1, sets[1][6])
+    total[...] = total[...] + add_up(last)
     if halo:
         turn = lambda d, high: 1 + jnp.where(high, d, -d)
-        sums[1, 1] = total[...]
+        parts[1, 1] = total[...]
         for a, b in DIRS:
             keep = [t for t, (i, j) in enumerate(tiles)
                     if (a == 0 or i == (0 if a < 0 else tx - 1)) and (b == 0 or j == (0 if b < 0 else ty - 1))]
@@ -287,7 +334,9 @@
                 right.append(one_hot(key, slots, (3 * a + b + 4) * slots))
             got = lax.dot_general(jnp.concatenate(left, axis=1), jnp.concatenate(right, axis=1),
                                   (((1,), (1,)), ((), ())), preferred_element_type=F32)
-            sums[turn(b, high_y), turn(a, high_x)] = got[0:8] + got[8:16]
+            parts[turn(b, high_y), turn(a, high_x)] = got[0:8] + got[8:16]
+        for q in range(3):
+            sums[q][...] = parts[q]
 
 
 def pairs(strips, halo, args, own, around):
@@ -299,36 +348,37 @@
     width_h = weight_u.shape[0] // chans
     rows = beads + EXTRA
     n = len(tiles)
-    out = (3, 3, 8, slots) if halo else (8, slots)
+    out = jax.ShapeDtypeStruct((3, 8, slots) if halo else (8, slots), F32)
     scratch = [
         pltpu.SMEM((n * nb,), jnp.int32),
         pltpu.SMEM((n * nb,), jnp.int32),
         pltpu.VMEM((n, f, beads), BF16),
+        pltpu.VMEM((9, EXTRA, beads), BF16),
+        pltpu.VMEM((9, 3, 8, beads), F32),
+        pltpu.VMEM((n, 16, beads), BF16),
+        pltpu.SemaphoreType.DMA((len(strips),)),
+    ]
+    scratch += 2 * [
         pltpu.VMEM((2, width_h, chans * beads), BF16),
         pltpu.VMEM((nb * beads, chans * beads), F32),
         pltpu.VMEM((nb * beads, chans * beads), F32),
-        pltpu.VMEM((nb // 2, beads, 2 * beads), F32),
-        pltpu.VMEM((nb // 2, beads, 2 * beads), F32),
+        pltpu.VMEM((nb // 2 * beads, 2 * beads), F32),
+        pltpu.VMEM((nb // 2 * beads, 2 * beads), F32),
         pltpu.VMEM((nb * beads, beads), BF16),
         pltpu.VMEM((nb * beads, beads), BF16),
-        pltpu.VMEM((nb // 2, 2 * EXTRA, 2 * beads), BF16),
-        pltpu.VMEM((nb // 2, 2 * EXTRA, 2 * beads), BF16),
-        pltpu.VMEM((9, 8, beads), F32),
-        pltpu.VMEM((9, 3, 8, beads), F32),
-        pltpu.VMEM((9, 16, beads), BF16),
-        pltpu.SemaphoreType.DMA((len(strips),)),
     ]
     if halo:
-        scratch += [pltpu.VMEM((n, 16, beads), BF16), pltpu.VMEM(((tx + 2) * (ty + 2), rows, beads), BF16),
-                    pltpu.SemaphoreType.DMA((3 * tx + 6,)), pltpu.VMEM((8, slots), F32)]
+        scratch += [pltpu.VMEM(((tx + 2) * (ty + 2), rows, beads), BF16),
+                    pltpu.SemaphoreType.DMA((3 * tx + 6,)), pltpu.VMEM((8, slots), F32),
+                    pltpu.VMEM((3, 3, 8, slots), F32)]
     ids = jnp.asarray([i * ty + j for i, j in tiles], jnp.int32)
     shape = (tx, ty, beads, width_h, chans, nb, slots)
     return pl.pallas_call(
         lambda *refs: pairs_kernel(strips, halo, shape, *refs),
-        out_shape=jax.ShapeDtypeStruct(out, F32),
+        out_shape=[out] * (3 if halo else 1),
         in_specs=[SMEM, SMEM, SMEM, HBM, VMEM, VMEM, VMEM, VMEM, HBM if halo else VMEM]
         + ([HBM] * 6 + [VMEM] if halo else []),
-        out_specs=VMEM,
+        out_specs=[VMEM] * (3 if halo else 1),
         scratch_shapes=scratch,
         compiler_params=pltpu.CompilerParams(vmem_limit_bytes=LIMIT),
         cost_estimate=pl.CostEstimate(flops=n * 150_000_000, bytes_accessed=n * 100_000, transcendentals=0),
@@ -365,10 +415,15 @@
     return new, vel, ang, [STEP_DT * v for v in vel] + rel
 
 
-def finish_kernel(totals, pose, motion, inverse, col_a, col_b, end_a, end_b, pos, lever, slot, owner,
+def finish_kernel(count, *refs):
+    sums, refs = refs[:count], refs[count:]
+    finish_body(sums, *refs)
+
+
+def finish_body(sums, pose, motion, inverse, col_a, col_b, end_a, end_b, pos, lever, slot, owner,
                   moved, state, table):
     tx, ty = pos.shape[0], pos.shape[2]
-    slots = totals.shape[3]
+    slots = owner.shape[2]
     high_x, high_y = outward("gx"), outward("gy")
     turn = lambda d, high: 1 + jnp.where(high, d, -d)
     rows_a, rows_b = end_a.shape[0] - 3 * BODY, col_a.shape[0] - BODY
@@ -376,9 +431,15 @@
     for a, end in ((0, end_a), (2, end_b)):
         for q, b in enumerate((1, 0, 2)):
             bodies[a, b] = (end, rows_a + q * BODY)
+    if len(sums) == 1:
+        totals = lambda b, a: sums[0][a, b]
+    else:
+        cols, other, got = sums
+        totals = lambda b, a: (other[1, b] + cols[0, b] + got[2, b], cols[1, b] + other[0, b] + got[0, b],
+                               got[1, b] + cols[2, b])[a]
     for a in range(3):
         for b in range(3):
-            f = totals[b, a]
+            f = totals(b, a)
             f = [f[r : r + 1] for r in range(6)]
             if (a, b) == (1, 1):
                 q = [pose[0, 3 + r] for r in range(4)]
@@ -412,7 +473,7 @@
                 moved[i, r, j : j + 1, :] = pos[i, r, j : j + 1, :].astype(F32) + val - lever[i, r, j : j + 1, :]
         return carry
 
-    lax.fori_loop(0, tx, line, 0)
+    lax.fori_loop(0, tx, line, 0, unroll=UNROLL)
     for a, b in DIRS:
         for i in range(tx) if a == 0 else [0 if a < 0 else tx - 1]:
             for j in range(ty) if b == 0 else [0 if b < 0 else ty - 1]:
@@ -420,16 +481,16 @@
                     moved[i, r, j : j + 1, :] = moved[i, r, j : j + 1, :] + val
 
 
-def finish(totals, pose, motion, inverse, cols, ends, pos, lever, slot, owner):
-    slots = totals.shape[3]
+def finish(sums, pose, motion, inverse, cols, ends, pos, lever, slot, owner):
+    slots = pose.shape[3]
     return pl.pallas_call(
-        finish_kernel,
+        lambda *refs: finish_kernel(len(sums), *refs),
         out_shape=[jax.ShapeDtypeStruct(lever.shape, F32), jax.ShapeDtypeStruct((1, 13, 1, slots), F32)],
-        in_specs=[VMEM] * 12,
+        in_specs=[VMEM] * (11 + len(sums)),
         out_specs=[VMEM] * 2,
         scratch_shapes=[pltpu.VMEM((3, 3, 32, slots), BF16)],
         compiler_params=pltpu.CompilerParams(vmem_limit_bytes=LIMIT),
-    )(totals, pose, motion, inverse, *cols, *ends, pos, lever, slot, owner)
+    )(*sums, pose, motion, inverse, *cols, *ends, pos, lever, slot, owner)
 
 
 def swap(value, axis, start):
@@ -467,25 +528,22 @@
     args = (codes, radial_rate, features, weight_u, lever, body_slot, owner_dir, slots)
     inner = [((i,), range(1, ty - 1)) for i in range(1, tx - 1)]
     rim = [((0,), range(ty)), ((tx - 1,), range(ty)), (range(1, tx - 1), (0,)), (range(1, tx - 1), (ty - 1,))]
-    first = pairs(inner, False, args, own, None)
+    (first,) = pairs(inner, False, args, own, None)
     parts = pairs(rim, True, args, own, [col_a, col_b, line_a, line_b, end_a, end_b, first])
     mine = parts[1] + inside(parts[0], "gy")
     got = outside(jnp.stack([parts[2], mine]), "gy")
     mine = mine + got[0]
-    cols = jnp.stack([inside(mine, "gy"), mine, got[1] + parts[2]])
+    cols = jnp.stack([inside(mine, "gy"), mine, got[1] + parts[2]], axis=1)
     if lax.axis_size("gx") == 4:
         other = inside(cols, "gx")
-        mine = cols[:, 1] + other[:, 0]
-        got = outside(jnp.stack([cols[:, 2], mine, other[:, 2]]), "gx")
+        got = outside(jnp.stack([cols[2], cols[1] + other[0], other[2]]), "gx")
+        sums = [cols, other, got]
+    else:
+        mine = cols[1] + inside(cols[0], "gx")
+        got = outside(jnp.stack([cols[2], mine]), "gx")
         mine = mine + got[0]
-        beside = other[:, 1] + cols[:, 0] + got[2]
-    else:
-        mine = cols[:, 1] + inside(cols[:, 0], "gx")
-        got = outside(jnp.stack([cols[:, 2], mine]), "gx")
-        mine = mine + got[0]
-        beside = inside(mine, "gx")
-    totals = jnp.stack([beside, mine, got[1] + cols[:, 2]], axis=1)
-    moved, state = finish(totals, pose, motion, body_inverse, (col_a, col_b), (end_a, end_b),
+        sums = [jnp.stack([inside(mine, "gx"), mine, got[1] + cols[2]])]
+    moved, state = finish(sums, pose, motion, body_inverse, (col_a, col_b), (end_a, end_b),
                           pos, lever, body_slot, owner_dir)
     return (jnp.transpose(moved, (0, 2, 1, 3)), jnp.transpose(state, (0, 2, 1, 3)))
 

time: 98.9 us -> 87.2 us (0.88)
  Pallas kernels: 60.4 us -> 44.9 us
  local copies, waits for them, and re-layouts: 2.97 us -> 9.1 us
  other arithmetic: 2.84 us -> 0.08 us
    pallas_call x2, Pallas kernels: 48 us -> 40.2 us  [pairs(): pl.pallas_call(lambda *refs: pairs_kernel(strips, halo, shape, *refs), ou...]
    pallas_call x2, Pallas kernels: 12.4 us -> 4.69 us  [the longest x1 2.45 us: finish(): pl.pallas_call(lambda *refs: finish_kernel(len(sums), *refs), out_shape=[...]
    unnamed x15 -> x40, local copies, waits for them, and re-layouts: 2.96 us -> 9.09 us
  transfers between devices with their start and end apart: 11 -> 11, of which waited for: 6 -> 6; matrix products, arithmetic and copies ran while one was open for 2% -> 0% of each run, Pallas kernels for 26% -> 25%
where the time goes in v3:
time: 87.2 us; the launch traced here: 86.8 us
  Pallas kernels  44.9 us (51%)
  starting transfers between devices  16 us (18%)
  waiting for transfers between devices  15.9 us (18%)
  local copies, waits for them, and re-layouts  9.1 us (10%)
    pallas_call x2, Pallas kernels, pairs(): pl.pallas_call(lambda *refs: pairs_kernel(strips, halo, shape, *refs), ou...  40.2 us
    ppermute x11, starting transfers between devices, swap(): return lax.ppermute(value, axis, route)  16 us
    ppermute x11, waiting for transfers between devices, swap(): return lax.ppermute(value, axis, route)  15.9 us
    unnamed x40, local copies, waits for them, and re-layouts  9.09 us
    pallas_call x1, Pallas kernels, finish(): pl.pallas_call(lambda *refs: finish_kernel(len(sums), *refs), out_shape=[...  2.45 us
    pallas_call x1, Pallas kernels, project(): pl.pallas_call(project_kernel, grid=(tx // STEP,), out_shape=[sds(tx, ty,...  2.24 us
  transfers between devices with their start and end apart: 11, of which 6 were waited for; matrix products, arithmetic and copies ran while one was open for 0% of the time, Pallas kernels for 25%

profile of v3, /device:TPU:0, one launch (start us, length us, event | category | flops | bytes accessed | tf_op | source)
XLA Modules:
  0.0 86.8 jit_solution(12714425071860867776)
XLA Ops:
  0.7 2.2 %copy-done = bf16[8,8,256,128]{3,2,1,0:T(8,128)(2,1)S(1)} copy-done((bf16[8,8,256,128]{3,2,1,0:T(8,128)(2,1)S(1)}, bf16[8,8,256,128]{3,2,1,0:T(8,128)(2,1)}, u32[]{:S(2)}) %copy-start) | copy-done | bytes 4194328
  2.9 0.8 copy-done.2
  3.7 0.8 copy-done.5
  4.5 0.7 copy-done.8
  6.6 2.2 %shard_map.149 = (bf16[8,8,144,128]{3,2,1,0:T(8,128)(2,1)S(1)}, bf16[1200,128]{1,0:T(8,128)(2,1)S(1)}, bf16[1200,128]{1,0:T(8,128)(2,1)}, bf16[8,144,128]{2,1,0:T(8,128)(2,1)}, bf16[8,144,128]{2,1,0:T(8,128)(2,1)}) custom-call(bf16[8,8,256,128]{3,2,1,0:T(8,128)(2,1)S(1)} %copy-done, bf16[8,3,8,128]{3,2,1,0:T(8,128)(2,1)S(1)} %bitcast.30, ...), custom_call_target="tpu_custom_call" | custom-call | tf_op jit(solution)/shard_map/pallas_call | solution.py:111
  9.2 3.6 %collective-permute-start.1 = (bf16[1200,128]{1,0:T(8,128)(2,1)}, bf16[1200,128]{1,0:T(8,128)(2,1)S(1)}, u32[]{:S(2)}, u32[]{:S(2)}) collective-permute-start(bf16[1200,128]{1,0:T(8,128)(2,1)} %get-tuple-element.14), channel_id=1, source_target_pairs={{1,2},{2,1},{3,4},{4,3},{5,6},{6,5},{7,0},{0,7},{9,10},{10,9},{11,... | collective-permute-start | bytes 921608 | tf_op jit(solution)/shard_map/ppermute | solution.py:501
  12.8 1.6 %collective-permute-start.2 = (bf16[8,144,128]{2,1,0:T(8,128)(2,1)}, bf16[8,144,128]{2,1,0:T(8,128)(2,1)}, u32[]{:S(2)}, u32[]{:S(2)}) collective-permute-start(bf16[8,144,128]{2,1,0:T(8,128)(2,1)} %get-tuple-element.15), channel_id=1, source_target_pairs={{0,8},{8,0},{16,24},{24,16},{1,9},{9,1},{17,25},{25,17},{2,10},{10... | collective-permute-start | bytes 884744 | tf_op jit(solution)/shard_map/ppermute | solution.py:501
  14.4 2.5 %collective-permute-start.3 = (bf16[8,144,128]{2,1,0:T(8,128)(2,1)}, bf16[8,144,128]{2,1,0:T(8,128)(2,1)}, u32[]{:S(2)}, u32[]{:S(2)}) collective-permute-start(bf16[8,144,128]{2,1,0:T(8,128)(2,1)} %get-tuple-element.16), channel_id=1, source_target_pairs={{8,16},{16,8},{24,0},{0,24},{9,17},{17,9},{25,1},{1,25},{10,18},{1... | collective-permute-start | bytes 884744 | tf_op jit(solution)/shard_map/ppermute | solution.py:501
  16.9 3.2 %collective-permute-done.1.refs_10_.refs_7_ = bf16[1200,128]{1,0:T(8,128)(2,1)S(1)} collective-permute-done((bf16[1200,128]{1,0:T(8,128)(2,1)}, bf16[1200,128]{1,0:T(8,128)(2,1)S(1)}, u32[]{:S(2)}, u32[]{:S(2)}) %collective-permute-start.1) | collective-permute-done | bytes 307232 | tf_op jit(solution)/shard_map/ppermute | solution.py:501
  20.1 1.8 %collective-permute-start.4 = (bf16[432,128]{1,0:T(8,128)(2,1)S(1)}, bf16[432,128]{1,0:T(8,128)(2,1)S(1)}, u32[]{:S(2)}, u32[]{:S(2)}) collective-permute-start(bf16[432,128]{1,0:T(8,128)(2,1)S(1)} %get-tuple-element.25), channel_id=1, source_target_pairs={{0,8},{8,0},{16,24},{24,16},{1,9},{9,1},{17,25},{25,17},{2,10},{10... | collective-permute-start | bytes 331784 | tf_op jit(solution)/shard_map/ppermute | solution.py:501
  21.9 2.5 %collective-permute-start.5 = (bf16[432,128]{1,0:T(8,128)(2,1)S(1)}, bf16[432,128]{1,0:T(8,128)(2,1)S(1)}, u32[]{:S(2)}, u32[]{:S(2)}) collective-permute-start(bf16[432,128]{1,0:T(8,128)(2,1)S(1)} %get-tuple-element.24), channel_id=1, source_target_pairs={{8,16},{16,8},{24,0},{0,24},{9,17},{17,9},{25,1},{1,25},{10,18},{1... | collective-permute-start | bytes 331784 | tf_op jit(solution)/shard_map/ppermute | solution.py:501
  24.5 2.2 %copy-done.1 = bf16[8,8,256,128]{3,2,1,0:T(8,128)(2,1)S(1)} copy-done((bf16[8,8,256,128]{3,2,1,0:T(8,128)(2,1)S(1)}, bf16[8,8,256,128]{3,2,1,0:T(8,128)(2,1)}, u32[]{:S(2)}) %copy-start.1) | copy-done | bytes 4194328
  26.6 0.9 %copy-done.14 = bf16[512,256]{1,0:T(8,128)(2,1)S(1)} copy-done((bf16[512,256]{1,0:T(8,128)(2,1)S(1)}, bf16[512,256]{1,0:T(8,128)(2,1)}, u32[]{:S(2)}) %copy-start.14) | copy-done | bytes 262168
  27.6 21.5 %shard_map.150.refs_15_ = f32[8,128]{1,0:T(8,128)S(1)} custom-call(s32[36]{0:T(128)S(1)} %copy-done.18, s32[6,8,8]{2,1,0:T(8,128)S(1)} %bitcast.42, f32[4]{0:T(128)S(1)} %copy-done.16, bf16[8,8,256,128]{3,2,1,0:T(8,128)(2,1)S(1)} %copy-done.1, bf16[512,256]{1,0:T(8,128)(2,1)S(1)} %copy-done.14, f32[8,3,8,128]{3,2,1,0:T(8,128)S(1)} %bitcast.32, ...), custom_call_target="tpu_custom_call" | custom-call | flops 5400000000 | bytes 3600000 | tf_op jit(solution)/shard_map/pallas_call | solution.py:376
  49.2 18.7 %shard_map.151 = (f32[3,8,128]{2,1,0:T(8,128)S(1)}, f32[3,8,128]{2,1,0:T(8,128)S(1)}, f32[3,8,128]{2,1,0:T(8,128)S(1)}) custom-call(s32[28]{0:T(128)S(1)} %copy-done.17, s32[6,8,8]{2,1,0:T(8,128)S(1)} %bitcast.43, f32[4]{0:T(128)S(1)} %copy-done.16, bf16[8,8,256,128]{3,2,1,0:T(8,128)(2,1)S(1)} %copy-done.1, bf16[512,256]{1,0:T(8,128)(2,1)S(1)} %copy-done.14, ...), custom_call_target="tpu_custom_call" | custom-call | flops 4200000000 | bytes 2800000 | tf_op jit(solution)/shard_map/pallas_call | solution.py:376
  68.0 1.2 %collective-permute-done.6 = f32[3,8,128]{2,1,0:T(8,128)S(1)} collective-permute-done((f32[3,8,128]{2,1,0:T(8,128)S(1)}, f32[3,8,128]{2,1,0:T(8,128)S(1)}, u32[]{:S(2)}, u32[]{:S(2)}) %collective-permute-start.6) | collective-permute-done | bytes 12320 | tf_op jit(solution)/shard_map/ppermute | solution.py:501
  69.2 1.5 %collective-permute-start.7 = (f32[2,3,8,128]{3,2,1,0:T(8,128)S(1)}, f32[2,3,8,128]{3,2,1,0:T(8,128)S(1)}, u32[]{:S(2)}, u32[]{:S(2)}) collective-permute-start(f32[2,3,8,128]{3,2,1,0:T(8,128)S(1)} %pad_maximum_fusion.2), channel_id=1, source_target_pairs={{1,2},{2,1},{3,4},{4,3},{5,6},{6,5},{7,0},{0,7},{9,10},{10,9},{11,... | collective-permute-start | bytes 73736 | tf_op jit(solution)/shard_map/ppermute | solution.py:501
  70.7 2.7 %collective-permute-done.7 = f32[2,3,8,128]{3,2,1,0:T(8,128)S(1)} collective-permute-done((f32[2,3,8,128]{3,2,1,0:T(8,128)S(1)}, f32[2,3,8,128]{3,2,1,0:T(8,128)S(1)}, u32[]{:S(2)}, u32[]{:S(2)}) %collective-permute-start.7) | collective-permute-done | bytes 24608 | tf_op jit(solution)/shard_map/ppermute | solution.py:501
  73.4 1.2 %collective-permute-done.8 = f32[3,8,128]{2,1,0:T(8,128)S(1)} collective-permute-done((f32[3,8,128]{2,1,0:T(8,128)S(1)}, f32[3,8,128]{2,1,0:T(8,128)S(1)}, u32[]{:S(2)}, u32[]{:S(2)}) %collective-permute-start.8) | collective-permute-done | bytes 12320 | tf_op jit(solution)/shard_map/ppermute | solution.py:501
  74.5 0.7 collective-permute-start.9
  75.2 3.3 %collective-permute-done.9.refs_1_ = f32[3,3,8,128]{3,2,1,0:T(8,128)S(1)} collective-permute-done((f32[3,3,8,128]{3,2,1,0:T(8,128)S(1)}, f32[3,3,8,128]{3,2,1,0:T(8,128)S(1)}, u32[]{:S(2)}, u32[]{:S(2)}) %collective-permute-start.9) | collective-permute-done | bytes 36896 | tf_op jit(solution)/shard_map/ppermute | solution.py:501
  78.5 1.4 %collective-permute-start.10 = (f32[3,3,8,128]{3,2,1,0:T(8,128)S(1)}, f32[3,3,8,128]{3,2,1,0:T(8,128)S(1)}, u32[]{:S(2)}, u32[]{:S(2)}) collective-permute-start(f32[3,3,8,128]{3,2,1,0:T(8,128)S(1)} %pad_maximum_fusion.1), channel_id=1, source_target_pairs={{8,16},{16,8},{24,0},{0,24},{9,17},{17,9},{25,1},{1,25},{10,18},{1... | collective-permute-start | bytes 110600 | tf_op jit(solution)/shard_map/ppermute | solution.py:501
  79.9 4.4 %collective-permute-done.10.refs_2_ = f32[3,3,8,128]{3,2,1,0:T(8,128)S(1)} collective-permute-done((f32[3,3,8,128]{3,2,1,0:T(8,128)S(1)}, f32[3,3,8,128]{3,2,1,0:T(8,128)S(1)}, u32[]{:S(2)}, u32[]{:S(2)}) %collective-permute-start.10) | collective-permute-done | bytes 36896 | tf_op jit(solution)/shard_map/ppermute | solution.py:501
  84.4 2.5 %shard_map.152 = (f32[8,3,8,128]{3,2,1,0:T(8,128)}, f32[1,13,1,128]{3,2,1,0:T(1,128)}) custom-call(f32[3,3,8,128]{3,2,1,0:T(8,128)S(1)} %pad_maximum_fusion.refs_0_, f32[3,3,8,128]{3,2,1,0:T(8,128)S(1)} %collective-permute-done.9.refs_1_, f32[3,3,8,128]{3,2,1,0:T(8,128)S(1)} %collective-permute-done.10.refs_2_, f32[1,7,1,128]{3,2,1,0:T(1,128)S(1)} %bitcast.37, ...), custom_call_target="tpu_custom_call" | custom-call | tf_op jit(solution)/shard_map/pallas_call | solution.py:486
  (51 shorter events, 2.1 us)
Async XLA Ops:
  0.6 23.8 %copy-start.18 = (s32[36]{0:T(128)S(1)}, s32[36]{0:T(128)}, u32[]{:S(2)}) copy-start(s32[36]{0:T(128)} %constant.15.clone.refs_0_) | copy-start | bytes 436
  0.6 23.8 %copy-start.16 = (f32[4]{0:T(128)S(1)}, f32[4]{0:T(128)}, u32[]{:S(2)}) copy-start(f32[4]{0:T(128)} %refs_2_.3) | copy-start | bytes 52
  0.7 2.2 %copy-start = (bf16[8,8,256,128]{3,2,1,0:T(8,128)(2,1)S(1)}, bf16[8,8,256,128]{3,2,1,0:T(8,128)(2,1)}, u32[]{:S(2)}) copy-start(bf16[8,8,256,128]{3,2,1,0:T(8,128)(2,1)} %refs_3_.3) | copy-start | bytes 12582916
  6.5 17.9 %copy-start.4 = (f32[8,8,3,128]{3,1,2,0:T(8,128)S(1)}, f32[8,8,3,128]{3,1,2,0:T(8,128)}, u32[]{:S(2)}) copy-start(f32[8,8,3,128]{3,1,2,0:T(8,128)} %param.16) | copy-start | bytes 294916
  6.5 17.9 %copy-start.6 = (s32[8,8,128]{2,1,0:T(8,128)S(1)}, s32[8,8,128]{2,1,0:T(8,128)}, u32[]{:S(2)}) copy-start(s32[8,8,128]{2,1,0:T(8,128)} %refs_12_.1) | copy-start | bytes 98308
  6.6 17.9 %copy-start.7 = (s32[8,8,128]{2,1,0:T(8,128)S(1)}, s32[8,8,128]{2,1,0:T(8,128)}, u32[]{:S(2)}) copy-start(s32[8,8,128]{2,1,0:T(8,128)} %refs_13_.1) | copy-start | bytes 98308
  6.6 17.9 %copy-start.15 = (s32[8,8,6]{1,0,2:T(8,128)S(1)}, s32[8,8,6]{1,0,2:T(8,128)}, u32[]{:S(2)}) copy-start(s32[8,8,6]{1,0,2:T(8,128)} %param.17) | copy-start | bytes 4612
  8.8 8.1 %collective-permute-start = (bf16[1200,128]{1,0:T(8,128)(2,1)S(1)}, bf16[1200,128]{1,0:T(8,128)(2,1)S(1)}, u32[]{:S(2)}, u32[]{:S(2)}) collective-permute-start(bf16[1200,128]{1,0:T(8,128)(2,1)S(1)} %get-tuple-element.13), channel_id=1, source_target_pairs={{0,1},{1,0},{2,3},{3,2},{4,5},{5,4},{6,7},{7,6},{8,9},{9,8},{10,11... | collective-permute-start | bytes 921608 | tf_op jit(solution)/shard_map/ppermute | solution.py:501
  9.2 10.8 %collective-permute-start.1 = (bf16[1200,128]{1,0:T(8,128)(2,1)}, bf16[1200,128]{1,0:T(8,128)(2,1)S(1)}, u32[]{:S(2)}, u32[]{:S(2)}) collective-permute-start(bf16[1200,128]{1,0:T(8,128)(2,1)} %get-tuple-element.14), channel_id=1, source_target_pairs={{1,2},{2,1},{3,4},{4,3},{5,6},{6,5},{7,0},{0,7},{9,10},{10,9},{11,... | collective-permute-start | bytes 921608 | tf_op jit(solution)/shard_map/ppermute | solution.py:501
  12.8 36.3 %collective-permute-start.2 = (bf16[8,144,128]{2,1,0:T(8,128)(2,1)}, bf16[8,144,128]{2,1,0:T(8,128)(2,1)}, u32[]{:S(2)}, u32[]{:S(2)}) collective-permute-start(bf16[8,144,128]{2,1,0:T(8,128)(2,1)} %get-tuple-element.15), channel_id=1, source_target_pairs={{0,8},{8,0},{16,24},{24,16},{1,9},{9,1},{17,25},{25,17},{2,10},{10... | collective-permute-start | bytes 884744 | tf_op jit(solution)/shard_map/ppermute | solution.py:501
  14.4 34.8 %collective-permute-start.3 = (bf16[8,144,128]{2,1,0:T(8,128)(2,1)}, bf16[8,144,128]{2,1,0:T(8,128)(2,1)}, u32[]{:S(2)}, u32[]{:S(2)}) collective-permute-start(bf16[8,144,128]{2,1,0:T(8,128)(2,1)} %get-tuple-element.16), channel_id=1, source_target_pairs={{8,16},{16,8},{24,0},{0,24},{9,17},{17,9},{25,1},{1,25},{10,18},{1... | collective-permute-start | bytes 884744 | tf_op jit(solution)/shard_map/ppermute | solution.py:501
  20.1 29.1 %collective-permute-start.4 = (bf16[432,128]{1,0:T(8,128)(2,1)S(1)}, bf16[432,128]{1,0:T(8,128)(2,1)S(1)}, u32[]{:S(2)}, u32[]{:S(2)}) collective-permute-start(bf16[432,128]{1,0:T(8,128)(2,1)S(1)} %get-tuple-element.25), channel_id=1, source_target_pairs={{0,8},{8,0},{16,24},{24,16},{1,9},{9,1},{17,25},{25,17},{2,10},{10... | collective-permute-start | bytes 331784 | tf_op jit(solution)/shard_map/ppermute | solution.py:501
  21.9 27.2 %collective-permute-start.5 = (bf16[432,128]{1,0:T(8,128)(2,1)S(1)}, bf16[432,128]{1,0:T(8,128)(2,1)S(1)}, u32[]{:S(2)}, u32[]{:S(2)}) collective-permute-start(bf16[432,128]{1,0:T(8,128)(2,1)S(1)} %get-tuple-element.24), channel_id=1, source_target_pairs={{8,16},{16,8},{24,0},{0,24},{9,17},{17,9},{25,1},{1,25},{10,18},{1... | collective-permute-start | bytes 331784 | tf_op jit(solution)/shard_map/ppermute | solution.py:501
  24.4 2.2 %copy-start.1 = (bf16[8,8,256,128]{3,2,1,0:T(8,128)(2,1)S(1)}, bf16[8,8,256,128]{3,2,1,0:T(8,128)(2,1)}, u32[]{:S(2)}) copy-start(bf16[8,8,256,128]{3,2,1,0:T(8,128)(2,1)} %refs_3_.3) | copy-start | bytes 12582916
  27.6 21.6 %copy-start.17 = (s32[28]{0:T(128)S(1)}, s32[28]{0:T(128)}, u32[]{:S(2)}) copy-start(s32[28]{0:T(128)} %constant.16.clone.refs_0_) | copy-start | bytes 340
  49.1 35.2 %copy-start.3 = (bf16[8,8,3,128]{3,1,2,0:T(8,128)(2,1)S(1)}, bf16[8,8,3,128]{3,1,2,0:T(8,128)(2,1)}, u32[]{:S(2)}) copy-start(bf16[8,8,3,128]{3,1,2,0:T(8,128)(2,1)} %param.14) | copy-start | bytes 147460
  49.1 35.2 %copy-start.9 = (f32[1,1,7,128]{3,1,2,0:T(1,128)S(1)}, f32[1,1,7,128]{3,1,2,0:T(1,128)}, u32[]{:S(2)}) copy-start(f32[1,1,7,128]{3,1,2,0:T(1,128)} %param.20) | copy-start | bytes 10756
  49.1 35.2 %copy-start.11 = (f32[1,1,6,128]{3,1,2,0:T(1,128)S(1)}, f32[1,1,6,128]{3,1,2,0:T(1,128)}, u32[]{:S(2)}) copy-start(f32[1,1,6,128]{3,1,2,0:T(1,128)} %param.21) | copy-start | bytes 9220
  49.1 35.2 %copy-start.13 = (f32[1,1,4,128]{3,2,1,0:T(4,128)S(1)}, f32[1,1,4,128]{3,2,1,0:T(4,128)}, u32[]{:S(2)}) copy-start(f32[1,1,4,128]{3,2,1,0:T(4,128)} %refs_5_.1) | copy-start | bytes 6148
  68.0 1.2 %collective-permute-start.6 = (f32[3,8,128]{2,1,0:T(8,128)S(1)}, f32[3,8,128]{2,1,0:T(8,128)S(1)}, u32[]{:S(2)}, u32[]{:S(2)}) collective-permute-start(f32[3,8,128]{2,1,0:T(8,128)S(1)} %get-tuple-element.18), channel_id=1, source_target_pairs={{0,1},{1,0},{2,3},{3,2},{4,5},{5,4},{6,7},{7,6},{8,9},{9,8},{10,11... | collective-permute-start | bytes 36872 | tf_op jit(solution)/shard_map/ppermute | solution.py:501
  69.2 4.2 %collective-permute-start.7 = (f32[2,3,8,128]{3,2,1,0:T(8,128)S(1)}, f32[2,3,8,128]{3,2,1,0:T(8,128)S(1)}, u32[]{:S(2)}, u32[]{:S(2)}) collective-permute-start(f32[2,3,8,128]{3,2,1,0:T(8,128)S(1)} %pad_maximum_fusion.2), channel_id=1, source_target_pairs={{1,2},{2,1},{3,4},{4,3},{5,6},{6,5},{7,0},{0,7},{9,10},{10,9},{11,... | collective-permute-start | bytes 73736 | tf_op jit(solution)/shard_map/ppermute | solution.py:501
  73.4 1.2 %collective-permute-start.8 = (f32[3,8,128]{2,1,0:T(8,128)S(1)}, f32[3,8,128]{2,1,0:T(8,128)S(1)}, u32[]{:S(2)}, u32[]{:S(2)}) collective-permute-start(f32[3,8,128]{2,1,0:T(8,128)S(1)} %get-tuple-element.37), channel_id=1, source_target_pairs={{0,1},{1,0},{2,3},{3,2},{4,5},{5,4},{6,7},{7,6},{8,9},{9,8},{10,11... | collective-permute-start | bytes 36872 | tf_op jit(solution)/shard_map/ppermute | solution.py:501
  74.5 4.0 %collective-permute-start.9 = (f32[3,3,8,128]{3,2,1,0:T(8,128)S(1)}, f32[3,3,8,128]{3,2,1,0:T(8,128)S(1)}, u32[]{:S(2)}, u32[]{:S(2)}) collective-permute-start(f32[3,3,8,128]{3,2,1,0:T(8,128)S(1)} %pad_maximum_fusion.refs_0_), channel_id=1, source_target_pairs={{0,8},{8,0},{16,24},{24,16},{1,9},{9,1},{17,25},{25,17},{2,10},{10... | collective-permute-start | bytes 110600 | tf_op jit(solution)/shard_map/ppermute | solution.py:501
  78.5 5.8 %collective-permute-start.10 = (f32[3,3,8,128]{3,2,1,0:T(8,128)S(1)}, f32[3,3,8,128]{3,2,1,0:T(8,128)S(1)}, u32[]{:S(2)}, u32[]{:S(2)}) collective-permute-start(f32[3,3,8,128]{3,2,1,0:T(8,128)S(1)} %pad_maximum_fusion.1), channel_id=1, source_target_pairs={{8,16},{16,8},{24,0},{0,24},{9,17},{17,9},{25,1},{1,25},{10,18},{1... | collective-permute-start | bytes 110600 | tf_op jit(solution)/shard_map/ppermute | solution.py:501
  (6 other events, 4.6 us)

commit v4 on v3

--- a/solution.py
+++ b/solution.py
@@ -13,7 +13,8 @@
 VMEM = pl.BlockSpec(memory_space=pltpu.VMEM)
 SMEM = pl.BlockSpec(memory_space=pltpu.SMEM)
 HBM = pl.BlockSpec(memory_space=pl.ANY)
-LIMIT = 24 * 2**20
+LIMIT = 56 * 2**20
+SMALL = 16 * 2**20
 DIRS = [(-1, -1), (-1, 0), (-1, 1), (0, -1), (0, 1), (1, -1), (1, 0), (1, 1)]
 EXTRA = 16
 BODY = 48
@@ -137,7 +138,8 @@
     where_to, code_of = take(2)
     feat, shift_of, norm_of, terms, fsem = take(5)
     sets = [take(7), take(7)]
-    vp, vsem, total, parts = take(4) if halo else (own, None, sums[0], None)
+    vp, vsem = take(2)
+    total, parts = take(2) if halo else (sums[0], None)
     wide = ty + 2
     here = lambda i, j: (i + 1) * wide + j + 1 if halo else i * ty + j
     side = chans * width_h
@@ -166,9 +168,11 @@
             pairs_of.append((src, line(x)))
             pairs_of.append((end.at[pl.ds(0, rows)], vp.at[x * wide + y_in]))
             pairs_of.append((end.at[pl.ds(rows, rows)], vp.at[x * wide + y_out]))
-        copies = [pltpu.make_async_copy(src, dst, vsem.at[q]) for q, (src, dst) in enumerate(pairs_of)]
-        for copy in copies:
-            copy.start()
+    else:
+        pairs_of = [(own, vp)]
+    copies = [pltpu.make_async_copy(src, dst, vsem.at[q]) for q, (src, dst) in enumerate(pairs_of)]
+    for copy in copies:
+        copy.start()
     total[...] = around[6][...] if halo else jnp.zeros_like(total)
 
     def where_is(t):
@@ -273,8 +277,6 @@
         return got[0:8] + got[8:16]
 
     lax.fori_loop(0, n, prepare, 0)
-    for load in loads:
-        load.wait()
     last = n // 2 - 1
 
     def fill(s, into):
@@ -304,12 +306,14 @@
         gather(2 * before + 1, later[6])
         total[...] = total[...] + jnp.where(s == 0, 0.0, add_up(before))
 
+    loads[0].wait()
     make_u(0, sets[0][0])
     make_u(min(1, last), sets[1][0])
-    if halo:
-        for copy in copies:
-            copy.wait()
+    for copy in copies:
+        copy.wait()
     fill(0, sets[0])
+    for load in loads[1:]:
+        load.wait()
 
     def body(g, carry):
         half(2 * g, sets[0], sets[1])
@@ -367,16 +371,16 @@
         pltpu.VMEM((nb * beads, beads), BF16),
         pltpu.VMEM((nb * beads, beads), BF16),
     ]
+    spread = (tx + 2) * (ty + 2) if halo else tx * ty
+    scratch += [pltpu.VMEM((spread, rows, beads), BF16), pltpu.SemaphoreType.DMA((3 * tx + 6 if halo else 1,))]
     if halo:
-        scratch += [pltpu.VMEM(((tx + 2) * (ty + 2), rows, beads), BF16),
-                    pltpu.SemaphoreType.DMA((3 * tx + 6,)), pltpu.VMEM((8, slots), F32),
-                    pltpu.VMEM((3, 3, 8, slots), F32)]
+        scratch += [pltpu.VMEM((8, slots), F32), pltpu.VMEM((3, 3, 8, slots), F32)]
     ids = jnp.asarray([i * ty + j for i, j in tiles], jnp.int32)
     shape = (tx, ty, beads, width_h, chans, nb, slots)
     return pl.pallas_call(
         lambda *refs: pairs_kernel(strips, halo, shape, *refs),
         out_shape=[out] * (3 if halo else 1),
-        in_specs=[SMEM, SMEM, SMEM, HBM, VMEM, VMEM, VMEM, VMEM, HBM if halo else VMEM]
+        in_specs=[SMEM, SMEM, SMEM, HBM, VMEM, VMEM, VMEM, VMEM, HBM]
         + ([HBM] * 6 + [VMEM] if halo else []),
         out_specs=[VMEM] * (3 if halo else 1),
         scratch_shapes=scratch,
@@ -489,7 +493,7 @@
         in_specs=[VMEM] * (11 + len(sums)),
         out_specs=[VMEM] * 2,
         scratch_shapes=[pltpu.VMEM((3, 3, 32, slots), BF16)],
-        compiler_params=pltpu.CompilerParams(vmem_limit_bytes=LIMIT),
+        compiler_params=pltpu.CompilerParams(vmem_limit_bytes=SMALL),
     )(*sums, pose, motion, inverse, *cols, *ends, pos, lever, slot, owner)
 
 

time: 87.2 us -> 87.8 us (level)
  local copies, waits for them, and re-layouts: 9.1 us -> 4.04 us
  Pallas kernels: 44.9 us -> 47.9 us
  other arithmetic: 0.08 us -> 2.19 us
    unnamed x40 -> x36, local copies, waits for them, and re-layouts: 9.09 us -> 4.03 us
    pallas_call x1, Pallas kernels: 2.24 us -> 4.41 us  [project(): pl.pallas_call(project_kernel, grid=(tx // STEP,), out_shape=[sds(tx, ty,...]
  transfers between devices with their start and end apart: 11 -> 11, of which waited for: 6 -> 6; matrix products, arithmetic and copies ran while one was open for 0% -> 1% of each run, Pallas kernels for 25% -> 25%
where the time goes in v4:
time: 87.8 us; the launch traced here: 87.3 us
  Pallas kernels  47.9 us (55%)
  starting transfers between devices  16.2 us (18%)
  waiting for transfers between devices  16.1 us (18%)
  local copies, waits for them, and re-layouts  4.04 us (5%)
  other arithmetic  2.19 us (2%)
  between operations  0.88 us (1%)
    pallas_call x2, Pallas kernels, pairs(): pl.pallas_call(lambda *refs: pairs_kernel(strips, halo, shape, *refs), ou...  41 us
    ppermute x11, starting transfers between devices, swap(): return lax.ppermute(value, axis, route)  16.2 us
    ppermute x11, waiting for transfers between devices, swap(): return lax.ppermute(value, axis, route)  16.1 us
    pallas_call x1, Pallas kernels, project(): pl.pallas_call(project_kernel, grid=(tx // STEP,), out_shape=[sds(tx, ty,...  4.41 us
    unnamed x36, local copies, waits for them, and re-layouts  4.03 us
    pallas_call x1, Pallas kernels, finish(): pl.pallas_call(lambda *refs: finish_kernel(len(sums), *refs), out_shape=[...  2.45 us
  transfers between devices with their start and end apart: 11, of which 6 were waited for; matrix products, arithmetic and copies ran while one was open for 1% of the time, Pallas kernels for 25%

profile of v4, /device:TPU:0, one launch (start us, length us, event | category | flops | bytes accessed | tf_op | source)
XLA Modules:
  0.0 87.3 jit_solution(8181674121207078871)
XLA Ops:
  0.6 4.4 %shard_map.149 = (bf16[8,8,144,128]{3,2,1,0:T(8,128)(2,1)}, bf16[1200,128]{1,0:T(8,128)(2,1)}, bf16[1200,128]{1,0:T(8,128)(2,1)}, bf16[8,144,128]{2,1,0:T(8,128)(2,1)}, bf16[8,144,128]{2,1,0:T(8,128)(2,1)}) custom-call(bf16[8,8,256,128]{3,2,1,0:T(8,128)(2,1)} %refs_3_.3, bf16[8,3,8,128]{3,2,1,0:T(8,128)(2,1)} %bitcast.30, bf16[128,256]{1,0:T(8,128)(2,1)} %weight_v.1, ...), custom_call_target="tpu_custom_call" | custom-call | tf_op jit(solution)/shard_map/pallas_call | solution.py:112
  5.6 3.6 %collective-permute-start.1 = (bf16[1200,128]{1,0:T(8,128)(2,1)}, bf16[1200,128]{1,0:T(8,128)(2,1)S(1)}, u32[]{:S(2)}, u32[]{:S(2)}) collective-permute-start(bf16[1200,128]{1,0:T(8,128)(2,1)} %get-tuple-element.14), channel_id=1, source_target_pairs={{1,2},{2,1},{3,4},{4,3},{5,6},{6,5},{7,0},{0,7},{9,10},{10,9},{11,... | collective-permute-start | bytes 921608 | tf_op jit(solution)/shard_map/ppermute | solution.py:505
  9.1 1.6 %collective-permute-start.2 = (bf16[8,144,128]{2,1,0:T(8,128)(2,1)}, bf16[8,144,128]{2,1,0:T(8,128)(2,1)S(1)}, u32[]{:S(2)}, u32[]{:S(2)}) collective-permute-start(bf16[8,144,128]{2,1,0:T(8,128)(2,1)} %get-tuple-element.15), channel_id=1, source_target_pairs={{0,8},{8,0},{16,24},{24,16},{1,9},{9,1},{17,25},{25,17},{2,10},{10... | collective-permute-start | bytes 884744 | tf_op jit(solution)/shard_map/ppermute | solution.py:505
  10.7 2.5 %collective-permute-start.3 = (bf16[8,144,128]{2,1,0:T(8,128)(2,1)}, bf16[8,144,128]{2,1,0:T(8,128)(2,1)S(1)}, u32[]{:S(2)}, u32[]{:S(2)}) collective-permute-start(bf16[8,144,128]{2,1,0:T(8,128)(2,1)} %get-tuple-element.16), channel_id=1, source_target_pairs={{8,16},{16,8},{24,0},{0,24},{9,17},{17,9},{25,1},{1,25},{10,18},{1... | collective-permute-start | bytes 884744 | tf_op jit(solution)/shard_map/ppermute | solution.py:505
  13.2 3.2 %collective-permute-done.1.refs_10_.refs_7_ = bf16[1200,128]{1,0:T(8,128)(2,1)S(1)} collective-permute-done((bf16[1200,128]{1,0:T(8,128)(2,1)}, bf16[1200,128]{1,0:T(8,128)(2,1)S(1)}, u32[]{:S(2)}, u32[]{:S(2)}) %collective-permute-start.1) | collective-permute-done | bytes 307232 | tf_op jit(solution)/shard_map/ppermute | solution.py:505
  16.4 0.8 constant_dynamic-update-slice_fusion.5
  17.2 2.0 %collective-permute-start.4 = (bf16[432,128]{1,0:T(8,128)(2,1)S(1)}, bf16[432,128]{1,0:T(8,128)(2,1)S(1)}, u32[]{:S(2)}, u32[]{:S(2)}) collective-permute-start(bf16[432,128]{1,0:T(8,128)(2,1)S(1)} %get-tuple-element.25), channel_id=1, source_target_pairs={{0,8},{8,0},{16,24},{24,16},{1,9},{9,1},{17,25},{25,17},{2,10},{10... | collective-permute-start | bytes 331784 | tf_op jit(solution)/shard_map/ppermute | solution.py:505
  19.1 2.5 %collective-permute-start.5 = (bf16[432,128]{1,0:T(8,128)(2,1)S(1)}, bf16[432,128]{1,0:T(8,128)(2,1)S(1)}, u32[]{:S(2)}, u32[]{:S(2)}) collective-permute-start(bf16[432,128]{1,0:T(8,128)(2,1)S(1)} %get-tuple-element.24), channel_id=1, source_target_pairs={{8,16},{16,8},{24,0},{0,24},{9,17},{17,9},{25,1},{1,25},{10,18},{1... | collective-permute-start | bytes 331784 | tf_op jit(solution)/shard_map/ppermute | solution.py:505
  21.6 22.1 %shard_map.150.refs_15_ = f32[8,128]{1,0:T(8,128)} custom-call(s32[36]{0:T(128)} %constant.15.clone.refs_0_, s32[6,8,8]{2,1,0:T(8,128)} %bitcast.46, f32[4]{0:T(128)} %refs_2_.3, bf16[8,8,256,128]{3,2,1,0:T(8,128)(2,1)} %refs_3_.3, bf16[512,256]{1,0:T(8,128)(2,1)} %refs_4_.3, f32[8,3,8,128]{3,2,1,0:T(8,128)} %bitcast.32, s32[8,8,128]{2,1,0:T(8,128)} %refs_12_.1, ...), custom_call_target="tpu_custom_call" | custom-call | flops 5400000000 | bytes 3600000 | tf_op jit(solution)/shard_map/pallas_call | solution.py:380
  45.3 19.0 %shard_map.151 = (f32[3,8,128]{2,1,0:T(8,128)}, f32[3,8,128]{2,1,0:T(8,128)}, f32[3,8,128]{2,1,0:T(8,128)}) custom-call(s32[28]{0:T(128)} %constant.16.clone.refs_0_, s32[6,8,8]{2,1,0:T(8,128)} %bitcast.47, f32[4]{0:T(128)} %refs_2_.3, bf16[8,8,256,128]{3,2,1,0:T(8,128)(2,1)} %refs_3_.3, bf16[512,256]{1,0:T(8,128)(2,1)} %refs_4_.3, ...), custom_call_target="tpu_custom_call" | custom-call | flops 4200000000 | bytes 2800000 | tf_op jit(solution)/shard_map/pallas_call | solution.py:380
  64.3 1.4 %collective-permute-done.6 = f32[3,8,128]{2,1,0:T(8,128)S(1)} collective-permute-done((f32[3,8,128]{2,1,0:T(8,128)}, f32[3,8,128]{2,1,0:T(8,128)S(1)}, u32[]{:S(2)}, u32[]{:S(2)}) %collective-permute-start.6) | collective-permute-done | bytes 12320 | tf_op jit(solution)/shard_map/ppermute | solution.py:505
  65.7 0.7 add.13
  66.4 0.7 pad_maximum_fusion.2
  67.1 1.4 %collective-permute-start.7 = (f32[2,3,8,128]{3,2,1,0:T(8,128)S(1)}, f32[2,3,8,128]{3,2,1,0:T(8,128)S(1)}, u32[]{:S(2)}, u32[]{:S(2)}) collective-permute-start(f32[2,3,8,128]{3,2,1,0:T(8,128)S(1)} %pad_maximum_fusion.2), channel_id=1, source_target_pairs={{1,2},{2,1},{3,4},{4,3},{5,6},{6,5},{7,0},{0,7},{9,10},{10,9},{11,... | collective-permute-start | bytes 73736 | tf_op jit(solution)/shard_map/ppermute | solution.py:505
  68.6 2.7 %collective-permute-done.7 = f32[2,3,8,128]{3,2,1,0:T(8,128)S(1)} collective-permute-done((f32[2,3,8,128]{3,2,1,0:T(8,128)S(1)}, f32[2,3,8,128]{3,2,1,0:T(8,128)S(1)}, u32[]{:S(2)}, u32[]{:S(2)}) %collective-permute-start.7) | collective-permute-done | bytes 24608 | tf_op jit(solution)/shard_map/ppermute | solution.py:505
  71.3 0.7 fusion.2
  72.0 1.2 %collective-permute-done.8 = f32[3,8,128]{2,1,0:T(8,128)S(1)} collective-permute-done((f32[3,8,128]{2,1,0:T(8,128)S(1)}, f32[3,8,128]{2,1,0:T(8,128)S(1)}, u32[]{:S(2)}, u32[]{:S(2)}) %collective-permute-start.8) | collective-permute-done | bytes 12320 | tf_op jit(solution)/shard_map/ppermute | solution.py:505
  73.2 0.7 collective-permute-start.9
  73.9 3.3 %collective-permute-done.9.refs_1_ = f32[3,3,8,128]{3,2,1,0:T(8,128)S(1)} collective-permute-done((f32[3,3,8,128]{3,2,1,0:T(8,128)S(1)}, f32[3,3,8,128]{3,2,1,0:T(8,128)S(1)}, u32[]{:S(2)}, u32[]{:S(2)}) %collective-permute-start.9) | collective-permute-done | bytes 36896 | tf_op jit(solution)/shard_map/ppermute | solution.py:505
  77.2 1.4 %collective-permute-start.10 = (f32[3,3,8,128]{3,2,1,0:T(8,128)S(1)}, f32[3,3,8,128]{3,2,1,0:T(8,128)S(1)}, u32[]{:S(2)}, u32[]{:S(2)}) collective-permute-start(f32[3,3,8,128]{3,2,1,0:T(8,128)S(1)} %pad_maximum_fusion.1), channel_id=1, source_target_pairs={{8,16},{16,8},{24,0},{0,24},{9,17},{17,9},{25,1},{1,25},{10,18},{1... | collective-permute-start | bytes 110600 | tf_op jit(solution)/shard_map/ppermute | solution.py:505
  78.6 4.4 %collective-permute-done.10.refs_2_ = f32[3,3,8,128]{3,2,1,0:T(8,128)S(1)} collective-permute-done((f32[3,3,8,128]{3,2,1,0:T(8,128)S(1)}, f32[3,3,8,128]{3,2,1,0:T(8,128)S(1)}, u32[]{:S(2)}, u32[]{:S(2)}) %collective-permute-start.10) | collective-permute-done | bytes 36896 | tf_op jit(solution)/shard_map/ppermute | solution.py:505
  83.1 0.9 %copy-done.6 = bf16[432,128]{1,0:T(8,128)(2,1)S(1)} copy-done((bf16[432,128]{1,0:T(8,128)(2,1)S(1)}, bf16[432,128]{1,0:T(8,128)(2,1)}, u32[]{:S(2)}) %copy-start.6) | copy-done | bytes 110616
  83.9 0.9 %copy-done.8 = bf16[432,128]{1,0:T(8,128)(2,1)S(1)} copy-done((bf16[432,128]{1,0:T(8,128)(2,1)S(1)}, bf16[432,128]{1,0:T(8,128)(2,1)}, u32[]{:S(2)}) %copy-start.8) | copy-done | bytes 110616
  84.8 2.4 %shard_map.152 = (f32[8,3,8,128]{3,2,1,0:T(8,128)}, f32[1,13,1,128]{3,2,1,0:T(1,128)}) custom-call(f32[3,3,8,128]{3,2,1,0:T(8,128)S(1)} %pad_maximum_fusion.refs_0_, f32[3,3,8,128]{3,2,1,0:T(8,128)S(1)} %collective-permute-done.9.refs_1_, f32[3,3,8,128]{3,2,1,0:T(8,128)S(1)} %collective-permute-done.10.refs_2_, f32[1,7,1,128]{3,2,1,0:T(1,128)S(1)} %bitcast.36, ...), custom_call_target="tpu_custom_call" | custom-call | tf_op jit(solution)/shard_map/pallas_call | solution.py:490
  (47 shorter events, 2.2 us)
Async XLA Ops:
  5.0 8.1 %collective-permute-start = (bf16[1200,128]{1,0:T(8,128)(2,1)}, bf16[1200,128]{1,0:T(8,128)(2,1)S(1)}, u32[]{:S(2)}, u32[]{:S(2)}) collective-permute-start(bf16[1200,128]{1,0:T(8,128)(2,1)} %get-tuple-element.13), channel_id=1, source_target_pairs={{0,1},{1,0},{2,3},{3,2},{4,5},{5,4},{6,7},{7,6},{8,9},{9,8},{10,11... | collective-permute-start | bytes 921608 | tf_op jit(solution)/shard_map/ppermute | solution.py:505
  5.6 10.8 %collective-permute-start.1 = (bf16[1200,128]{1,0:T(8,128)(2,1)}, bf16[1200,128]{1,0:T(8,128)(2,1)S(1)}, u32[]{:S(2)}, u32[]{:S(2)}) collective-permute-start(bf16[1200,128]{1,0:T(8,128)(2,1)} %get-tuple-element.14), channel_id=1, source_target_pairs={{1,2},{2,1},{3,4},{4,3},{5,6},{6,5},{7,0},{0,7},{9,10},{10,9},{11,... | collective-permute-start | bytes 921608 | tf_op jit(solution)/shard_map/ppermute | solution.py:505
  9.1 34.7 %collective-permute-start.2 = (bf16[8,144,128]{2,1,0:T(8,128)(2,1)}, bf16[8,144,128]{2,1,0:T(8,128)(2,1)S(1)}, u32[]{:S(2)}, u32[]{:S(2)}) collective-permute-start(bf16[8,144,128]{2,1,0:T(8,128)(2,1)} %get-tuple-element.15), channel_id=1, source_target_pairs={{0,8},{8,0},{16,24},{24,16},{1,9},{9,1},{17,25},{25,17},{2,10},{10... | collective-permute-start | bytes 884744 | tf_op jit(solution)/shard_map/ppermute | solution.py:505
  10.7 33.1 %collective-permute-start.3 = (bf16[8,144,128]{2,1,0:T(8,128)(2,1)}, bf16[8,144,128]{2,1,0:T(8,128)(2,1)S(1)}, u32[]{:S(2)}, u32[]{:S(2)}) collective-permute-start(bf16[8,144,128]{2,1,0:T(8,128)(2,1)} %get-tuple-element.16), channel_id=1, source_target_pairs={{8,16},{16,8},{24,0},{0,24},{9,17},{17,9},{25,1},{1,25},{10,18},{1... | collective-permute-start | bytes 884744 | tf_op jit(solution)/shard_map/ppermute | solution.py:505
  13.2 30.5 %copy-start = (bf16[1200,128]{1,0:T(8,128)(2,1)}, bf16[1200,128]{1,0:T(8,128)(2,1)S(1)}, u32[]{:S(2)}) copy-start(bf16[1200,128]{1,0:T(8,128)(2,1)S(1)} %collective-permute-done.refs_9_.refs_6_) | copy-start | bytes 921604
  16.4 27.3 %copy-start.2 = (bf16[1200,128]{1,0:T(8,128)(2,1)}, bf16[1200,128]{1,0:T(8,128)(2,1)S(1)}, u32[]{:S(2)}) copy-start(bf16[1200,128]{1,0:T(8,128)(2,1)S(1)} %collective-permute-done.1.refs_10_.refs_7_) | copy-start | bytes 921604
  17.2 26.7 %collective-permute-start.4 = (bf16[432,128]{1,0:T(8,128)(2,1)S(1)}, bf16[432,128]{1,0:T(8,128)(2,1)S(1)}, u32[]{:S(2)}, u32[]{:S(2)}) collective-permute-start(bf16[432,128]{1,0:T(8,128)(2,1)S(1)} %get-tuple-element.25), channel_id=1, source_target_pairs={{0,8},{8,0},{16,24},{24,16},{1,9},{9,1},{17,25},{25,17},{2,10},{10... | collective-permute-start | bytes 331784 | tf_op jit(solution)/shard_map/ppermute | solution.py:505
  19.1 24.7 %collective-permute-start.5 = (bf16[432,128]{1,0:T(8,128)(2,1)S(1)}, bf16[432,128]{1,0:T(8,128)(2,1)S(1)}, u32[]{:S(2)}, u32[]{:S(2)}) collective-permute-start(bf16[432,128]{1,0:T(8,128)(2,1)S(1)} %get-tuple-element.24), channel_id=1, source_target_pairs={{8,16},{16,8},{24,0},{0,24},{9,17},{17,9},{25,1},{1,25},{10,18},{1... | collective-permute-start | bytes 331784 | tf_op jit(solution)/shard_map/ppermute | solution.py:505
  43.7 39.3 %copy-start.4 = (bf16[8,8,3,128]{3,1,2,0:T(8,128)(2,1)S(1)}, bf16[8,8,3,128]{3,1,2,0:T(8,128)(2,1)}, u32[]{:S(2)}) copy-start(bf16[8,8,3,128]{3,1,2,0:T(8,128)(2,1)} %param.14) | copy-start | bytes 147460
  43.7 39.3 %copy-start.9 = (f32[8,8,3,128]{3,1,2,0:T(8,128)S(1)}, f32[8,8,3,128]{3,1,2,0:T(8,128)}, u32[]{:S(2)}) copy-start(f32[8,8,3,128]{3,1,2,0:T(8,128)} %param.16) | copy-start | bytes 294916
  43.7 39.3 %copy-start.10 = (s32[8,8,128]{2,1,0:T(8,128)S(1)}, s32[8,8,128]{2,1,0:T(8,128)}, u32[]{:S(2)}) copy-start(s32[8,8,128]{2,1,0:T(8,128)} %refs_12_.1) | copy-start | bytes 98308
  43.7 39.3 %copy-start.11 = (s32[8,8,128]{2,1,0:T(8,128)S(1)}, s32[8,8,128]{2,1,0:T(8,128)}, u32[]{:S(2)}) copy-start(s32[8,8,128]{2,1,0:T(8,128)} %refs_13_.1) | copy-start | bytes 98308
  43.7 39.3 %copy-start.12 = (f32[1,1,7,128]{3,1,2,0:T(1,128)S(1)}, f32[1,1,7,128]{3,1,2,0:T(1,128)}, u32[]{:S(2)}) copy-start(f32[1,1,7,128]{3,1,2,0:T(1,128)} %param.20) | copy-start | bytes 10756
  43.8 39.3 %copy-start.13 = (f32[1,1,6,128]{3,1,2,0:T(1,128)S(1)}, f32[1,1,6,128]{3,1,2,0:T(1,128)}, u32[]{:S(2)}) copy-start(f32[1,1,6,128]{3,1,2,0:T(1,128)} %param.21) | copy-start | bytes 9220
  43.8 39.3 %copy-start.14 = (f32[1,1,4,128]{3,2,1,0:T(4,128)S(1)}, f32[1,1,4,128]{3,2,1,0:T(4,128)}, u32[]{:S(2)}) copy-start(f32[1,1,4,128]{3,2,1,0:T(4,128)} %refs_5_.1) | copy-start | bytes 6148
  43.8 39.2 %copy-start.1 = (bf16[1200,128]{1,0:T(8,128)(2,1)S(1)}, bf16[1200,128]{1,0:T(8,128)(2,1)}, u32[]{:S(2)}) copy-start(bf16[1200,128]{1,0:T(8,128)(2,1)} %copy-done) | copy-start | bytes 921604
  43.8 39.2 %copy-start.3 = (bf16[1200,128]{1,0:T(8,128)(2,1)S(1)}, bf16[1200,128]{1,0:T(8,128)(2,1)}, u32[]{:S(2)}) copy-start(bf16[1200,128]{1,0:T(8,128)(2,1)} %copy-done.2) | copy-start | bytes 921604
  64.3 1.5 %collective-permute-start.6 = (f32[3,8,128]{2,1,0:T(8,128)}, f32[3,8,128]{2,1,0:T(8,128)S(1)}, u32[]{:S(2)}, u32[]{:S(2)}) collective-permute-start(f32[3,8,128]{2,1,0:T(8,128)} %get-tuple-element.18), channel_id=1, source_target_pairs={{0,1},{1,0},{2,3},{3,2},{4,5},{5,4},{6,7},{7,6},{8,9},{9,8},{10,11... | collective-permute-start | bytes 36872 | tf_op jit(solution)/shard_map/ppermute | solution.py:505
  67.1 4.2 %collective-permute-start.7 = (f32[2,3,8,128]{3,2,1,0:T(8,128)S(1)}, f32[2,3,8,128]{3,2,1,0:T(8,128)S(1)}, u32[]{:S(2)}, u32[]{:S(2)}) collective-permute-start(f32[2,3,8,128]{3,2,1,0:T(8,128)S(1)} %pad_maximum_fusion.2), channel_id=1, source_target_pairs={{1,2},{2,1},{3,4},{4,3},{5,6},{6,5},{7,0},{0,7},{9,10},{10,9},{11,... | collective-permute-start | bytes 73736 | tf_op jit(solution)/shard_map/ppermute | solution.py:505
  72.0 1.2 %collective-permute-start.8 = (f32[3,8,128]{2,1,0:T(8,128)S(1)}, f32[3,8,128]{2,1,0:T(8,128)S(1)}, u32[]{:S(2)}, u32[]{:S(2)}) collective-permute-start(f32[3,8,128]{2,1,0:T(8,128)S(1)} %get-tuple-element.37), channel_id=1, source_target_pairs={{0,1},{1,0},{2,3},{3,2},{4,5},{5,4},{6,7},{7,6},{8,9},{9,8},{10,11... | collective-permute-start | bytes 36872 | tf_op jit(solution)/shard_map/ppermute | solution.py:505
  73.2 4.0 %collective-permute-start.9 = (f32[3,3,8,128]{3,2,1,0:T(8,128)S(1)}, f32[3,3,8,128]{3,2,1,0:T(8,128)S(1)}, u32[]{:S(2)}, u32[]{:S(2)}) collective-permute-start(f32[3,3,8,128]{3,2,1,0:T(8,128)S(1)} %pad_maximum_fusion.refs_0_), channel_id=1, source_target_pairs={{0,8},{8,0},{16,24},{24,16},{1,9},{9,1},{17,25},{25,17},{2,10},{10... | collective-permute-start | bytes 110600 | tf_op jit(solution)/shard_map/ppermute | solution.py:505
  77.2 5.8 %collective-permute-start.10 = (f32[3,3,8,128]{3,2,1,0:T(8,128)S(1)}, f32[3,3,8,128]{3,2,1,0:T(8,128)S(1)}, u32[]{:S(2)}, u32[]{:S(2)}) collective-permute-start(f32[3,3,8,128]{3,2,1,0:T(8,128)S(1)} %pad_maximum_fusion.1), channel_id=1, source_target_pairs={{8,16},{16,8},{24,0},{0,24},{9,17},{17,9},{25,1},{1,25},{10,18},{1... | collective-permute-start | bytes 110600 | tf_op jit(solution)/shard_map/ppermute | solution.py:505
  83.0 0.9 %copy-start.6 = (bf16[432,128]{1,0:T(8,128)(2,1)S(1)}, bf16[432,128]{1,0:T(8,128)(2,1)}, u32[]{:S(2)}) copy-start(bf16[432,128]{1,0:T(8,128)(2,1)} %copy-done.5) | copy-start | bytes 331780
  83.9 0.9 %copy-start.8 = (bf16[432,128]{1,0:T(8,128)(2,1)S(1)}, bf16[432,128]{1,0:T(8,128)(2,1)}, u32[]{:S(2)}) copy-start(bf16[432,128]{1,0:T(8,128)(2,1)} %copy-done.7) | copy-start | bytes 331780
  (4 other events, 2.9 us)

commit v5 on v4

--- a/solution.py
+++ b/solution.py
@@ -14,6 +14,7 @@
 SMEM = pl.BlockSpec(memory_space=pltpu.SMEM)
 HBM = pl.BlockSpec(memory_space=pl.ANY)
 LIMIT = 56 * 2**20
+MEDIUM = 24 * 2**20
 SMALL = 16 * 2**20
 DIRS = [(-1, -1), (-1, 0), (-1, 1), (0, -1), (0, 1), (1, -1), (1, 0), (1, 1)]
 EXTRA = 16
@@ -132,10 +133,10 @@
     tx, ty, beads, width_h, chans, nb, slots = shape
     refs = list(refs)
     take = lambda k: [refs.pop(0) for _ in range(k)]
-    ids, partner, rate, features, weight_u, lever, slot, owner, own = take(9)
+    ids, partner, codes, rate, features, weight_u, lever, slot, owner, own = take(10)
     around = take(7) if halo else []
     sums = take(3 if halo else 1)
-    where_to, code_of = take(2)
+    table, where_to, tsem = take(3)
     feat, shift_of, norm_of, terms, fsem = take(5)
     sets = [take(7), take(7)]
     vp, vsem = take(2)
@@ -178,14 +179,14 @@
     def where_is(t):
         return lax.div(ids[t], jnp.int32(ty)), lax.rem(ids[t], jnp.int32(ty))
 
-    def prepare(t, carry):
-        i, j = where_is(t)
-        for m in range(nb):
-            code = partner[m, i, j]
-            a = lax.shift_right_logical(code * 11, 5)
-            where_to[t * nb + m] = here(i + a - 1, j + code - 3 * a - 1)
-            code_of[t * nb + m] = code
-        return carry
+    both = codes.shape
+    code = codes[...]
+    a = lax.shift_right_logical(code * 11, 5)
+    pitch = wide if halo else ty
+    first = lax.broadcasted_iota(jnp.int32, both, 1) * pitch + lax.broadcasted_iota(jnp.int32, both, 2)
+    table[:, :, 0:ty] = first + (a - 1) * pitch + code - 3 * a - 1 + (wide + 1 if halo else 0)
+    tables = pltpu.make_async_copy(table, where_to, tsem)
+    tables.start()
 
     row8 = rows_iota(8, beads)
     row16 = rows_iota(EXTRA, beads)
@@ -203,12 +204,13 @@
                 ub[e, :, k * beads : (k + 1) * beads] = u[
                     k * width_h : (k + 1) * width_h, e * beads : (e + 1) * beads]
 
-    def moved_block(t, m):
-        return vp[where_to[t * nb + m], beads : beads + EXTRA, :] + shift_of[code_of[t * nb + m]]
+    def moved_block(i, j, m):
+        return vp[where_to[m, i, j], beads : beads + EXTRA, :] + shift_of[partner[m, i, j]]
 
     def products(t, ub, e, buf, g):
         cols = slice(2 * g * beads, 2 * (g + 1) * beads)
-        lhs = jnp.concatenate([vp[where_to[t * nb + m], 0:beads, :] for m in range(nb)], axis=0)
+        i, j = where_is(t)
+        lhs = jnp.concatenate([vp[where_to[m, i, j], 0:beads, :] for m in range(nb)], axis=0)
         buf[:, cols] = jnp.dot(lhs, ub[e, :, cols], preferred_element_type=F32)
 
     def scores(t, ub, e, buf, zbuf):
@@ -222,8 +224,8 @@
         mine = jnp.concatenate([jnp.concatenate([mine, none], axis=1), jnp.concatenate([none, mine], axis=1)], axis=0)
         feats = []
         for m in range(nb):
-            code = code_of[t * nb + m]
-            block = moved_block(t, m).astype(F32)
+            code = partner[m, i, j]
+            block = moved_block(i, j, m).astype(F32)
             up = block[0:8]
             qx, qy = (jnp.broadcast_to(up[c : c + 1], (8, beads)) for c in (0, 1))
             norm = jnp.broadcast_to(up[5:6] + up[6:7] + up[7:8], (8, beads)) + norm_of[code, 2]
@@ -251,7 +253,7 @@
 
     def gather(t, cbuf):
         i, j = where_is(t)
-        lhs = jnp.concatenate([moved_block(t, m) for m in range(nb)], axis=1)
+        lhs = jnp.concatenate([moved_block(i, j, m) for m in range(nb)], axis=1)
         out = jnp.dot(lhs, cbuf[...], preferred_element_type=F32) * (1.0 / width_h)
         mine = vp[here(i, j), beads : beads + EXTRA, :].astype(F32)
         w = out[8:9]
@@ -276,7 +278,6 @@
                               (((1,), (1,)), ((), ())), preferred_element_type=F32)
         return got[0:8] + got[8:16]
 
-    lax.fori_loop(0, n, prepare, 0)
     last = n // 2 - 1
 
     def fill(s, into):
@@ -311,6 +312,7 @@
     make_u(min(1, last), sets[1][0])
     for copy in copies:
         copy.wait()
+    tables.wait()
     fill(0, sets[0])
     for load in loads[1:]:
         load.wait()
@@ -354,8 +356,9 @@
     n = len(tiles)
     out = jax.ShapeDtypeStruct((3, 8, slots) if halo else (8, slots), F32)
     scratch = [
-        pltpu.SMEM((n * nb,), jnp.int32),
-        pltpu.SMEM((n * nb,), jnp.int32),
+        pltpu.VMEM((nb, tx, beads), jnp.int32),
+        pltpu.SMEM((nb, tx, beads), jnp.int32),
+        pltpu.SemaphoreType.DMA,
         pltpu.VMEM((n, f, beads), BF16),
         pltpu.VMEM((9, EXTRA, beads), BF16),
         pltpu.VMEM((9, 3, 8, beads), F32),
@@ -380,13 +383,13 @@
     return pl.pallas_call(
         lambda *refs: pairs_kernel(strips, halo, shape, *refs),
         out_shape=[out] * (3 if halo else 1),
-        in_specs=[SMEM, SMEM, SMEM, HBM, VMEM, VMEM, VMEM, VMEM, HBM]
+        in_specs=[SMEM, SMEM, VMEM, SMEM, HBM, VMEM, VMEM, VMEM, VMEM, HBM]
         + ([HBM] * 6 + [VMEM] if halo else []),
         out_specs=[VMEM] * (3 if halo else 1),
         scratch_shapes=scratch,
-        compiler_params=pltpu.CompilerParams(vmem_limit_bytes=LIMIT),
+        compiler_params=pltpu.CompilerParams(vmem_limit_bytes=MEDIUM if halo else LIMIT),
         cost_estimate=pl.CostEstimate(flops=n * 150_000_000, bytes_accessed=n * 100_000, transcendentals=0),
-    )(ids, partner, rate, features, weight_u, lever, slot, owner, own.reshape((tx * ty, rows, beads)), *(around if halo else []))
+    )(ids, partner, partner, rate, features, weight_u, lever, slot, owner, own.reshape((tx * ty, rows, beads)), *(around if halo else []))
 
 
 def rotation_rows(q):

time: 87.8 us -> 85.7 us (0.976)
  other arithmetic: 2.19 us -> 1.31 us
    unnamed x36 -> x30, local copies, waits for them, and re-layouts: 4.03 us -> 2.68 us
    unnamed x2, other arithmetic: 0.05 us -> 1.29 us
  transfers between devices with their start and end apart: 11 -> 11, of which waited for: 6 -> 6; matrix products, arithmetic and copies ran while one was open for 1% -> 4% of each run, Pallas kernels for 25% -> 27%
where the time goes in v5:
time: 85.7 us; the launch traced here: 85.4 us
  Pallas kernels  48.6 us (57%)
  starting transfers between devices  16 us (19%)
  waiting for transfers between devices  15.4 us (18%)
  local copies, waits for them, and re-layouts  3.28 us (4%)
  other arithmetic  1.31 us (2%)
  between operations  0.87 us (1%)
    pallas_call x2, Pallas kernels, pairs(): pl.pallas_call(lambda *refs: pairs_kernel(strips, halo, shape, *refs), ou...  41.7 us
    ppermute x11, starting transfers between devices, swap(): return lax.ppermute(value, axis, route)  16 us
    ppermute x11, waiting for transfers between devices, swap(): return lax.ppermute(value, axis, route)  15.4 us
    pallas_call x1, Pallas kernels, project(): pl.pallas_call(project_kernel, grid=(tx // STEP,), out_shape=[sds(tx, ty,...  4.41 us
    unnamed x30, local copies, waits for them, and re-layouts  2.68 us
    pallas_call x1, Pallas kernels, finish(): pl.pallas_call(lambda *refs: finish_kernel(len(sums), *refs), out_shape=[...  2.45 us
  transfers between devices with their start and end apart: 11, of which 6 were waited for; matrix products, arithmetic and copies ran while one was open for 4% of the time, Pallas kernels for 27%

profile of v5, /device:TPU:0, one launch (start us, length us, event | category | flops | bytes accessed | tf_op | source)
XLA Modules:
  0.0 85.4 jit_solution(15141439364453879685)
XLA Ops:
  0.6 4.4 %shard_map.149 = (bf16[8,8,144,128]{3,2,1,0:T(8,128)(2,1)}, bf16[1200,128]{1,0:T(8,128)(2,1)}, bf16[1200,128]{1,0:T(8,128)(2,1)}, bf16[8,144,128]{2,1,0:T(8,128)(2,1)}, bf16[8,144,128]{2,1,0:T(8,128)(2,1)}) custom-call(bf16[8,8,256,128]{3,2,1,0:T(8,128)(2,1)} %refs_4_.3, bf16[8,3,8,128]{3,2,1,0:T(8,128)(2,1)} %bitcast.30, bf16[128,256]{1,0:T(8,128)(2,1)} %weight_v.1, ...), custom_call_target="tpu_custom_call" | custom-call | tf_op jit(solution)/shard_map/pallas_call | solution.py:113
  5.6 3.6 %collective-permute-start.1 = (bf16[1200,128]{1,0:T(8,128)(2,1)}, bf16[1200,128]{1,0:T(8,128)(2,1)S(1)}, u32[]{:S(2)}, u32[]{:S(2)}) collective-permute-start(bf16[1200,128]{1,0:T(8,128)(2,1)} %get-tuple-element.14), channel_id=1, source_target_pairs={{1,2},{2,1},{3,4},{4,3},{5,6},{6,5},{7,0},{0,7},{9,10},{10,9},{11,... | collective-permute-start | bytes 921608 | tf_op jit(solution)/shard_map/ppermute | solution.py:508
  9.1 1.6 %collective-permute-start.2 = (bf16[8,144,128]{2,1,0:T(8,128)(2,1)}, bf16[8,144,128]{2,1,0:T(8,128)(2,1)S(1)}, u32[]{:S(2)}, u32[]{:S(2)}) collective-permute-start(bf16[8,144,128]{2,1,0:T(8,128)(2,1)} %get-tuple-element.15), channel_id=1, source_target_pairs={{0,8},{8,0},{16,24},{24,16},{1,9},{9,1},{17,25},{25,17},{2,10},{10... | collective-permute-start | bytes 884744 | tf_op jit(solution)/shard_map/ppermute | solution.py:508
  10.7 2.5 %collective-permute-start.3 = (bf16[8,144,128]{2,1,0:T(8,128)(2,1)}, bf16[8,144,128]{2,1,0:T(8,128)(2,1)}, u32[]{:S(2)}, u32[]{:S(2)}) collective-permute-start(bf16[8,144,128]{2,1,0:T(8,128)(2,1)} %get-tuple-element.16), channel_id=1, source_target_pairs={{8,16},{16,8},{24,0},{0,24},{9,17},{17,9},{25,1},{1,25},{10,18},{1... | collective-permute-start | bytes 884744 | tf_op jit(solution)/shard_map/ppermute | solution.py:508
  13.2 0.6 select_dynamic-update-slice_fusion.1
  13.8 2.5 %collective-permute-done.1.refs_11_.refs_7_ = bf16[1200,128]{1,0:T(8,128)(2,1)S(1)} collective-permute-done((bf16[1200,128]{1,0:T(8,128)(2,1)}, bf16[1200,128]{1,0:T(8,128)(2,1)S(1)}, u32[]{:S(2)}, u32[]{:S(2)}) %collective-permute-start.1) | collective-permute-done | bytes 307232 | tf_op jit(solution)/shard_map/ppermute | solution.py:508
  16.3 0.6 select_dynamic-update-slice_fusion
  17.0 1.3 %constant_dynamic-update-slice_fusion.5 = (bf16[432,128]{1,0:T(8,128)(2,1)}, bf16[432,128]{1,0:T(8,128)(2,1)}) fusion(bf16[432,128]{1,0:T(8,128)(2,1)} %get-tuple-element.30, bf16[1200,128]{1,0:T(8,128)(2,1)} %get-tuple-element.13, bf16[432,128]{1,0:T(8,128)(2,1)} %get-tuple-element.31), kind=kLoop, calls=%fused_computation.12 | loop fusion | bytes 36864
  18.3 0.6 constant_dynamic-update-slice_fusion.4
  18.9 0.6 constant_dynamic-update-slice_fusion.3
  19.5 1.9 %collective-permute-start.4 = (bf16[432,128]{1,0:T(8,128)(2,1)}, bf16[432,128]{1,0:T(8,128)(2,1)S(1)}, u32[]{:S(2)}, u32[]{:S(2)}) collective-permute-start(bf16[432,128]{1,0:T(8,128)(2,1)} %get-tuple-element.25), channel_id=1, source_target_pairs={{0,8},{8,0},{16,24},{24,16},{1,9},{9,1},{17,25},{25,17},{2,10},{10... | collective-permute-start | bytes 331784 | tf_op jit(solution)/shard_map/ppermute | solution.py:508
  21.4 2.5 %collective-permute-start.5 = (bf16[432,128]{1,0:T(8,128)(2,1)}, bf16[432,128]{1,0:T(8,128)(2,1)S(1)}, u32[]{:S(2)}, u32[]{:S(2)}) collective-permute-start(bf16[432,128]{1,0:T(8,128)(2,1)} %get-tuple-element.24), channel_id=1, source_target_pairs={{8,16},{16,8},{24,0},{0,24},{9,17},{17,9},{25,1},{1,25},{10,18},{1... | collective-permute-start | bytes 331784 | tf_op jit(solution)/shard_map/ppermute | solution.py:508
  24.0 23.0 %shard_map.150.refs_16_ = f32[8,128]{1,0:T(8,128)} custom-call(s32[36]{0:T(128)} %constant.15.clone.refs_0_, s32[6,8,8]{2,1,0:T(8,128)} %bitcast.42, s32[6,8,8]{2,1,0:T(8,128)} %bitcast.43, f32[4]{0:T(128)} %refs_3_.3, bf16[8,8,256,128]{3,2,1,0:T(8,128)(2,1)} %refs_4_.3, bf16[512,256]{1,0:T(8,128)(2,1)} %refs_5_.4, f32[8,3,8,128]{3,2,1,0:T(8,128)} %bitcast.32, ...), custom_call_target="tpu_custom_call" | custom-call | flops 5400000000 | bytes 3600000 | tf_op jit(solution)/shard_map/pallas_call | solution.py:383
  47.2 0.7 copy-done.13
  47.9 18.7 %shard_map.151 = (f32[3,8,128]{2,1,0:T(8,128)S(1)}, f32[3,8,128]{2,1,0:T(8,128)S(1)}, f32[3,8,128]{2,1,0:T(8,128)S(1)}) custom-call(s32[28]{0:T(128)S(1)} %copy-done.12, s32[6,8,8]{2,1,0:T(8,128)S(1)} %bitcast.44, s32[6,8,8]{2,1,0:T(8,128)S(1)} %bitcast.45, f32[4]{0:T(128)S(1)} %copy-done.11, bf16[8,8,256,128]{3,2,1,0:T(8,128)(2,1)S(1)} %copy-done, ...), custom_call_target="tpu_custom_call" | custom-call | flops 4200000000 | bytes 2800000 | tf_op jit(solution)/shard_map/pallas_call | solution.py:383
  66.7 1.2 %collective-permute-done.6 = f32[3,8,128]{2,1,0:T(8,128)S(1)} collective-permute-done((f32[3,8,128]{2,1,0:T(8,128)S(1)}, f32[3,8,128]{2,1,0:T(8,128)S(1)}, u32[]{:S(2)}, u32[]{:S(2)}) %collective-permute-start.6) | collective-permute-done | bytes 12320 | tf_op jit(solution)/shard_map/ppermute | solution.py:508
  67.8 1.4 %collective-permute-start.7 = (f32[2,3,8,128]{3,2,1,0:T(8,128)S(1)}, f32[2,3,8,128]{3,2,1,0:T(8,128)S(1)}, u32[]{:S(2)}, u32[]{:S(2)}) collective-permute-start(f32[2,3,8,128]{3,2,1,0:T(8,128)S(1)} %pad_maximum_fusion.2), channel_id=1, source_target_pairs={{1,2},{2,1},{3,4},{4,3},{5,6},{6,5},{7,0},{0,7},{9,10},{10,9},{11,... | collective-permute-start | bytes 73736 | tf_op jit(solution)/shard_map/ppermute | solution.py:508
  69.2 2.7 %collective-permute-done.7 = f32[2,3,8,128]{3,2,1,0:T(8,128)S(1)} collective-permute-done((f32[2,3,8,128]{3,2,1,0:T(8,128)S(1)}, f32[2,3,8,128]{3,2,1,0:T(8,128)S(1)}, u32[]{:S(2)}, u32[]{:S(2)}) %collective-permute-start.7) | collective-permute-done | bytes 24608 | tf_op jit(solution)/shard_map/ppermute | solution.py:508
  72.0 1.2 %collective-permute-done.8 = f32[3,8,128]{2,1,0:T(8,128)S(1)} collective-permute-done((f32[3,8,128]{2,1,0:T(8,128)S(1)}, f32[3,8,128]{2,1,0:T(8,128)S(1)}, u32[]{:S(2)}, u32[]{:S(2)}) %collective-permute-start.8) | collective-permute-done | bytes 12320 | tf_op jit(solution)/shard_map/ppermute | solution.py:508
  73.2 0.7 collective-permute-start.9
  73.8 3.3 %collective-permute-done.9.refs_1_ = f32[3,3,8,128]{3,2,1,0:T(8,128)S(1)} collective-permute-done((f32[3,3,8,128]{3,2,1,0:T(8,128)S(1)}, f32[3,3,8,128]{3,2,1,0:T(8,128)S(1)}, u32[]{:S(2)}, u32[]{:S(2)}) %collective-permute-start.9) | collective-permute-done | bytes 36896 | tf_op jit(solution)/shard_map/ppermute | solution.py:508
  77.1 1.4 %collective-permute-start.10 = (f32[3,3,8,128]{3,2,1,0:T(8,128)S(1)}, f32[3,3,8,128]{3,2,1,0:T(8,128)S(1)}, u32[]{:S(2)}, u32[]{:S(2)}) collective-permute-start(f32[3,3,8,128]{3,2,1,0:T(8,128)S(1)} %pad_maximum_fusion.1), channel_id=1, source_target_pairs={{8,16},{16,8},{24,0},{0,24},{9,17},{17,9},{25,1},{1,25},{10,18},{1... | collective-permute-start | bytes 110600 | tf_op jit(solution)/shard_map/ppermute | solution.py:508
  78.5 4.5 %collective-permute-done.10.refs_2_ = f32[3,3,8,128]{3,2,1,0:T(8,128)S(1)} collective-permute-done((f32[3,3,8,128]{3,2,1,0:T(8,128)S(1)}, f32[3,3,8,128]{3,2,1,0:T(8,128)S(1)}, u32[]{:S(2)}, u32[]{:S(2)}) %collective-permute-start.10) | collective-permute-done | bytes 36896 | tf_op jit(solution)/shard_map/ppermute | solution.py:508
  83.0 2.5 %shard_map.152 = (f32[8,3,8,128]{3,2,1,0:T(8,128)}, f32[1,13,1,128]{3,2,1,0:T(1,128)}) custom-call(f32[3,3,8,128]{3,2,1,0:T(8,128)S(1)} %pad_maximum_fusion.refs_0_, f32[3,3,8,128]{3,2,1,0:T(8,128)S(1)} %collective-permute-done.9.refs_1_, f32[3,3,8,128]{3,2,1,0:T(8,128)S(1)} %collective-permute-done.10.refs_2_, f32[1,7,1,128]{3,2,1,0:T(1,128)S(1)} %bitcast.37, ...), custom_call_target="tpu_custom_call" | custom-call | tf_op jit(solution)/shard_map/pallas_call | solution.py:493
  (41 shorter events, 0.7 us)
Async XLA Ops:
  5.0 8.1 %collective-permute-start = (bf16[1200,128]{1,0:T(8,128)(2,1)}, bf16[1200,128]{1,0:T(8,128)(2,1)S(1)}, u32[]{:S(2)}, u32[]{:S(2)}) collective-permute-start(bf16[1200,128]{1,0:T(8,128)(2,1)} %get-tuple-element.13), channel_id=1, source_target_pairs={{0,1},{1,0},{2,3},{3,2},{4,5},{5,4},{6,7},{7,6},{8,9},{9,8},{10,11... | collective-permute-start | bytes 921608 | tf_op jit(solution)/shard_map/ppermute | solution.py:508
  5.6 10.8 %collective-permute-start.1 = (bf16[1200,128]{1,0:T(8,128)(2,1)}, bf16[1200,128]{1,0:T(8,128)(2,1)S(1)}, u32[]{:S(2)}, u32[]{:S(2)}) collective-permute-start(bf16[1200,128]{1,0:T(8,128)(2,1)} %get-tuple-element.14), channel_id=1, source_target_pairs={{1,2},{2,1},{3,4},{4,3},{5,6},{6,5},{7,0},{0,7},{9,10},{10,9},{11,... | collective-permute-start | bytes 921608 | tf_op jit(solution)/shard_map/ppermute | solution.py:508
  9.1 38.0 %collective-permute-start.2 = (bf16[8,144,128]{2,1,0:T(8,128)(2,1)}, bf16[8,144,128]{2,1,0:T(8,128)(2,1)S(1)}, u32[]{:S(2)}, u32[]{:S(2)}) collective-permute-start(bf16[8,144,128]{2,1,0:T(8,128)(2,1)} %get-tuple-element.15), channel_id=1, source_target_pairs={{0,8},{8,0},{16,24},{24,16},{1,9},{9,1},{17,25},{25,17},{2,10},{10... | collective-permute-start | bytes 884744 | tf_op jit(solution)/shard_map/ppermute | solution.py:508
  10.7 36.4 %collective-permute-start.3 = (bf16[8,144,128]{2,1,0:T(8,128)(2,1)}, bf16[8,144,128]{2,1,0:T(8,128)(2,1)}, u32[]{:S(2)}, u32[]{:S(2)}) collective-permute-start(bf16[8,144,128]{2,1,0:T(8,128)(2,1)} %get-tuple-element.16), channel_id=1, source_target_pairs={{8,16},{16,8},{24,0},{0,24},{9,17},{17,9},{25,1},{1,25},{10,18},{1... | collective-permute-start | bytes 884744 | tf_op jit(solution)/shard_map/ppermute | solution.py:508
  19.5 27.6 %collective-permute-start.4 = (bf16[432,128]{1,0:T(8,128)(2,1)}, bf16[432,128]{1,0:T(8,128)(2,1)S(1)}, u32[]{:S(2)}, u32[]{:S(2)}) collective-permute-start(bf16[432,128]{1,0:T(8,128)(2,1)} %get-tuple-element.25), channel_id=1, source_target_pairs={{0,8},{8,0},{16,24},{24,16},{1,9},{9,1},{17,25},{25,17},{2,10},{10... | collective-permute-start | bytes 331784 | tf_op jit(solution)/shard_map/ppermute | solution.py:508
  21.4 25.7 %collective-permute-start.5 = (bf16[432,128]{1,0:T(8,128)(2,1)}, bf16[432,128]{1,0:T(8,128)(2,1)S(1)}, u32[]{:S(2)}, u32[]{:S(2)}) collective-permute-start(bf16[432,128]{1,0:T(8,128)(2,1)} %get-tuple-element.24), channel_id=1, source_target_pairs={{8,16},{16,8},{24,0},{0,24},{9,17},{17,9},{25,1},{1,25},{10,18},{1... | collective-permute-start | bytes 331784 | tf_op jit(solution)/shard_map/ppermute | solution.py:508
  23.9 23.2 %copy-start = (bf16[8,8,256,128]{3,2,1,0:T(8,128)(2,1)S(1)}, bf16[8,8,256,128]{3,2,1,0:T(8,128)(2,1)}, u32[]{:S(2)}) copy-start(bf16[8,8,256,128]{3,2,1,0:T(8,128)(2,1)} %refs_4_.3) | copy-start | bytes 12582916
  23.9 23.2 %copy-start.2 = (f32[8,8,3,128]{3,1,2,0:T(8,128)S(1)}, f32[8,8,3,128]{3,1,2,0:T(8,128)}, u32[]{:S(2)}) copy-start(f32[8,8,3,128]{3,1,2,0:T(8,128)} %param.16) | copy-start | bytes 294916
  23.9 23.2 %copy-start.3 = (s32[8,8,128]{2,1,0:T(8,128)S(1)}, s32[8,8,128]{2,1,0:T(8,128)}, u32[]{:S(2)}) copy-start(s32[8,8,128]{2,1,0:T(8,128)} %refs_12_.1) | copy-start | bytes 98308
  23.9 23.2 %copy-start.4 = (s32[8,8,128]{2,1,0:T(8,128)S(1)}, s32[8,8,128]{2,1,0:T(8,128)}, u32[]{:S(2)}) copy-start(s32[8,8,128]{2,1,0:T(8,128)} %refs_13_.1) | copy-start | bytes 98308
  23.9 23.2 %copy-start.8 = (bf16[8,8,144,128]{3,2,1,0:T(8,128)(2,1)S(1)}, bf16[8,8,144,128]{3,2,1,0:T(8,128)(2,1)}, u32[]{:S(2)}) copy-start(bf16[8,8,144,128]{3,2,1,0:T(8,128)(2,1)} %get-tuple-element.12) | copy-start | bytes 7077892
  23.9 23.2 %copy-start.9 = (bf16[512,256]{1,0:T(8,128)(2,1)S(1)}, bf16[512,256]{1,0:T(8,128)(2,1)}, u32[]{:S(2)}) copy-start(bf16[512,256]{1,0:T(8,128)(2,1)} %refs_5_.4) | copy-start | bytes 786436
  23.9 23.2 %copy-start.10 = (s32[8,8,6]{1,0,2:T(8,128)S(1)}, s32[8,8,6]{1,0,2:T(8,128)}, u32[]{:S(2)}) copy-start(s32[8,8,6]{1,0,2:T(8,128)} %param.17) | copy-start | bytes 4612
  24.0 23.2 %copy-start.11 = (f32[4]{0:T(128)S(1)}, f32[4]{0:T(128)}, u32[]{:S(2)}) copy-start(f32[4]{0:T(128)} %refs_3_.3) | copy-start | bytes 52
  24.0 23.2 %copy-start.12 = (s32[28]{0:T(128)S(1)}, s32[28]{0:T(128)}, u32[]{:S(2)}) copy-start(s32[28]{0:T(128)} %constant.16.clone.refs_0_) | copy-start | bytes 340
  47.0 36.0 %copy-start.1 = (bf16[8,8,3,128]{3,1,2,0:T(8,128)(2,1)S(1)}, bf16[8,8,3,128]{3,1,2,0:T(8,128)(2,1)}, u32[]{:S(2)}) copy-start(bf16[8,8,3,128]{3,1,2,0:T(8,128)(2,1)} %param.14) | copy-start | bytes 147460
  47.0 36.0 %copy-start.5 = (f32[1,1,7,128]{3,1,2,0:T(1,128)S(1)}, f32[1,1,7,128]{3,1,2,0:T(1,128)}, u32[]{:S(2)}) copy-start(f32[1,1,7,128]{3,1,2,0:T(1,128)} %param.20) | copy-start | bytes 10756
  47.0 35.9 %copy-start.6 = (f32[1,1,6,128]{3,1,2,0:T(1,128)S(1)}, f32[1,1,6,128]{3,1,2,0:T(1,128)}, u32[]{:S(2)}) copy-start(f32[1,1,6,128]{3,1,2,0:T(1,128)} %param.21) | copy-start | bytes 9220
  47.0 35.9 %copy-start.7 = (f32[1,1,4,128]{3,2,1,0:T(4,128)S(1)}, f32[1,1,4,128]{3,2,1,0:T(4,128)}, u32[]{:S(2)}) copy-start(f32[1,1,4,128]{3,2,1,0:T(4,128)} %refs_5_.5) | copy-start | bytes 6148
  66.6 1.2 %collective-permute-start.6 = (f32[3,8,128]{2,1,0:T(8,128)S(1)}, f32[3,8,128]{2,1,0:T(8,128)S(1)}, u32[]{:S(2)}, u32[]{:S(2)}) collective-permute-start(f32[3,8,128]{2,1,0:T(8,128)S(1)} %get-tuple-element.18), channel_id=1, source_target_pairs={{0,1},{1,0},{2,3},{3,2},{4,5},{5,4},{6,7},{7,6},{8,9},{9,8},{10,11... | collective-permute-start | bytes 36872 | tf_op jit(solution)/shard_map/ppermute | solution.py:508
  67.8 4.2 %collective-permute-start.7 = (f32[2,3,8,128]{3,2,1,0:T(8,128)S(1)}, f32[2,3,8,128]{3,2,1,0:T(8,128)S(1)}, u32[]{:S(2)}, u32[]{:S(2)}) collective-permute-start(f32[2,3,8,128]{3,2,1,0:T(8,128)S(1)} %pad_maximum_fusion.2), channel_id=1, source_target_pairs={{1,2},{2,1},{3,4},{4,3},{5,6},{6,5},{7,0},{0,7},{9,10},{10,9},{11,... | collective-permute-start | bytes 73736 | tf_op jit(solution)/shard_map/ppermute | solution.py:508
  72.0 1.2 %collective-permute-start.8 = (f32[3,8,128]{2,1,0:T(8,128)S(1)}, f32[3,8,128]{2,1,0:T(8,128)S(1)}, u32[]{:S(2)}, u32[]{:S(2)}) collective-permute-start(f32[3,8,128]{2,1,0:T(8,128)S(1)} %get-tuple-element.37), channel_id=1, source_target_pairs={{0,1},{1,0},{2,3},{3,2},{4,5},{5,4},{6,7},{7,6},{8,9},{9,8},{10,11... | collective-permute-start | bytes 36872 | tf_op jit(solution)/shard_map/ppermute | solution.py:508
  73.2 4.0 %collective-permute-start.9 = (f32[3,3,8,128]{3,2,1,0:T(8,128)S(1)}, f32[3,3,8,128]{3,2,1,0:T(8,128)S(1)}, u32[]{:S(2)}, u32[]{:S(2)}) collective-permute-start(f32[3,3,8,128]{3,2,1,0:T(8,128)S(1)} %pad_maximum_fusion.refs_0_), channel_id=1, source_target_pairs={{0,8},{8,0},{16,24},{24,16},{1,9},{9,1},{17,25},{25,17},{2,10},{10... | collective-permute-start | bytes 110600 | tf_op jit(solution)/shard_map/ppermute | solution.py:508
  77.1 5.8 %collective-permute-start.10 = (f32[3,3,8,128]{3,2,1,0:T(8,128)S(1)}, f32[3,3,8,128]{3,2,1,0:T(8,128)S(1)}, u32[]{:S(2)}, u32[]{:S(2)}) collective-permute-start(f32[3,3,8,128]{3,2,1,0:T(8,128)S(1)} %pad_maximum_fusion.1), channel_id=1, source_target_pairs={{8,16},{16,8},{24,0},{0,24},{9,17},{17,9},{25,1},{1,25},{10,18},{1... | collective-permute-start | bytes 110600 | tf_op jit(solution)/shard_map/ppermute | solution.py:508
  (1 other events, 0.7 us)

commit v6 on v5

--- a/solution.py
+++ b/solution.py
@@ -73,25 +73,29 @@
         col_in[at, :] = jnp.where(high_y, low, high)
         col_out[at, :] = jnp.where(high_y, high, low)
 
+    def put(row, z):
+        for y in range(tiles_y):
+            row[y * rows : (y + 1) * rows, :] = own[z, y]
+
     @pl.when(x == 0)
     def _():
         @pl.when(high_x)
         def _():
-            row_in[...] = own[0]
+            put(row_in, 0)
 
         @pl.when(~high_x)
         def _():
-            row_out[...] = own[0]
+            put(row_out, 0)
 
     @pl.when(x == tiles_x - 1)
     def _():
         @pl.when(high_x)
         def _():
-            row_out[...] = own[step - 1]
+            put(row_out, step - 1)
 
         @pl.when(~high_x)
         def _():
-            row_in[...] = own[step - 1]
+            put(row_in, step - 1)
 
     @pl.when(x == 0)
     def _():
@@ -99,9 +103,8 @@
             [pose[0, r] for r in range(3, 7)] + [motion[0, r] for r in range(6)]
             + [inverse[0, 0, r : r + 1, :] for r in range(4)] + [jnp.zeros((2, beads), F32)], axis=0)
         body = jnp.concatenate(split_three(body), axis=0)
-        end = col_in.shape[0] - BODY
-        col_in[end:, :] = body
-        col_out[end:, :] = body
+        for message in (col_in, col_out, row_in, row_out):
+            message[message.shape[0] - BODY :, :] = body
 
 
 def project(features, pos, weight_v, pose, motion, inverse):
@@ -109,11 +112,11 @@
     rows = beads + EXTRA
     whole = lambda s: pl.BlockSpec(s, lambda i: (0,) * len(s))
     sds = lambda *s: jax.ShapeDtypeStruct(s, BF16)
-    col = (tx * rows + BODY, beads)
+    col, line = (tx * rows + BODY, beads), (ty * rows + BODY, beads)
     return pl.pallas_call(
         project_kernel,
         grid=(tx // STEP,),
-        out_shape=[sds(tx, ty, rows, beads), sds(*col), sds(*col), sds(ty, rows, beads), sds(ty, rows, beads)],
+        out_shape=[sds(tx, ty, rows, beads), sds(*col), sds(*col), sds(*line), sds(*line)],
         in_specs=[
             pl.BlockSpec((STEP, ty, f, beads), lambda i: (i, 0, 0, 0)),
             pl.BlockSpec((STEP, 3, ty, beads), lambda i: (i, 0, 0, 0)),
@@ -121,7 +124,7 @@
         ],
         out_specs=[
             pl.BlockSpec((STEP, ty, rows, beads), lambda i: (i, 0, 0, 0)),
-            whole(col), whole(col), whole((ty, rows, beads)), whole((ty, rows, beads)),
+            whole(col), whole(col), whole(line), whole(line),
         ],
         compiler_params=pltpu.CompilerParams(vmem_limit_bytes=LIMIT),
     )(features, pos, weight_v, pose, motion, inverse)
@@ -137,22 +140,13 @@
     around = take(7) if halo else []
     sums = take(3 if halo else 1)
     table, where_to, tsem = take(3)
-    feat, shift_of, norm_of, terms, fsem = take(5)
+    shift_of, norm_of, terms = take(3)
     sets = [take(7), take(7)]
-    vp, vsem = take(2)
-    total, parts = take(2) if halo else (sums[0], None)
+    vp, vsem, total, parts = take(4) if halo else (own, None, sums[0], None)
     wide = ty + 2
     here = lambda i, j: (i + 1) * wide + j + 1 if halo else i * ty + j
     side = chans * width_h
 
-    at = 0
-    loads = []
-    for q, (i, j) in enumerate(strips):
-        size = max(len(i), len(j))
-        src = features.at[i[0], j[0] : j[-1] + 1] if len(i) == 1 else features.at[i[0] : i[-1] + 1, j[0]]
-        loads.append(pltpu.make_async_copy(src, feat.at[at : at + size], fsem.at[q]))
-        loads[-1].start()
-        at += size
     if halo:
         rows = beads + EXTRA
         high_x, high_y = outward("gx"), outward("gy")
@@ -166,14 +160,13 @@
                 pairs_of.append((col.at[pl.ds(i * rows, rows)], vp.at[(i + 1) * wide + y]))
             pairs_of.append((own.at[i * ty : (i + 1) * ty], line(i + 1)))
         for src, end, x in zip(lines, ends, (x_in, x_out)):
-            pairs_of.append((src, line(x)))
+            for y in range(ty):
+                pairs_of.append((src.at[pl.ds(y * rows, rows)], vp.at[x * wide + 1 + y]))
             pairs_of.append((end.at[pl.ds(0, rows)], vp.at[x * wide + y_in]))
             pairs_of.append((end.at[pl.ds(rows, rows)], vp.at[x * wide + y_out]))
-    else:
-        pairs_of = [(own, vp)]
-    copies = [pltpu.make_async_copy(src, dst, vsem.at[q]) for q, (src, dst) in enumerate(pairs_of)]
-    for copy in copies:
-        copy.start()
+        copies = [pltpu.make_async_copy(src, dst, vsem.at[q]) for q, (src, dst) in enumerate(pairs_of)]
+        for copy in copies:
+            copy.start()
     total[...] = around[6][...] if halo else jnp.zeros_like(total)
 
     def where_is(t):
@@ -197,7 +190,8 @@
             norm_of[c, q] = jnp.full((8, beads), val, F32)
 
     def make_u(s, ub):
-        both = jnp.concatenate([feat[2 * s], feat[2 * s + 1]], axis=1)
+        (i, j), (k, l) = where_is(2 * s), where_is(2 * s + 1)
+        both = jnp.concatenate([features[i, j], features[k, l]], axis=1)
         u = jnp.dot(weight_u[...], both, preferred_element_type=F32).astype(BF16)
         for e in range(2):
             for k in range(chans):
@@ -307,15 +301,13 @@
         gather(2 * before + 1, later[6])
         total[...] = total[...] + jnp.where(s == 0, 0.0, add_up(before))
 
-    loads[0].wait()
     make_u(0, sets[0][0])
     make_u(min(1, last), sets[1][0])
-    for copy in copies:
-        copy.wait()
+    if halo:
+        for copy in copies:
+            copy.wait()
     tables.wait()
     fill(0, sets[0])
-    for load in loads[1:]:
-        load.wait()
 
     def body(g, carry):
         half(2 * g, sets[0], sets[1])
@@ -359,11 +351,9 @@
         pltpu.VMEM((nb, tx, beads), jnp.int32),
         pltpu.SMEM((nb, tx, beads), jnp.int32),
         pltpu.SemaphoreType.DMA,
-        pltpu.VMEM((n, f, beads), BF16),
         pltpu.VMEM((9, EXTRA, beads), BF16),
         pltpu.VMEM((9, 3, 8, beads), F32),
         pltpu.VMEM((n, 16, beads), BF16),
-        pltpu.SemaphoreType.DMA((len(strips),)),
     ]
     scratch += 2 * [
         pltpu.VMEM((2, width_h, chans * beads), BF16),
@@ -374,20 +364,19 @@
         pltpu.VMEM((nb * beads, beads), BF16),
         pltpu.VMEM((nb * beads, beads), BF16),
     ]
-    spread = (tx + 2) * (ty + 2) if halo else tx * ty
-    scratch += [pltpu.VMEM((spread, rows, beads), BF16), pltpu.SemaphoreType.DMA((3 * tx + 6 if halo else 1,))]
     if halo:
-        scratch += [pltpu.VMEM((8, slots), F32), pltpu.VMEM((3, 3, 8, slots), F32)]
+        scratch += [pltpu.VMEM(((tx + 2) * (ty + 2), rows, beads), BF16), pltpu.SemaphoreType.DMA((3 * tx + 2 * ty + 4,)),
+                    pltpu.VMEM((8, slots), F32), pltpu.VMEM((3, 3, 8, slots), F32)]
     ids = jnp.asarray([i * ty + j for i, j in tiles], jnp.int32)
     shape = (tx, ty, beads, width_h, chans, nb, slots)
     return pl.pallas_call(
         lambda *refs: pairs_kernel(strips, halo, shape, *refs),
         out_shape=[out] * (3 if halo else 1),
-        in_specs=[SMEM, SMEM, VMEM, SMEM, HBM, VMEM, VMEM, VMEM, VMEM, HBM]
+        in_specs=[SMEM, SMEM, VMEM, SMEM, VMEM, VMEM, VMEM, VMEM, VMEM, HBM if halo else VMEM]
         + ([HBM] * 6 + [VMEM] if halo else []),
         out_specs=[VMEM] * (3 if halo else 1),
         scratch_shapes=scratch,
-        compiler_params=pltpu.CompilerParams(vmem_limit_bytes=MEDIUM if halo else LIMIT),
+        compiler_params=pltpu.CompilerParams(vmem_limit_bytes=MEDIUM),
         cost_estimate=pl.CostEstimate(flops=n * 150_000_000, bytes_accessed=n * 100_000, transcendentals=0),
     )(ids, partner, partner, rate, features, weight_u, lever, slot, owner, own.reshape((tx * ty, rows, beads)), *(around if halo else []))
 
@@ -427,17 +416,17 @@
     finish_body(sums, *refs)
 
 
-def finish_body(sums, pose, motion, inverse, col_a, col_b, end_a, end_b, pos, lever, slot, owner,
-                  moved, state, table):
+def finish_body(sums, pose, motion, inverse, col_a, col_b, line_a, line_b, end_a, end_b, pos, lever, slot, owner,
+                moved, state, table):
     tx, ty = pos.shape[0], pos.shape[2]
     slots = owner.shape[2]
     high_x, high_y = outward("gx"), outward("gy")
     turn = lambda d, high: 1 + jnp.where(high, d, -d)
-    rows_a, rows_b = end_a.shape[0] - 3 * BODY, col_a.shape[0] - BODY
-    bodies = {(1, 0): (col_a, rows_b), (1, 2): (col_b, rows_b)}
-    for a, end in ((0, end_a), (2, end_b)):
-        for q, b in enumerate((1, 0, 2)):
-            bodies[a, b] = (end, rows_a + q * BODY)
+    bodies = {}
+    for (a, b), ref in {(1, 0): col_a, (1, 2): col_b, (0, 1): line_a, (2, 1): line_b, (0, 2): end_a, (2, 2): end_b}.items():
+        bodies[a, b] = (ref, ref.shape[0] - BODY)
+    for a, ref in ((0, end_a), (2, end_b)):
+        bodies[a, 0] = (ref, ref.shape[0] - 2 * BODY)
     if len(sums) == 1:
         totals = lambda b, a: sums[0][a, b]
     else:
@@ -488,16 +477,42 @@
                     moved[i, r, j : j + 1, :] = moved[i, r, j : j + 1, :] + val
 
 
-def finish(sums, pose, motion, inverse, cols, ends, pos, lever, slot, owner):
+def finish(sums, pose, motion, inverse, cols, lines, ends, pos, lever, slot, owner):
     slots = pose.shape[3]
     return pl.pallas_call(
         lambda *refs: finish_kernel(len(sums), *refs),
         out_shape=[jax.ShapeDtypeStruct(lever.shape, F32), jax.ShapeDtypeStruct((1, 13, 1, slots), F32)],
-        in_specs=[VMEM] * (11 + len(sums)),
+        in_specs=[VMEM] * (13 + len(sums)),
         out_specs=[VMEM] * 2,
         scratch_shapes=[pltpu.VMEM((3, 3, 32, slots), BF16)],
         compiler_params=pltpu.CompilerParams(vmem_limit_bytes=SMALL),
-    )(*sums, pose, motion, inverse, *cols, *ends, pos, lever, slot, owner)
+    )(*sums, pose, motion, inverse, *cols, *lines, *ends, pos, lever, slot, owner)
+
+
+def corner_kernel(col_a, col_b, end_in, end_out):
+    rows = (end_in.shape[0] - 2 * BODY) // 2
+    last = col_a.shape[0] - BODY - rows
+    high = outward("gx")
+    for q, col in enumerate((col_a, col_b)):
+        first, final = col[0:rows, :], col[last : last + rows, :]
+        end_in[q * rows : (q + 1) * rows, :] = jnp.where(high, first, final)
+        end_out[q * rows : (q + 1) * rows, :] = jnp.where(high, final, first)
+    for q, col in enumerate((col_a, col_b)):
+        body = col[last + rows :, :]
+        at = 2 * rows + q * BODY
+        end_in[at : at + BODY, :] = body
+        end_out[at : at + BODY, :] = body
+
+
+def corners(col_a, col_b, rows):
+    out = jax.ShapeDtypeStruct((2 * (rows + BODY), col_a.shape[1]), BF16)
+    return pl.pallas_call(
+        corner_kernel,
+        out_shape=[out] * 2,
+        in_specs=[VMEM] * 2,
+        out_specs=[VMEM] * 2,
+        compiler_params=pltpu.CompilerParams(vmem_limit_bytes=SMALL),
+    )(col_a, col_b)
 
 
 def swap(value, axis, start):
@@ -527,11 +542,8 @@
     own, col_in, col_out, row_in, row_out = project(features, pos, weight_v, pose, motion, body_inverse)
     line_a, line_b = inside(row_in, "gx"), outside(row_out, "gx")
     col_a, col_b = inside(col_in, "gy"), outside(col_out, "gy")
-    high_x = outward("gx")
-    bodies = [v[tx * rows :] for v in (col_in, col_a, col_b)]
-    corner = lambda high: jnp.concatenate(
-        [jnp.where(high, v[(tx - 1) * rows : tx * rows], v[:rows]) for v in (col_a, col_b)] + bodies, axis=0)
-    end_a, end_b = inside(corner(~high_x), "gx"), outside(corner(high_x), "gx")
+    end_in, end_out = corners(col_a, col_b, rows)
+    end_a, end_b = inside(end_in, "gx"), outside(end_out, "gx")
     args = (codes, radial_rate, features, weight_u, lever, body_slot, owner_dir, slots)
     inner = [((i,), range(1, ty - 1)) for i in range(1, tx - 1)]
     rim = [((0,), range(ty)), ((tx - 1,), range(ty)), (range(1, tx - 1), (0,)), (range(1, tx - 1), (ty - 1,))]
@@ -550,7 +562,7 @@
         got = outside(jnp.stack([cols[2], mine]), "gx")
         mine = mine + got[0]
         sums = [jnp.stack([inside(mine, "gx"), mine, got[1] + cols[2]])]
-    moved, state = finish(sums, pose, motion, body_inverse, (col_a, col_b), (end_a, end_b),
+    moved, state = finish(sums, pose, motion, body_inverse, (col_a, col_b), (line_a, line_b), (end_a, end_b),
                           pos, lever, body_slot, owner_dir)
     return (jnp.transpose(moved, (0, 2, 1, 3)), jnp.transpose(state, (0, 2, 1, 3)))
 

time: 85.7 us -> 81.7 us (0.953)
  Pallas kernels: 48.6 us -> 46.8 us
  local copies, waits for them, and re-layouts: 3.28 us -> 1.72 us
  other arithmetic: 1.31 us -> 0.03 us
    pallas_call x2, Pallas kernels: 41.7 us -> 39.7 us  [pairs(): pl.pallas_call(lambda *refs: pairs_kernel(strips, halo, shape, *refs), ou...]
    unnamed x2 -> x0, other arithmetic: 1.29 us -> none
    unnamed x30 -> x28, local copies, waits for them, and re-layouts: 2.68 us -> 1.72 us
  transfers between devices with their start and end apart: 11 -> 11, of which waited for: 6 -> 6; matrix products, arithmetic and copies ran while one was open for 4% -> 0% of each run, Pallas kernels for 27% -> 25%
where the time goes in v6:
time: 81.7 us; the launch traced here: 81.5 us
  Pallas kernels  46.8 us (57%)
  starting transfers between devices  16.2 us (20%)
  waiting for transfers between devices  15.9 us (19%)
  local copies, waits for them, and re-layouts  1.72 us (2%)
  between operations  0.87 us (1%)
    pallas_call x2, Pallas kernels, pairs(): pl.pallas_call(lambda *refs: pairs_kernel(strips, halo, shape, *refs), ou...  39.7 us
    ppermute x11, starting transfers between devices, swap(): return lax.ppermute(value, axis, route)  16.2 us
    ppermute x11, waiting for transfers between devices, swap(): return lax.ppermute(value, axis, route)  15.9 us
    pallas_call x1, Pallas kernels, project(): pl.pallas_call(project_kernel, grid=(tx // STEP,), out_shape=[sds(tx, ty,...  4.6 us
    pallas_call x1, Pallas kernels, finish(): pl.pallas_call(lambda *refs: finish_kernel(len(sums), *refs), out_shape=[...  2.45 us
    unnamed x28, local copies, waits for them, and re-layouts  1.72 us
  transfers between devices with their start and end apart: 11, of which 6 were waited for; matrix products, arithmetic and copies ran while one was open for 0% of the time, Pallas kernels for 25%

profile of v6, /device:TPU:0, one launch (start us, length us, event | category | flops | bytes accessed | tf_op | source)
XLA Modules:
  0.0 81.5 jit_solution(2859087850543517304)
XLA Ops:
  0.6 0.0 copy-start.13
  0.7 4.6 %shard_map.149 = (bf16[8,8,144,128]{3,2,1,0:T(8,128)(2,1)}, bf16[1200,128]{1,0:T(8,128)(2,1)}, bf16[1200,128]{1,0:T(8,128)(2,1)}, bf16[1200,128]{1,0:T(8,128)(2,1)}, bf16[1200,128]{1,0:T(8,128)(2,1)}) custom-call(bf16[8,8,256,128]{3,2,1,0:T(8,128)(2,1)} %refs_4_.3, bf16[8,3,8,128]{3,2,1,0:T(8,128)(2,1)} %bitcast.30, bf16[128,256]{1,0:T(8,128)(2,1)} %weight_v.1, ...), custom_call_target="tpu_custom_call" | custom-call | tf_op jit(solution)/shard_map/pallas_call | solution.py:116
  5.3 0.5 collective-permute-start
  5.8 3.6 %collective-permute-start.1 = (bf16[1200,128]{1,0:T(8,128)(2,1)}, bf16[1200,128]{1,0:T(8,128)(2,1)S(1)}, u32[]{:S(2)}, u32[]{:S(2)}) collective-permute-start(bf16[1200,128]{1,0:T(8,128)(2,1)} %get-tuple-element.16), channel_id=1, source_target_pairs={{1,2},{2,1},{3,4},{4,3},{5,6},{6,5},{7,0},{0,7},{9,10},{10,9},{11,... | collective-permute-start | bytes 921608 | tf_op jit(solution)/shard_map/ppermute | solution.py:523
  9.4 1.6 %collective-permute-start.2 = (bf16[1200,128]{1,0:T(8,128)(2,1)}, bf16[1200,128]{1,0:T(8,128)(2,1)S(1)}, u32[]{:S(2)}, u32[]{:S(2)}) collective-permute-start(bf16[1200,128]{1,0:T(8,128)(2,1)} %get-tuple-element.17), channel_id=1, source_target_pairs={{0,8},{8,0},{16,24},{24,16},{1,9},{9,1},{17,25},{25,17},{2,10},{10... | collective-permute-start | bytes 921608 | tf_op jit(solution)/shard_map/ppermute | solution.py:523
  11.0 2.5 %collective-permute-start.3 = (bf16[1200,128]{1,0:T(8,128)(2,1)}, bf16[1200,128]{1,0:T(8,128)(2,1)S(1)}, u32[]{:S(2)}, u32[]{:S(2)}) collective-permute-start(bf16[1200,128]{1,0:T(8,128)(2,1)} %get-tuple-element.18), channel_id=1, source_target_pairs={{8,16},{16,8},{24,0},{0,24},{9,17},{17,9},{25,1},{1,25},{10,18},{1... | collective-permute-start | bytes 921608 | tf_op jit(solution)/shard_map/ppermute | solution.py:523
  13.4 3.2 %collective-permute-done.1.col_b.refs_11_.refs_7_ = bf16[1200,128]{1,0:T(8,128)(2,1)S(1)} collective-permute-done((bf16[1200,128]{1,0:T(8,128)(2,1)}, bf16[1200,128]{1,0:T(8,128)(2,1)S(1)}, u32[]{:S(2)}, u32[]{:S(2)}) %collective-permute-start.1) | collective-permute-done | bytes 307232 | tf_op jit(solution)/shard_map/ppermute | solution.py:523
  16.7 2.0 %collective-permute-start.4 = (bf16[384,128]{1,0:T(8,128)(2,1)S(1)}, bf16[384,128]{1,0:T(8,128)(2,1)S(1)}, u32[]{:S(2)}, u32[]{:S(2)}) collective-permute-start(bf16[384,128]{1,0:T(8,128)(2,1)S(1)} %get-tuple-element.19), channel_id=1, source_target_pairs={{0,8},{8,0},{16,24},{24,16},{1,9},{9,1},{17,25},{25,17},{2,10},{10... | collective-permute-start | bytes 294920 | tf_op jit(solution)/shard_map/ppermute | solution.py:523
  18.6 2.5 %collective-permute-start.5 = (bf16[384,128]{1,0:T(8,128)(2,1)S(1)}, bf16[384,128]{1,0:T(8,128)(2,1)S(1)}, u32[]{:S(2)}, u32[]{:S(2)}) collective-permute-start(bf16[384,128]{1,0:T(8,128)(2,1)S(1)} %get-tuple-element.20), channel_id=1, source_target_pairs={{8,16},{16,8},{24,0},{0,24},{9,17},{17,9},{25,1},{1,25},{10,18},{1... | collective-permute-start | bytes 294920 | tf_op jit(solution)/shard_map/ppermute | solution.py:523
  21.2 1.7 %copy-done.8 = bf16[8,8,144,128]{3,2,1,0:T(8,128)(2,1)S(1)} copy-done((bf16[8,8,144,128]{3,2,1,0:T(8,128)(2,1)S(1)}, bf16[8,8,144,128]{3,2,1,0:T(8,128)(2,1)}, u32[]{:S(2)}) %copy-start.8) | copy-done | bytes 2359320
  22.8 20.3 %shard_map.151.refs_16_ = f32[8,128]{1,0:T(8,128)S(1)} custom-call(s32[36]{0:T(128)S(1)} %copy-done.13, s32[6,8,8]{2,1,0:T(8,128)S(1)} %bitcast.42, s32[6,8,8]{2,1,0:T(8,128)S(1)} %bitcast.43, f32[4]{0:T(128)S(1)} %copy-done.11, bf16[8,8,256,128]{3,2,1,0:T(8,128)(2,1)S(1)} %copy-done, bf16[512,256]{1,0:T(8,128)(2,1)S(1)} %copy-done.9, ...), custom_call_target="tpu_custom_call" | custom-call | flops 5400000000 | bytes 3600000 | tf_op jit(solution)/shard_map/pallas_call | solution.py:372
  43.1 0.0 copy-start.1
  43.1 0.0 copy-start.5
  43.2 19.5 %shard_map.152 = (f32[3,8,128]{2,1,0:T(8,128)S(1)}, f32[3,8,128]{2,1,0:T(8,128)S(1)}, f32[3,8,128]{2,1,0:T(8,128)S(1)}) custom-call(s32[28]{0:T(128)S(1)} %copy-done.12, s32[6,8,8]{2,1,0:T(8,128)S(1)} %bitcast.44, s32[6,8,8]{2,1,0:T(8,128)S(1)} %bitcast.45, f32[4]{0:T(128)S(1)} %copy-done.11, bf16[8,8,256,128]{3,2,1,0:T(8,128)(2,1)S(1)} %copy-done, ...), custom_call_target="tpu_custom_call" | custom-call | flops 4200000000 | bytes 2800000 | tf_op jit(solution)/shard_map/pallas_call | solution.py:372
  62.7 0.1 collective-permute-start.6
  62.7 1.2 %collective-permute-done.6 = f32[3,8,128]{2,1,0:T(8,128)S(1)} collective-permute-done((f32[3,8,128]{2,1,0:T(8,128)S(1)}, f32[3,8,128]{2,1,0:T(8,128)S(1)}, u32[]{:S(2)}, u32[]{:S(2)}) %collective-permute-start.6) | collective-permute-done | bytes 12320 | tf_op jit(solution)/shard_map/ppermute | solution.py:523
  63.9 1.5 %collective-permute-start.7 = (f32[2,3,8,128]{3,2,1,0:T(8,128)S(1)}, f32[2,3,8,128]{3,2,1,0:T(8,128)S(1)}, u32[]{:S(2)}, u32[]{:S(2)}) collective-permute-start(f32[2,3,8,128]{3,2,1,0:T(8,128)S(1)} %pad_maximum_fusion.2), channel_id=1, source_target_pairs={{1,2},{2,1},{3,4},{4,3},{5,6},{6,5},{7,0},{0,7},{9,10},{10,9},{11,... | collective-permute-start | bytes 73736 | tf_op jit(solution)/shard_map/ppermute | solution.py:523
  65.4 2.7 %collective-permute-done.7 = f32[2,3,8,128]{3,2,1,0:T(8,128)S(1)} collective-permute-done((f32[2,3,8,128]{3,2,1,0:T(8,128)S(1)}, f32[2,3,8,128]{3,2,1,0:T(8,128)S(1)}, u32[]{:S(2)}, u32[]{:S(2)}) %collective-permute-start.7) | collective-permute-done | bytes 24608 | tf_op jit(solution)/shard_map/ppermute | solution.py:523
  68.1 1.2 %collective-permute-done.8 = f32[3,8,128]{2,1,0:T(8,128)S(1)} collective-permute-done((f32[3,8,128]{2,1,0:T(8,128)S(1)}, f32[3,8,128]{2,1,0:T(8,128)S(1)}, u32[]{:S(2)}, u32[]{:S(2)}) %collective-permute-start.8) | collective-permute-done | bytes 12320 | tf_op jit(solution)/shard_map/ppermute | solution.py:523
  69.3 0.7 collective-permute-start.9
  69.9 3.3 %collective-permute-done.9.refs_1_ = f32[3,3,8,128]{3,2,1,0:T(8,128)S(1)} collective-permute-done((f32[3,3,8,128]{3,2,1,0:T(8,128)S(1)}, f32[3,3,8,128]{3,2,1,0:T(8,128)S(1)}, u32[]{:S(2)}, u32[]{:S(2)}) %collective-permute-start.9) | collective-permute-done | bytes 36896 | tf_op jit(solution)/shard_map/ppermute | solution.py:523
  73.2 1.4 %collective-permute-start.10 = (f32[3,3,8,128]{3,2,1,0:T(8,128)S(1)}, f32[3,3,8,128]{3,2,1,0:T(8,128)S(1)}, u32[]{:S(2)}, u32[]{:S(2)}) collective-permute-start(f32[3,3,8,128]{3,2,1,0:T(8,128)S(1)} %pad_maximum_fusion.1), channel_id=1, source_target_pairs={{8,16},{16,8},{24,0},{0,24},{9,17},{17,9},{25,1},{1,25},{10,18},{1... | collective-permute-start | bytes 110600 | tf_op jit(solution)/shard_map/ppermute | solution.py:523
  74.7 4.4 %collective-permute-done.10.refs_2_ = f32[3,3,8,128]{3,2,1,0:T(8,128)S(1)} collective-permute-done((f32[3,3,8,128]{3,2,1,0:T(8,128)S(1)}, f32[3,3,8,128]{3,2,1,0:T(8,128)S(1)}, u32[]{:S(2)}, u32[]{:S(2)}) %collective-permute-start.10) | collective-permute-done | bytes 36896 | tf_op jit(solution)/shard_map/ppermute | solution.py:523
  79.1 2.5 %shard_map.153 = (f32[8,3,8,128]{3,2,1,0:T(8,128)}, f32[1,13,1,128]{3,2,1,0:T(1,128)}) custom-call(f32[3,3,8,128]{3,2,1,0:T(8,128)S(1)} %pad_maximum_fusion.refs_0_, f32[3,3,8,128]{3,2,1,0:T(8,128)S(1)} %collective-permute-done.9.refs_1_, f32[3,3,8,128]{3,2,1,0:T(8,128)S(1)} %collective-permute-done.10.refs_2_, f32[1,7,1,128]{3,2,1,0:T(1,128)S(1)} %bitcast.37, ...), custom_call_target="tpu_custom_call" | custom-call | tf_op jit(solution)/shard_map/pallas_call | solution.py:482
  (37 shorter events, 0.1 us)
Async XLA Ops:
  0.6 20.5 %copy-start.13 = (s32[36]{0:T(128)S(1)}, s32[36]{0:T(128)}, u32[]{:S(2)}) copy-start(s32[36]{0:T(128)} %constant.4.clone.refs_0_) | copy-start | bytes 436
  0.6 20.5 %copy-start = (bf16[8,8,256,128]{3,2,1,0:T(8,128)(2,1)S(1)}, bf16[8,8,256,128]{3,2,1,0:T(8,128)(2,1)}, u32[]{:S(2)}) copy-start(bf16[8,8,256,128]{3,2,1,0:T(8,128)(2,1)} %refs_4_.3) | copy-start | bytes 12582916
  0.7 20.5 %copy-start.10 = (s32[8,8,6]{1,0,2:T(8,128)S(1)}, s32[8,8,6]{1,0,2:T(8,128)}, u32[]{:S(2)}) copy-start(s32[8,8,6]{1,0,2:T(8,128)} %param.17) | copy-start | bytes 4612
  0.7 20.5 %copy-start.11 = (f32[4]{0:T(128)S(1)}, f32[4]{0:T(128)}, u32[]{:S(2)}) copy-start(f32[4]{0:T(128)} %refs_3_.3) | copy-start | bytes 52
  0.7 20.5 %copy-start.9 = (bf16[512,256]{1,0:T(8,128)(2,1)S(1)}, bf16[512,256]{1,0:T(8,128)(2,1)}, u32[]{:S(2)}) copy-start(bf16[512,256]{1,0:T(8,128)(2,1)} %refs_5_.4) | copy-start | bytes 786436
  0.7 20.5 %copy-start.2 = (f32[8,8,3,128]{3,1,2,0:T(8,128)S(1)}, f32[8,8,3,128]{3,1,2,0:T(8,128)}, u32[]{:S(2)}) copy-start(f32[8,8,3,128]{3,1,2,0:T(8,128)} %param.16) | copy-start | bytes 294916
  0.7 20.5 %copy-start.3 = (s32[8,8,128]{2,1,0:T(8,128)S(1)}, s32[8,8,128]{2,1,0:T(8,128)}, u32[]{:S(2)}) copy-start(s32[8,8,128]{2,1,0:T(8,128)} %refs_14_.1) | copy-start | bytes 98308
  0.7 20.5 %copy-start.4 = (s32[8,8,128]{2,1,0:T(8,128)S(1)}, s32[8,8,128]{2,1,0:T(8,128)}, u32[]{:S(2)}) copy-start(s32[8,8,128]{2,1,0:T(8,128)} %refs_15_.1) | copy-start | bytes 98308
  5.3 8.1 %collective-permute-start = (bf16[1200,128]{1,0:T(8,128)(2,1)}, bf16[1200,128]{1,0:T(8,128)(2,1)S(1)}, u32[]{:S(2)}, u32[]{:S(2)}) collective-permute-start(bf16[1200,128]{1,0:T(8,128)(2,1)} %get-tuple-element.15), channel_id=1, source_target_pairs={{0,1},{1,0},{2,3},{3,2},{4,5},{5,4},{6,7},{7,6},{8,9},{9,8},{10,11... | collective-permute-start | bytes 921608 | tf_op jit(solution)/shard_map/ppermute | solution.py:523
  5.8 10.8 %collective-permute-start.1 = (bf16[1200,128]{1,0:T(8,128)(2,1)}, bf16[1200,128]{1,0:T(8,128)(2,1)S(1)}, u32[]{:S(2)}, u32[]{:S(2)}) collective-permute-start(bf16[1200,128]{1,0:T(8,128)(2,1)} %get-tuple-element.16), channel_id=1, source_target_pairs={{1,2},{2,1},{3,4},{4,3},{5,6},{6,5},{7,0},{0,7},{9,10},{10,9},{11,... | collective-permute-start | bytes 921608 | tf_op jit(solution)/shard_map/ppermute | solution.py:523
  9.4 33.8 %collective-permute-start.2 = (bf16[1200,128]{1,0:T(8,128)(2,1)}, bf16[1200,128]{1,0:T(8,128)(2,1)S(1)}, u32[]{:S(2)}, u32[]{:S(2)}) collective-permute-start(bf16[1200,128]{1,0:T(8,128)(2,1)} %get-tuple-element.17), channel_id=1, source_target_pairs={{0,8},{8,0},{16,24},{24,16},{1,9},{9,1},{17,25},{25,17},{2,10},{10... | collective-permute-start | bytes 921608 | tf_op jit(solution)/shard_map/ppermute | solution.py:523
  11.0 32.2 %collective-permute-start.3 = (bf16[1200,128]{1,0:T(8,128)(2,1)}, bf16[1200,128]{1,0:T(8,128)(2,1)S(1)}, u32[]{:S(2)}, u32[]{:S(2)}) collective-permute-start(bf16[1200,128]{1,0:T(8,128)(2,1)} %get-tuple-element.18), channel_id=1, source_target_pairs={{8,16},{16,8},{24,0},{0,24},{9,17},{17,9},{25,1},{1,25},{10,18},{1... | collective-permute-start | bytes 921608 | tf_op jit(solution)/shard_map/ppermute | solution.py:523
  16.7 26.5 %collective-permute-start.4 = (bf16[384,128]{1,0:T(8,128)(2,1)S(1)}, bf16[384,128]{1,0:T(8,128)(2,1)S(1)}, u32[]{:S(2)}, u32[]{:S(2)}) collective-permute-start(bf16[384,128]{1,0:T(8,128)(2,1)S(1)} %get-tuple-element.19), channel_id=1, source_target_pairs={{0,8},{8,0},{16,24},{24,16},{1,9},{9,1},{17,25},{25,17},{2,10},{10... | collective-permute-start | bytes 294920 | tf_op jit(solution)/shard_map/ppermute | solution.py:523
  18.6 24.5 %collective-permute-start.5 = (bf16[384,128]{1,0:T(8,128)(2,1)S(1)}, bf16[384,128]{1,0:T(8,128)(2,1)S(1)}, u32[]{:S(2)}, u32[]{:S(2)}) collective-permute-start(bf16[384,128]{1,0:T(8,128)(2,1)S(1)} %get-tuple-element.20), channel_id=1, source_target_pairs={{8,16},{16,8},{24,0},{0,24},{9,17},{17,9},{25,1},{1,25},{10,18},{1... | collective-permute-start | bytes 294920 | tf_op jit(solution)/shard_map/ppermute | solution.py:523
  22.8 20.4 %copy-start.12 = (s32[28]{0:T(128)S(1)}, s32[28]{0:T(128)}, u32[]{:S(2)}) copy-start(s32[28]{0:T(128)} %constant.5.clone.refs_0_) | copy-start | bytes 340
  43.1 36.0 %copy-start.1 = (bf16[8,8,3,128]{3,1,2,0:T(8,128)(2,1)S(1)}, bf16[8,8,3,128]{3,1,2,0:T(8,128)(2,1)}, u32[]{:S(2)}) copy-start(bf16[8,8,3,128]{3,1,2,0:T(8,128)(2,1)} %param.14) | copy-start | bytes 147460
  43.1 35.9 %copy-start.5 = (f32[1,1,7,128]{3,1,2,0:T(1,128)S(1)}, f32[1,1,7,128]{3,1,2,0:T(1,128)}, u32[]{:S(2)}) copy-start(f32[1,1,7,128]{3,1,2,0:T(1,128)} %param.20) | copy-start | bytes 10756
  43.1 35.9 %copy-start.6 = (f32[1,1,6,128]{3,1,2,0:T(1,128)S(1)}, f32[1,1,6,128]{3,1,2,0:T(1,128)}, u32[]{:S(2)}) copy-start(f32[1,1,6,128]{3,1,2,0:T(1,128)} %param.21) | copy-start | bytes 9220
  43.1 35.9 %copy-start.7 = (f32[1,1,4,128]{3,2,1,0:T(4,128)S(1)}, f32[1,1,4,128]{3,2,1,0:T(4,128)}, u32[]{:S(2)}) copy-start(f32[1,1,4,128]{3,2,1,0:T(4,128)} %refs_5_.5) | copy-start | bytes 6148
  62.7 1.2 %collective-permute-start.6 = (f32[3,8,128]{2,1,0:T(8,128)S(1)}, f32[3,8,128]{2,1,0:T(8,128)S(1)}, u32[]{:S(2)}, u32[]{:S(2)}) collective-permute-start(f32[3,8,128]{2,1,0:T(8,128)S(1)} %get-tuple-element.22), channel_id=1, source_target_pairs={{0,1},{1,0},{2,3},{3,2},{4,5},{5,4},{6,7},{7,6},{8,9},{9,8},{10,11... | collective-permute-start | bytes 36872 | tf_op jit(solution)/shard_map/ppermute | solution.py:523
  63.9 4.2 %collective-permute-start.7 = (f32[2,3,8,128]{3,2,1,0:T(8,128)S(1)}, f32[2,3,8,128]{3,2,1,0:T(8,128)S(1)}, u32[]{:S(2)}, u32[]{:S(2)}) collective-permute-start(f32[2,3,8,128]{3,2,1,0:T(8,128)S(1)} %pad_maximum_fusion.2), channel_id=1, source_target_pairs={{1,2},{2,1},{3,4},{4,3},{5,6},{6,5},{7,0},{0,7},{9,10},{10,9},{11,... | collective-permute-start | bytes 73736 | tf_op jit(solution)/shard_map/ppermute | solution.py:523
  68.1 1.2 %collective-permute-start.8 = (f32[3,8,128]{2,1,0:T(8,128)S(1)}, f32[3,8,128]{2,1,0:T(8,128)S(1)}, u32[]{:S(2)}, u32[]{:S(2)}) collective-permute-start(f32[3,8,128]{2,1,0:T(8,128)S(1)} %get-tuple-element.31), channel_id=1, source_target_pairs={{0,1},{1,0},{2,3},{3,2},{4,5},{5,4},{6,7},{7,6},{8,9},{9,8},{10,11... | collective-permute-start | bytes 36872 | tf_op jit(solution)/shard_map/ppermute | solution.py:523
  69.3 4.0 %collective-permute-start.9 = (f32[3,3,8,128]{3,2,1,0:T(8,128)S(1)}, f32[3,3,8,128]{3,2,1,0:T(8,128)S(1)}, u32[]{:S(2)}, u32[]{:S(2)}) collective-permute-start(f32[3,3,8,128]{3,2,1,0:T(8,128)S(1)} %pad_maximum_fusion.refs_0_), channel_id=1, source_target_pairs={{0,8},{8,0},{16,24},{24,16},{1,9},{9,1},{17,25},{25,17},{2,10},{10... | collective-permute-start | bytes 110600 | tf_op jit(solution)/shard_map/ppermute | solution.py:523
  73.2 5.8 %collective-permute-start.10 = (f32[3,3,8,128]{3,2,1,0:T(8,128)S(1)}, f32[3,3,8,128]{3,2,1,0:T(8,128)S(1)}, u32[]{:S(2)}, u32[]{:S(2)}) collective-permute-start(f32[3,3,8,128]{3,2,1,0:T(8,128)S(1)} %pad_maximum_fusion.1), channel_id=1, source_target_pairs={{8,16},{16,8},{24,0},{0,24},{9,17},{17,9},{25,1},{1,25},{10,18},{1... | collective-permute-start | bytes 110600 | tf_op jit(solution)/shard_map/ppermute | solution.py:523
  (1 other events, 1.7 us)

commit v7 on v6

--- a/solution.py
+++ b/solution.py
@@ -512,6 +512,7 @@
         in_specs=[VMEM] * 2,
         out_specs=[VMEM] * 2,
         compiler_params=pltpu.CompilerParams(vmem_limit_bytes=SMALL),
+        cost_estimate=pl.CostEstimate(flops=8_000_000_000, bytes_accessed=20_000_000, transcendentals=0),
     )(col_a, col_b)
 
 

time: 81.7 us -> 79.9 us (0.978)
  local copies, waits for them, and re-layouts: 1.72 us -> 0.08 us
    unnamed x28, local copies, waits for them, and re-layouts: 1.72 us -> 0.08 us
  transfers between devices with their start and end apart: 11 -> 11, of which waited for: 6 -> 6; matrix products, arithmetic and copies ran while one was open for 0% -> 0% of each run, Pallas kernels for 25% -> 26%
where the time goes in v7:
time: 79.9 us; the launch traced here: 79.8 us
  Pallas kernels  46.8 us (59%)
  starting transfers between devices  16.2 us (20%)
  waiting for transfers between devices  15.9 us (20%)
  between operations  0.85 us (1%)
    pallas_call x2, Pallas kernels, pairs(): pl.pallas_call(lambda *refs: pairs_kernel(strips, halo, shape, *refs), ou...  39.9 us
    ppermute x11, starting transfers between devices, swap(): return lax.ppermute(value, axis, route)  16.2 us
    ppermute x11, waiting for transfers between devices, swap(): return lax.ppermute(value, axis, route)  15.9 us
    pallas_call x1, Pallas kernels, project(): pl.pallas_call(project_kernel, grid=(tx // STEP,), out_shape=[sds(tx, ty,...  4.41 us
    pallas_call x1, Pallas kernels, finish(): pl.pallas_call(lambda *refs: finish_kernel(len(sums), *refs), out_shape=[...  2.45 us
  transfers between devices with their start and end apart: 11, of which 6 were waited for; matrix products, arithmetic and copies ran while one was open for 0% of the time, Pallas kernels for 26%

profile of v7, /device:TPU:0, one launch (start us, length us, event | category | flops | bytes accessed | tf_op | source)
XLA Modules:
  0.0 79.8 jit_solution(16266272927922379059)
XLA Ops:
  0.6 4.4 %shard_map.149 = (bf16[8,8,144,128]{3,2,1,0:T(8,128)(2,1)}, bf16[1200,128]{1,0:T(8,128)(2,1)}, bf16[1200,128]{1,0:T(8,128)(2,1)}, bf16[1200,128]{1,0:T(8,128)(2,1)}, bf16[1200,128]{1,0:T(8,128)(2,1)}) custom-call(bf16[8,8,256,128]{3,2,1,0:T(8,128)(2,1)} %refs_4_.3, bf16[8,3,8,128]{3,2,1,0:T(8,128)(2,1)} %bitcast.30, bf16[128,256]{1,0:T(8,128)(2,1)} %weight_v.1, ...), custom_call_target="tpu_custom_call" | custom-call | tf_op jit(solution)/shard_map/pallas_call | solution.py:116
  5.0 0.5 collective-permute-start
  5.6 3.6 %collective-permute-start.1 = (bf16[1200,128]{1,0:T(8,128)(2,1)}, bf16[1200,128]{1,0:T(8,128)(2,1)S(1)}, u32[]{:S(2)}, u32[]{:S(2)}) collective-permute-start(bf16[1200,128]{1,0:T(8,128)(2,1)} %get-tuple-element.16), channel_id=1, source_target_pairs={{1,2},{2,1},{3,4},{4,3},{5,6},{6,5},{7,0},{0,7},{9,10},{10,9},{11,... | collective-permute-start | bytes 921608 | tf_op jit(solution)/shard_map/ppermute | solution.py:524
  9.1 1.6 %collective-permute-start.2 = (bf16[1200,128]{1,0:T(8,128)(2,1)}, bf16[1200,128]{1,0:T(8,128)(2,1)S(1)}, u32[]{:S(2)}, u32[]{:S(2)}) collective-permute-start(bf16[1200,128]{1,0:T(8,128)(2,1)} %get-tuple-element.17), channel_id=1, source_target_pairs={{0,8},{8,0},{16,24},{24,16},{1,9},{9,1},{17,25},{25,17},{2,10},{10... | collective-permute-start | bytes 921608 | tf_op jit(solution)/shard_map/ppermute | solution.py:524
  10.7 0.0 copy-start.9
  10.7 0.0 copy-start.10
  10.7 0.0 copy-start.13
  10.8 2.5 %collective-permute-start.3 = (bf16[1200,128]{1,0:T(8,128)(2,1)}, bf16[1200,128]{1,0:T(8,128)(2,1)S(1)}, u32[]{:S(2)}, u32[]{:S(2)}) collective-permute-start(bf16[1200,128]{1,0:T(8,128)(2,1)} %get-tuple-element.18), channel_id=1, source_target_pairs={{8,16},{16,8},{24,0},{0,24},{9,17},{17,9},{25,1},{1,25},{10,18},{1... | collective-permute-start | bytes 921608 | tf_op jit(solution)/shard_map/ppermute | solution.py:524
  13.3 3.0 %collective-permute-done.1.col_b.refs_11_.refs_7_ = bf16[1200,128]{1,0:T(8,128)(2,1)S(1)} collective-permute-done((bf16[1200,128]{1,0:T(8,128)(2,1)}, bf16[1200,128]{1,0:T(8,128)(2,1)S(1)}, u32[]{:S(2)}, u32[]{:S(2)}) %collective-permute-start.1) | collective-permute-done | bytes 307232 | tf_op jit(solution)/shard_map/ppermute | solution.py:524
  16.4 2.0 %collective-permute-start.4 = (bf16[384,128]{1,0:T(8,128)(2,1)S(1)}, bf16[384,128]{1,0:T(8,128)(2,1)S(1)}, u32[]{:S(2)}, u32[]{:S(2)}) collective-permute-start(bf16[384,128]{1,0:T(8,128)(2,1)S(1)} %get-tuple-element.19), channel_id=1, source_target_pairs={{0,8},{8,0},{16,24},{24,16},{1,9},{9,1},{17,25},{25,17},{2,10},{10... | collective-permute-start | bytes 294920 | tf_op jit(solution)/shard_map/ppermute | solution.py:524
  18.4 2.5 %collective-permute-start.5 = (bf16[384,128]{1,0:T(8,128)(2,1)S(1)}, bf16[384,128]{1,0:T(8,128)(2,1)S(1)}, u32[]{:S(2)}, u32[]{:S(2)}) collective-permute-start(bf16[384,128]{1,0:T(8,128)(2,1)S(1)} %get-tuple-element.20), channel_id=1, source_target_pairs={{8,16},{16,8},{24,0},{0,24},{9,17},{17,9},{25,1},{1,25},{10,18},{1... | collective-permute-start | bytes 294920 | tf_op jit(solution)/shard_map/ppermute | solution.py:524
  20.9 0.0 copy-start.12
  20.9 20.3 %shard_map.151.refs_16_ = f32[8,128]{1,0:T(8,128)S(1)} custom-call(s32[36]{0:T(128)S(1)} %copy-done.13, s32[6,8,8]{2,1,0:T(8,128)S(1)} %bitcast.42, s32[6,8,8]{2,1,0:T(8,128)S(1)} %bitcast.43, f32[4]{0:T(128)S(1)} %copy-done.11, bf16[8,8,256,128]{3,2,1,0:T(8,128)(2,1)S(1)} %copy-done, bf16[512,256]{1,0:T(8,128)(2,1)S(1)} %copy-done.9, ...), custom_call_target="tpu_custom_call" | custom-call | flops 5400000000 | bytes 3600000 | tf_op jit(solution)/shard_map/pallas_call | solution.py:372
  41.4 19.6 %shard_map.152 = (f32[3,8,128]{2,1,0:T(8,128)S(1)}, f32[3,8,128]{2,1,0:T(8,128)S(1)}, f32[3,8,128]{2,1,0:T(8,128)S(1)}) custom-call(s32[28]{0:T(128)S(1)} %copy-done.12, s32[6,8,8]{2,1,0:T(8,128)S(1)} %bitcast.44, s32[6,8,8]{2,1,0:T(8,128)S(1)} %bitcast.45, f32[4]{0:T(128)S(1)} %copy-done.11, bf16[8,8,256,128]{3,2,1,0:T(8,128)(2,1)S(1)} %copy-done, ...), custom_call_target="tpu_custom_call" | custom-call | flops 4200000000 | bytes 2800000 | tf_op jit(solution)/shard_map/pallas_call | solution.py:372
  60.9 0.1 collective-permute-start.6
  61.0 1.2 %collective-permute-done.6 = f32[3,8,128]{2,1,0:T(8,128)S(1)} collective-permute-done((f32[3,8,128]{2,1,0:T(8,128)S(1)}, f32[3,8,128]{2,1,0:T(8,128)S(1)}, u32[]{:S(2)}, u32[]{:S(2)}) %collective-permute-start.6) | collective-permute-done | bytes 12320 | tf_op jit(solution)/shard_map/ppermute | solution.py:524
  62.2 1.4 %collective-permute-start.7 = (f32[2,3,8,128]{3,2,1,0:T(8,128)S(1)}, f32[2,3,8,128]{3,2,1,0:T(8,128)S(1)}, u32[]{:S(2)}, u32[]{:S(2)}) collective-permute-start(f32[2,3,8,128]{3,2,1,0:T(8,128)S(1)} %pad_maximum_fusion.2), channel_id=1, source_target_pairs={{1,2},{2,1},{3,4},{4,3},{5,6},{6,5},{7,0},{0,7},{9,10},{10,9},{11,... | collective-permute-start | bytes 73736 | tf_op jit(solution)/shard_map/ppermute | solution.py:524
  63.6 2.8 %collective-permute-done.7 = f32[2,3,8,128]{3,2,1,0:T(8,128)S(1)} collective-permute-done((f32[2,3,8,128]{3,2,1,0:T(8,128)S(1)}, f32[2,3,8,128]{3,2,1,0:T(8,128)S(1)}, u32[]{:S(2)}, u32[]{:S(2)}) %collective-permute-start.7) | collective-permute-done | bytes 24608 | tf_op jit(solution)/shard_map/ppermute | solution.py:524
  66.3 1.2 %collective-permute-done.8 = f32[3,8,128]{2,1,0:T(8,128)S(1)} collective-permute-done((f32[3,8,128]{2,1,0:T(8,128)S(1)}, f32[3,8,128]{2,1,0:T(8,128)S(1)}, u32[]{:S(2)}, u32[]{:S(2)}) %collective-permute-start.8) | collective-permute-done | bytes 12320 | tf_op jit(solution)/shard_map/ppermute | solution.py:524
  67.5 0.7 collective-permute-start.9
  68.2 3.3 %collective-permute-done.9.refs_1_ = f32[3,3,8,128]{3,2,1,0:T(8,128)S(1)} collective-permute-done((f32[3,3,8,128]{3,2,1,0:T(8,128)S(1)}, f32[3,3,8,128]{3,2,1,0:T(8,128)S(1)}, u32[]{:S(2)}, u32[]{:S(2)}) %collective-permute-start.9) | collective-permute-done | bytes 36896 | tf_op jit(solution)/shard_map/ppermute | solution.py:524
  71.5 1.4 %collective-permute-start.10 = (f32[3,3,8,128]{3,2,1,0:T(8,128)S(1)}, f32[3,3,8,128]{3,2,1,0:T(8,128)S(1)}, u32[]{:S(2)}, u32[]{:S(2)}) collective-permute-start(f32[3,3,8,128]{3,2,1,0:T(8,128)S(1)} %pad_maximum_fusion.1), channel_id=1, source_target_pairs={{8,16},{16,8},{24,0},{0,24},{9,17},{17,9},{25,1},{1,25},{10,18},{1... | collective-permute-start | bytes 110600 | tf_op jit(solution)/shard_map/ppermute | solution.py:524
  72.9 4.4 %collective-permute-done.10.refs_2_ = f32[3,3,8,128]{3,2,1,0:T(8,128)S(1)} collective-permute-done((f32[3,3,8,128]{3,2,1,0:T(8,128)S(1)}, f32[3,3,8,128]{3,2,1,0:T(8,128)S(1)}, u32[]{:S(2)}, u32[]{:S(2)}) %collective-permute-start.10) | collective-permute-done | bytes 36896 | tf_op jit(solution)/shard_map/ppermute | solution.py:524
  77.3 2.5 %shard_map.153 = (f32[8,3,8,128]{3,2,1,0:T(8,128)}, f32[1,13,1,128]{3,2,1,0:T(1,128)}) custom-call(f32[3,3,8,128]{3,2,1,0:T(8,128)S(1)} %pad_maximum_fusion.refs_0_, f32[3,3,8,128]{3,2,1,0:T(8,128)S(1)} %collective-permute-done.9.refs_1_, f32[3,3,8,128]{3,2,1,0:T(8,128)S(1)} %collective-permute-done.10.refs_2_, f32[1,7,1,128]{3,2,1,0:T(1,128)S(1)} %bitcast.37, ...), custom_call_target="tpu_custom_call" | custom-call | tf_op jit(solution)/shard_map/pallas_call | solution.py:482
  (37 shorter events, 0.1 us)
Async XLA Ops:
  5.0 8.3 %collective-permute-start = (bf16[1200,128]{1,0:T(8,128)(2,1)}, bf16[1200,128]{1,0:T(8,128)(2,1)S(1)}, u32[]{:S(2)}, u32[]{:S(2)}) collective-permute-start(bf16[1200,128]{1,0:T(8,128)(2,1)} %get-tuple-element.15), channel_id=1, source_target_pairs={{0,1},{1,0},{2,3},{3,2},{4,5},{5,4},{6,7},{7,6},{8,9},{9,8},{10,11... | collective-permute-start | bytes 921608 | tf_op jit(solution)/shard_map/ppermute | solution.py:524
  5.6 10.8 %collective-permute-start.1 = (bf16[1200,128]{1,0:T(8,128)(2,1)}, bf16[1200,128]{1,0:T(8,128)(2,1)S(1)}, u32[]{:S(2)}, u32[]{:S(2)}) collective-permute-start(bf16[1200,128]{1,0:T(8,128)(2,1)} %get-tuple-element.16), channel_id=1, source_target_pairs={{1,2},{2,1},{3,4},{4,3},{5,6},{6,5},{7,0},{0,7},{9,10},{10,9},{11,... | collective-permute-start | bytes 921608 | tf_op jit(solution)/shard_map/ppermute | solution.py:524
  9.1 32.2 %collective-permute-start.2 = (bf16[1200,128]{1,0:T(8,128)(2,1)}, bf16[1200,128]{1,0:T(8,128)(2,1)S(1)}, u32[]{:S(2)}, u32[]{:S(2)}) collective-permute-start(bf16[1200,128]{1,0:T(8,128)(2,1)} %get-tuple-element.17), channel_id=1, source_target_pairs={{0,8},{8,0},{16,24},{24,16},{1,9},{9,1},{17,25},{25,17},{2,10},{10... | collective-permute-start | bytes 921608 | tf_op jit(solution)/shard_map/ppermute | solution.py:524
  10.7 10.2 %copy-start = (bf16[8,8,256,128]{3,2,1,0:T(8,128)(2,1)S(1)}, bf16[8,8,256,128]{3,2,1,0:T(8,128)(2,1)}, u32[]{:S(2)}) copy-start(bf16[8,8,256,128]{3,2,1,0:T(8,128)(2,1)} %refs_4_.3) | copy-start | bytes 12582916
  10.7 10.2 %copy-start.2 = (f32[8,8,3,128]{3,1,2,0:T(8,128)S(1)}, f32[8,8,3,128]{3,1,2,0:T(8,128)}, u32[]{:S(2)}) copy-start(f32[8,8,3,128]{3,1,2,0:T(8,128)} %param.16) | copy-start | bytes 294916
  10.7 10.2 %copy-start.3 = (s32[8,8,128]{2,1,0:T(8,128)S(1)}, s32[8,8,128]{2,1,0:T(8,128)}, u32[]{:S(2)}) copy-start(s32[8,8,128]{2,1,0:T(8,128)} %refs_14_.1) | copy-start | bytes 98308
  10.7 10.2 %copy-start.4 = (s32[8,8,128]{2,1,0:T(8,128)S(1)}, s32[8,8,128]{2,1,0:T(8,128)}, u32[]{:S(2)}) copy-start(s32[8,8,128]{2,1,0:T(8,128)} %refs_15_.1) | copy-start | bytes 98308
  10.7 10.2 %copy-start.8 = (bf16[8,8,144,128]{3,2,1,0:T(8,128)(2,1)S(1)}, bf16[8,8,144,128]{3,2,1,0:T(8,128)(2,1)}, u32[]{:S(2)}) copy-start(bf16[8,8,144,128]{3,2,1,0:T(8,128)(2,1)} %get-tuple-element.14) | copy-start | bytes 7077892
  10.7 10.2 %copy-start.9 = (bf16[512,256]{1,0:T(8,128)(2,1)S(1)}, bf16[512,256]{1,0:T(8,128)(2,1)}, u32[]{:S(2)}) copy-start(bf16[512,256]{1,0:T(8,128)(2,1)} %refs_5_.4) | copy-start | bytes 786436
  10.7 10.2 %copy-start.10 = (s32[8,8,6]{1,0,2:T(8,128)S(1)}, s32[8,8,6]{1,0,2:T(8,128)}, u32[]{:S(2)}) copy-start(s32[8,8,6]{1,0,2:T(8,128)} %param.17) | copy-start | bytes 4612
  10.7 10.2 %copy-start.11 = (f32[4]{0:T(128)S(1)}, f32[4]{0:T(128)}, u32[]{:S(2)}) copy-start(f32[4]{0:T(128)} %refs_3_.3) | copy-start | bytes 52
  10.8 30.6 %collective-permute-start.3 = (bf16[1200,128]{1,0:T(8,128)(2,1)}, bf16[1200,128]{1,0:T(8,128)(2,1)S(1)}, u32[]{:S(2)}, u32[]{:S(2)}) collective-permute-start(bf16[1200,128]{1,0:T(8,128)(2,1)} %get-tuple-element.18), channel_id=1, source_target_pairs={{8,16},{16,8},{24,0},{0,24},{9,17},{17,9},{25,1},{1,25},{10,18},{1... | collective-permute-start | bytes 921608 | tf_op jit(solution)/shard_map/ppermute | solution.py:524
  16.4 24.9 %collective-permute-start.4 = (bf16[384,128]{1,0:T(8,128)(2,1)S(1)}, bf16[384,128]{1,0:T(8,128)(2,1)S(1)}, u32[]{:S(2)}, u32[]{:S(2)}) collective-permute-start(bf16[384,128]{1,0:T(8,128)(2,1)S(1)} %get-tuple-element.19), channel_id=1, source_target_pairs={{0,8},{8,0},{16,24},{24,16},{1,9},{9,1},{17,25},{25,17},{2,10},{10... | collective-permute-start | bytes 294920 | tf_op jit(solution)/shard_map/ppermute | solution.py:524
  18.4 23.0 %collective-permute-start.5 = (bf16[384,128]{1,0:T(8,128)(2,1)S(1)}, bf16[384,128]{1,0:T(8,128)(2,1)S(1)}, u32[]{:S(2)}, u32[]{:S(2)}) collective-permute-start(bf16[384,128]{1,0:T(8,128)(2,1)S(1)} %get-tuple-element.20), channel_id=1, source_target_pairs={{8,16},{16,8},{24,0},{0,24},{9,17},{17,9},{25,1},{1,25},{10,18},{1... | collective-permute-start | bytes 294920 | tf_op jit(solution)/shard_map/ppermute | solution.py:524
  20.9 20.4 %copy-start.12 = (s32[28]{0:T(128)S(1)}, s32[28]{0:T(128)}, u32[]{:S(2)}) copy-start(s32[28]{0:T(128)} %constant.5.clone.refs_0_) | copy-start | bytes 340
  41.3 36.0 %copy-start.1 = (bf16[8,8,3,128]{3,1,2,0:T(8,128)(2,1)S(1)}, bf16[8,8,3,128]{3,1,2,0:T(8,128)(2,1)}, u32[]{:S(2)}) copy-start(bf16[8,8,3,128]{3,1,2,0:T(8,128)(2,1)} %param.14) | copy-start | bytes 147460
  41.3 36.0 %copy-start.5 = (f32[1,1,7,128]{3,1,2,0:T(1,128)S(1)}, f32[1,1,7,128]{3,1,2,0:T(1,128)}, u32[]{:S(2)}) copy-start(f32[1,1,7,128]{3,1,2,0:T(1,128)} %param.20) | copy-start | bytes 10756
  41.3 36.0 %copy-start.6 = (f32[1,1,6,128]{3,1,2,0:T(1,128)S(1)}, f32[1,1,6,128]{3,1,2,0:T(1,128)}, u32[]{:S(2)}) copy-start(f32[1,1,6,128]{3,1,2,0:T(1,128)} %param.21) | copy-start | bytes 9220
  41.3 36.0 %copy-start.7 = (f32[1,1,4,128]{3,2,1,0:T(4,128)S(1)}, f32[1,1,4,128]{3,2,1,0:T(4,128)}, u32[]{:S(2)}) copy-start(f32[1,1,4,128]{3,2,1,0:T(4,128)} %refs_5_.5) | copy-start | bytes 6148
  60.9 1.2 %collective-permute-start.6 = (f32[3,8,128]{2,1,0:T(8,128)S(1)}, f32[3,8,128]{2,1,0:T(8,128)S(1)}, u32[]{:S(2)}, u32[]{:S(2)}) collective-permute-start(f32[3,8,128]{2,1,0:T(8,128)S(1)} %get-tuple-element.22), channel_id=1, source_target_pairs={{0,1},{1,0},{2,3},{3,2},{4,5},{5,4},{6,7},{7,6},{8,9},{9,8},{10,11... | collective-permute-start | bytes 36872 | tf_op jit(solution)/shard_map/ppermute | solution.py:524
  62.2 4.2 %collective-permute-start.7 = (f32[2,3,8,128]{3,2,1,0:T(8,128)S(1)}, f32[2,3,8,128]{3,2,1,0:T(8,128)S(1)}, u32[]{:S(2)}, u32[]{:S(2)}) collective-permute-start(f32[2,3,8,128]{3,2,1,0:T(8,128)S(1)} %pad_maximum_fusion.2), channel_id=1, source_target_pairs={{1,2},{2,1},{3,4},{4,3},{5,6},{6,5},{7,0},{0,7},{9,10},{10,9},{11,... | collective-permute-start | bytes 73736 | tf_op jit(solution)/shard_map/ppermute | solution.py:524
  66.3 1.2 %collective-permute-start.8 = (f32[3,8,128]{2,1,0:T(8,128)S(1)}, f32[3,8,128]{2,1,0:T(8,128)S(1)}, u32[]{:S(2)}, u32[]{:S(2)}) collective-permute-start(f32[3,8,128]{2,1,0:T(8,128)S(1)} %get-tuple-element.31), channel_id=1, source_target_pairs={{0,1},{1,0},{2,3},{3,2},{4,5},{5,4},{6,7},{7,6},{8,9},{9,8},{10,11... | collective-permute-start | bytes 36872 | tf_op jit(solution)/shard_map/ppermute | solution.py:524
  67.5 4.0 %collective-permute-start.9 = (f32[3,3,8,128]{3,2,1,0:T(8,128)S(1)}, f32[3,3,8,128]{3,2,1,0:T(8,128)S(1)}, u32[]{:S(2)}, u32[]{:S(2)}) collective-permute-start(f32[3,3,8,128]{3,2,1,0:T(8,128)S(1)} %pad_maximum_fusion.refs_0_), channel_id=1, source_target_pairs={{0,8},{8,0},{16,24},{24,16},{1,9},{9,1},{17,25},{25,17},{2,10},{10... | collective-permute-start | bytes 110600 | tf_op jit(solution)/shard_map/ppermute | solution.py:524
  71.5 5.8 %collective-permute-start.10 = (f32[3,3,8,128]{3,2,1,0:T(8,128)S(1)}, f32[3,3,8,128]{3,2,1,0:T(8,128)S(1)}, u32[]{:S(2)}, u32[]{:S(2)}) collective-permute-start(f32[3,3,8,128]{3,2,1,0:T(8,128)S(1)} %pad_maximum_fusion.1), channel_id=1, source_target_pairs={{8,16},{16,8},{24,0},{0,24},{9,17},{17,9},{25,1},{1,25},{10,18},{1... | collective-permute-start | bytes 110600 | tf_op jit(solution)/shard_map/ppermute | solution.py:524
  (1 other events, 10.2 us)

commit v8 on v7

--- a/solution.py
+++ b/solution.py
@@ -48,7 +48,7 @@
     return first, second, (rest - second.astype(F32)).astype(BF16)
 
 
-def project_kernel(feat, pos, weight_v, pose, motion, inverse, own, col_in, col_out, row_in, row_out):
+def project_kernel(feat, pos, weight_v, pose, motion, inverse, own, col_in, ends_out, col_out, row_in, row_out):
     x = pl.program_id(0)
     tiles_x, tiles_y, beads = pl.num_programs(0), feat.shape[1], feat.shape[3]
     rows = beads + EXTRA
@@ -79,6 +79,8 @@
 
     @pl.when(x == 0)
     def _():
+        ends_out[0:rows, :] = jnp.where(high_y, own[0, tiles_y - 1], own[0, 0])
+
         @pl.when(high_x)
         def _():
             put(row_in, 0)
@@ -89,6 +91,8 @@
 
     @pl.when(x == tiles_x - 1)
     def _():
+        ends_out[rows : 2 * rows, :] = jnp.where(high_y, own[step - 1, tiles_y - 1], own[step - 1, 0])
+
         @pl.when(high_x)
         def _():
             put(row_out, step - 1)
@@ -103,7 +107,7 @@
             [pose[0, r] for r in range(3, 7)] + [motion[0, r] for r in range(6)]
             + [inverse[0, 0, r : r + 1, :] for r in range(4)] + [jnp.zeros((2, beads), F32)], axis=0)
         body = jnp.concatenate(split_three(body), axis=0)
-        for message in (col_in, col_out, row_in, row_out):
+        for message in (col_in, ends_out, row_in, row_out):
             message[message.shape[0] - BODY :, :] = body
 
 
@@ -112,11 +116,11 @@
     rows = beads + EXTRA
     whole = lambda s: pl.BlockSpec(s, lambda i: (0,) * len(s))
     sds = lambda *s: jax.ShapeDtypeStruct(s, BF16)
-    col, line = (tx * rows + BODY, beads), (ty * rows + BODY, beads)
+    col, line, end = (tx * rows + BODY, beads), (ty * rows + BODY, beads), (2 * rows + BODY, beads)
     return pl.pallas_call(
         project_kernel,
         grid=(tx // STEP,),
-        out_shape=[sds(tx, ty, rows, beads), sds(*col), sds(*col), sds(*line), sds(*line)],
+        out_shape=[sds(tx, ty, rows, beads), sds(*col), sds(*end), sds(tx * rows, beads), sds(*line), sds(*line)],
         in_specs=[
             pl.BlockSpec((STEP, ty, f, beads), lambda i: (i, 0, 0, 0)),
             pl.BlockSpec((STEP, 3, ty, beads), lambda i: (i, 0, 0, 0)),
@@ -124,7 +128,7 @@
         ],
         out_specs=[
             pl.BlockSpec((STEP, ty, rows, beads), lambda i: (i, 0, 0, 0)),
-            whole(col), whole(col), whole(line), whole(line),
+            whole(col), whole(end), whole((tx * rows, beads)), whole(line), whole(line),
         ],
         compiler_params=pltpu.CompilerParams(vmem_limit_bytes=LIMIT),
     )(features, pos, weight_v, pose, motion, inverse)
@@ -155,15 +159,16 @@
         line = lambda i: vp.at[pl.ds(i * wide + 1, ty)]
         cols, lines, ends = around[0:2], around[2:4], around[4:6]
         pairs_of = []
-        for i in range(tx):
-            for col, y in zip(cols, (y_in, y_out)):
-                pairs_of.append((col.at[pl.ds(i * rows, rows)], vp.at[(i + 1) * wide + y]))
-            pairs_of.append((own.at[i * ty : (i + 1) * ty], line(i + 1)))
         for src, end, x in zip(lines, ends, (x_in, x_out)):
             for y in range(ty):
                 pairs_of.append((src.at[pl.ds(y * rows, rows)], vp.at[x * wide + 1 + y]))
             pairs_of.append((end.at[pl.ds(0, rows)], vp.at[x * wide + y_in]))
             pairs_of.append((end.at[pl.ds(rows, rows)], vp.at[x * wide + y_out]))
+        for i in range(tx):
+            for col, y in zip(cols, (y_in, y_out)):
+                pairs_of.append((col.at[pl.ds(i * rows, rows)], vp.at[(i + 1) * wide + y]))
+            pairs_of.append((own.at[i * ty : (i + 1) * ty], line(i + 1)))
+        early = 2 * (ty + 2) + 6
         copies = [pltpu.make_async_copy(src, dst, vsem.at[q]) for q, (src, dst) in enumerate(pairs_of)]
         for copy in copies:
             copy.start()
@@ -304,10 +309,13 @@
     make_u(0, sets[0][0])
     make_u(min(1, last), sets[1][0])
     if halo:
-        for copy in copies:
+        for copy in copies[:early]:
             copy.wait()
     tables.wait()
     fill(0, sets[0])
+    if halo:
+        for copy in copies[early:]:
+            copy.wait()
 
     def body(g, carry):
         half(2 * g, sets[0], sets[1])
@@ -493,12 +501,12 @@
     rows = (end_in.shape[0] - 2 * BODY) // 2
     last = col_a.shape[0] - BODY - rows
     high = outward("gx")
-    for q, col in enumerate((col_a, col_b)):
+    for q, (col, last) in enumerate(((col_a, last), (col_b, rows))):
         first, final = col[0:rows, :], col[last : last + rows, :]
         end_in[q * rows : (q + 1) * rows, :] = jnp.where(high, first, final)
         end_out[q * rows : (q + 1) * rows, :] = jnp.where(high, final, first)
     for q, col in enumerate((col_a, col_b)):
-        body = col[last + rows :, :]
+        body = col[col.shape[0] - BODY :, :]
         at = 2 * rows + q * BODY
         end_in[at : at + BODY, :] = body
         end_out[at : at + BODY, :] = body
@@ -540,10 +548,11 @@
     pos, lever = (jnp.transpose(v, (0, 2, 1, 3)) for v in (positions, lever))
     pose, motion = (jnp.transpose(v, (0, 2, 1, 3)) for v in (body_pose, body_motion))
     codes = jnp.transpose(partner, (2, 0, 1))
-    own, col_in, col_out, row_in, row_out = project(features, pos, weight_v, pose, motion, body_inverse)
+    own, col_in, ends_out, col_out, row_in, row_out = project(features, pos, weight_v, pose, motion, body_inverse)
     line_a, line_b = inside(row_in, "gx"), outside(row_out, "gx")
-    col_a, col_b = inside(col_in, "gy"), outside(col_out, "gy")
-    end_in, end_out = corners(col_a, col_b, rows)
+    col_a, ends_b = inside(col_in, "gy"), outside(ends_out, "gy")
+    col_b = outside(col_out, "gy")
+    end_in, end_out = corners(col_a, ends_b, rows)
     end_a, end_b = inside(end_in, "gx"), outside(end_out, "gx")
     args = (codes, radial_rate, features, weight_u, lever, body_slot, owner_dir, slots)
     inner = [((i,), range(1, ty - 1)) for i in range(1, tx - 1)]
@@ -563,7 +572,7 @@
         got = outside(jnp.stack([cols[2], mine]), "gx")
         mine = mine + got[0]
         sums = [jnp.stack([inside(mine, "gx"), mine, got[1] + cols[2]])]
-    moved, state = finish(sums, pose, motion, body_inverse, (col_a, col_b), (line_a, line_b), (end_a, end_b),
+    moved, state = finish(sums, pose, motion, body_inverse, (col_a, ends_b), (line_a, line_b), (end_a, end_b),
                           pos, lever, body_slot, owner_dir)
     return (jnp.transpose(moved, (0, 2, 1, 3)), jnp.transpose(state, (0, 2, 1, 3)))
 

time: 79.9 us -> 75.7 us (0.947)
  waiting for transfers between devices: 15.9 us -> 11.9 us
    ppermute x11 -> x12, waiting for transfers between devices: 15.9 us -> 11.9 us  [swap(): return lax.ppermute(value, axis, route)]
    ppermute x11 -> x12, starting transfers between devices: 16.2 us -> 15.8 us  [swap(): return lax.ppermute(value, axis, route)]
  transfers between devices with their start and end apart: 11 -> 12, of which waited for: 6 -> 5; matrix products, arithmetic and copies ran while one was open for 0% -> 0% of each run, Pallas kernels for 26% -> 27%
where the time goes in v8:
time: 75.7 us; the launch traced here: 75.6 us
  Pallas kernels  46.9 us (62%)
  starting transfers between devices  15.8 us (21%)
  waiting for transfers between devices  11.9 us (16%)
  between operations  0.86 us (1%)
    pallas_call x2, Pallas kernels, pairs(): pl.pallas_call(lambda *refs: pairs_kernel(strips, halo, shape, *refs), ou...  39.9 us
    ppermute x12, starting transfers between devices, swap(): return lax.ppermute(value, axis, route)  15.8 us
    ppermute x12, waiting for transfers between devices, swap(): return lax.ppermute(value, axis, route)  11.9 us
    pallas_call x1, Pallas kernels, project(): pl.pallas_call(project_kernel, grid=(tx // STEP,), out_shape=[sds(tx, ty,...  4.44 us
    pallas_call x1, Pallas kernels, finish(): pl.pallas_call(lambda *refs: finish_kernel(len(sums), *refs), out_shape=[...  2.45 us
  transfers between devices with their start and end apart: 12, of which 5 were waited for; matrix products, arithmetic and copies ran while one was open for 0% of the time, Pallas kernels for 27%

profile of v8, /device:TPU:0, one launch (start us, length us, event | category | flops | bytes accessed | tf_op | source)
XLA Modules:
  0.0 75.6 jit_solution(8699532510728842035)
XLA Ops:
  0.6 4.4 %shard_map.149 = (bf16[8,8,144,128]{3,2,1,0:T(8,128)(2,1)}, bf16[1200,128]{1,0:T(8,128)(2,1)}, bf16[336,128]{1,0:T(8,128)(2,1)}, bf16[1152,128]{1,0:T(8,128)(2,1...) custom-call(bf16[8,8,256,128]{3,2,1,0:T(8,128)(2,1)} %refs_4_.3, bf16[8,3,8,128]{3,2,1,0:T(8,128)(2,1)} %bitcast.30, ...), custom_call_target="tpu_custom_call" | custom-call | tf_op jit(solution)/shard_map/pallas_call | solution.py:120
  5.1 0.5 collective-permute-start
  5.6 3.6 %collective-permute-start.4 = (bf16[336,128]{1,0:T(8,128)(2,1)}, bf16[336,128]{1,0:T(8,128)(2,1)S(1)}, u32[]{:S(2)}, u32[]{:S(2)}) collective-permute-start(bf16[336,128]{1,0:T(8,128)(2,1)} %get-tuple-element.20), channel_id=1, source_target_pairs={{1,2},{2,1},{3,4},{4,3},{5,6},{6,5},{7,0},{0,7},{9,10},{10,9},{11,... | collective-permute-start | bytes 258056 | tf_op jit(solution)/shard_map/ppermute | solution.py:532
  9.1 0.0 collective-permute-start.1
  9.2 1.7 %collective-permute-start.2 = (bf16[1200,128]{1,0:T(8,128)(2,1)}, bf16[1200,128]{1,0:T(8,128)(2,1)S(1)}, u32[]{:S(2)}, u32[]{:S(2)}) collective-permute-start(bf16[1200,128]{1,0:T(8,128)(2,1)} %get-tuple-element.18), channel_id=1, source_target_pairs={{0,8},{8,0},{16,24},{24,16},{1,9},{9,1},{17,25},{25,17},{2,10},{10... | collective-permute-start | bytes 921608 | tf_op jit(solution)/shard_map/ppermute | solution.py:532
  10.9 0.0 copy-start.9
  10.9 0.0 copy-start.10
  10.9 0.0 copy-start.13
  10.9 2.5 %collective-permute-start.3 = (bf16[1200,128]{1,0:T(8,128)(2,1)}, bf16[1200,128]{1,0:T(8,128)(2,1)S(1)}, u32[]{:S(2)}, u32[]{:S(2)}) collective-permute-start(bf16[1200,128]{1,0:T(8,128)(2,1)} %get-tuple-element.19), channel_id=1, source_target_pairs={{8,16},{16,8},{24,0},{0,24},{9,17},{17,9},{25,1},{1,25},{10,18},{1... | collective-permute-start | bytes 921608 | tf_op jit(solution)/shard_map/ppermute | solution.py:532
  13.5 0.7 collective-permute-start.5
  14.3 2.3 %collective-permute-start.6 = (bf16[384,128]{1,0:T(8,128)(2,1)S(1)}, bf16[384,128]{1,0:T(8,128)(2,1)S(1)}, u32[]{:S(2)}, u32[]{:S(2)}) collective-permute-start(bf16[384,128]{1,0:T(8,128)(2,1)S(1)} %get-tuple-element.22), channel_id=1, source_target_pairs={{8,16},{16,8},{24,0},{0,24},{9,17},{17,9},{25,1},{1,25},{10,18},{1... | collective-permute-start | bytes 294920 | tf_op jit(solution)/shard_map/ppermute | solution.py:532
  16.7 0.0 copy-start.12
  16.7 20.4 %shard_map.151.refs_16_ = f32[8,128]{1,0:T(8,128)S(1)} custom-call(s32[36]{0:T(128)S(1)} %copy-done.13, s32[6,8,8]{2,1,0:T(8,128)S(1)} %bitcast.42, s32[6,8,8]{2,1,0:T(8,128)S(1)} %bitcast.43, f32[4]{0:T(128)S(1)} %copy-done.11, bf16[8,8,256,128]{3,2,1,0:T(8,128)(2,1)S(1)} %copy-done, bf16[512,256]{1,0:T(8,128)(2,1)S(1)} %copy-done.9, ...), custom_call_target="tpu_custom_call" | custom-call | flops 5400000000 | bytes 3600000 | tf_op jit(solution)/shard_map/pallas_call | solution.py:380
  37.2 19.5 %shard_map.152 = (f32[3,8,128]{2,1,0:T(8,128)S(1)}, f32[3,8,128]{2,1,0:T(8,128)S(1)}, f32[3,8,128]{2,1,0:T(8,128)S(1)}) custom-call(s32[28]{0:T(128)S(1)} %copy-done.12, s32[6,8,8]{2,1,0:T(8,128)S(1)} %bitcast.44, s32[6,8,8]{2,1,0:T(8,128)S(1)} %bitcast.45, f32[4]{0:T(128)S(1)} %copy-done.11, bf16[8,8,256,128]{3,2,1,0:T(8,128)(2,1)S(1)} %copy-done, ...), custom_call_target="tpu_custom_call" | custom-call | flops 4200000000 | bytes 2800000 | tf_op jit(solution)/shard_map/pallas_call | solution.py:380
  56.7 0.1 collective-permute-start.7
  56.8 1.2 %collective-permute-done.7 = f32[3,8,128]{2,1,0:T(8,128)S(1)} collective-permute-done((f32[3,8,128]{2,1,0:T(8,128)S(1)}, f32[3,8,128]{2,1,0:T(8,128)S(1)}, u32[]{:S(2)}, u32[]{:S(2)}) %collective-permute-start.7) | collective-permute-done | bytes 12320 | tf_op jit(solution)/shard_map/ppermute | solution.py:532
  58.0 2.1 %collective-permute-start.8 = (f32[2,3,8,128]{3,2,1,0:T(8,128)S(1)}, f32[2,3,8,128]{3,2,1,0:T(8,128)S(1)}, u32[]{:S(2)}, u32[]{:S(2)}) collective-permute-start(f32[2,3,8,128]{3,2,1,0:T(8,128)S(1)} %pad_maximum_fusion.2), channel_id=1, source_target_pairs={{1,2},{2,1},{3,4},{4,3},{5,6},{6,5},{7,0},{0,7},{9,10},{10,9},{11,... | collective-permute-start | bytes 73736 | tf_op jit(solution)/shard_map/ppermute | solution.py:532
  60.1 2.0 %collective-permute-done.8 = f32[2,3,8,128]{3,2,1,0:T(8,128)S(1)} collective-permute-done((f32[2,3,8,128]{3,2,1,0:T(8,128)S(1)}, f32[2,3,8,128]{3,2,1,0:T(8,128)S(1)}, u32[]{:S(2)}, u32[]{:S(2)}) %collective-permute-start.8) | collective-permute-done | bytes 24608 | tf_op jit(solution)/shard_map/ppermute | solution.py:532
  62.2 1.2 %collective-permute-done.9 = f32[3,8,128]{2,1,0:T(8,128)S(1)} collective-permute-done((f32[3,8,128]{2,1,0:T(8,128)S(1)}, f32[3,8,128]{2,1,0:T(8,128)S(1)}, u32[]{:S(2)}, u32[]{:S(2)}) %collective-permute-start.9) | collective-permute-done | bytes 12320 | tf_op jit(solution)/shard_map/ppermute | solution.py:532
  63.3 0.6 collective-permute-start.10
  64.0 3.3 %collective-permute-done.10.refs_1_ = f32[3,3,8,128]{3,2,1,0:T(8,128)S(1)} collective-permute-done((f32[3,3,8,128]{3,2,1,0:T(8,128)S(1)}, f32[3,3,8,128]{3,2,1,0:T(8,128)S(1)}, u32[]{:S(2)}, u32[]{:S(2)}) %collective-permute-start.10) | collective-permute-done | bytes 36896 | tf_op jit(solution)/shard_map/ppermute | solution.py:532
  67.3 1.6 %collective-permute-start.11 = (f32[3,3,8,128]{3,2,1,0:T(8,128)S(1)}, f32[3,3,8,128]{3,2,1,0:T(8,128)S(1)}, u32[]{:S(2)}, u32[]{:S(2)}) collective-permute-start(f32[3,3,8,128]{3,2,1,0:T(8,128)S(1)} %pad_maximum_fusion.1), channel_id=1, source_target_pairs={{8,16},{16,8},{24,0},{0,24},{9,17},{17,9},{25,1},{1,25},{10,18},{1... | collective-permute-start | bytes 110600 | tf_op jit(solution)/shard_map/ppermute | solution.py:532
  68.9 4.2 %collective-permute-done.11.refs_2_ = f32[3,3,8,128]{3,2,1,0:T(8,128)S(1)} collective-permute-done((f32[3,3,8,128]{3,2,1,0:T(8,128)S(1)}, f32[3,3,8,128]{3,2,1,0:T(8,128)S(1)}, u32[]{:S(2)}, u32[]{:S(2)}) %collective-permute-start.11) | collective-permute-done | bytes 36896 | tf_op jit(solution)/shard_map/ppermute | solution.py:532
  73.1 2.5 %shard_map.153 = (f32[8,3,8,128]{3,2,1,0:T(8,128)}, f32[1,13,1,128]{3,2,1,0:T(1,128)}) custom-call(f32[3,3,8,128]{3,2,1,0:T(8,128)S(1)} %pad_maximum_fusion.refs_0_, f32[3,3,8,128]{3,2,1,0:T(8,128)S(1)} %collective-permute-done.10.refs_1_, f32[3,3,8,128]{3,2,1,0:T(8,128)S(1)} %collective-permute-done.11.refs_2_, f32[1,7,1,128]{3,2,1,0:T(1,128)S(1)} %bitcast.37, ...), custom_call_target="tpu_custom_call" | custom-call | tf_op jit(solution)/shard_map/pallas_call | solution.py:490
  (39 shorter events, 0.1 us)
Async XLA Ops:
  5.1 8.4 %collective-permute-start = (bf16[1200,128]{1,0:T(8,128)(2,1)}, bf16[1200,128]{1,0:T(8,128)(2,1)S(1)}, u32[]{:S(2)}, u32[]{:S(2)}) collective-permute-start(bf16[1200,128]{1,0:T(8,128)(2,1)} %get-tuple-element.16), channel_id=1, source_target_pairs={{0,1},{1,0},{2,3},{3,2},{4,5},{5,4},{6,7},{7,6},{8,9},{9,8},{10,11... | collective-permute-start | bytes 921608 | tf_op jit(solution)/shard_map/ppermute | solution.py:532
  5.6 7.9 %collective-permute-start.4 = (bf16[336,128]{1,0:T(8,128)(2,1)}, bf16[336,128]{1,0:T(8,128)(2,1)S(1)}, u32[]{:S(2)}, u32[]{:S(2)}) collective-permute-start(bf16[336,128]{1,0:T(8,128)(2,1)} %get-tuple-element.20), channel_id=1, source_target_pairs={{1,2},{2,1},{3,4},{4,3},{5,6},{6,5},{7,0},{0,7},{9,10},{10,9},{11,... | collective-permute-start | bytes 258056 | tf_op jit(solution)/shard_map/ppermute | solution.py:532
  9.1 28.0 %collective-permute-start.1 = (bf16[1152,128]{1,0:T(8,128)(2,1)}, bf16[1152,128]{1,0:T(8,128)(2,1)S(1)}, u32[]{:S(2)}, u32[]{:S(2)}) collective-permute-start(bf16[1152,128]{1,0:T(8,128)(2,1)} %get-tuple-element.17), channel_id=1, source_target_pairs={{1,2},{2,1},{3,4},{4,3},{5,6},{6,5},{7,0},{0,7},{9,10},{10,9},{11,... | collective-permute-start | bytes 884744 | tf_op jit(solution)/shard_map/ppermute | solution.py:532
  9.2 28.0 %collective-permute-start.2 = (bf16[1200,128]{1,0:T(8,128)(2,1)}, bf16[1200,128]{1,0:T(8,128)(2,1)S(1)}, u32[]{:S(2)}, u32[]{:S(2)}) collective-permute-start(bf16[1200,128]{1,0:T(8,128)(2,1)} %get-tuple-element.18), channel_id=1, source_target_pairs={{0,8},{8,0},{16,24},{24,16},{1,9},{9,1},{17,25},{25,17},{2,10},{10... | collective-permute-start | bytes 921608 | tf_op jit(solution)/shard_map/ppermute | solution.py:532
  10.9 5.7 %copy-start = (bf16[8,8,256,128]{3,2,1,0:T(8,128)(2,1)S(1)}, bf16[8,8,256,128]{3,2,1,0:T(8,128)(2,1)}, u32[]{:S(2)}) copy-start(bf16[8,8,256,128]{3,2,1,0:T(8,128)(2,1)} %refs_4_.3) | copy-start | bytes 12582916
  10.9 5.7 %copy-start.2 = (f32[8,8,3,128]{3,1,2,0:T(8,128)S(1)}, f32[8,8,3,128]{3,1,2,0:T(8,128)}, u32[]{:S(2)}) copy-start(f32[8,8,3,128]{3,1,2,0:T(8,128)} %param.16) | copy-start | bytes 294916
  10.9 5.7 %copy-start.3 = (s32[8,8,128]{2,1,0:T(8,128)S(1)}, s32[8,8,128]{2,1,0:T(8,128)}, u32[]{:S(2)}) copy-start(s32[8,8,128]{2,1,0:T(8,128)} %refs_14_.1) | copy-start | bytes 98308
  10.9 5.7 %copy-start.4 = (s32[8,8,128]{2,1,0:T(8,128)S(1)}, s32[8,8,128]{2,1,0:T(8,128)}, u32[]{:S(2)}) copy-start(s32[8,8,128]{2,1,0:T(8,128)} %refs_15_.1) | copy-start | bytes 98308
  10.9 5.7 %copy-start.8 = (bf16[8,8,144,128]{3,2,1,0:T(8,128)(2,1)S(1)}, bf16[8,8,144,128]{3,2,1,0:T(8,128)(2,1)}, u32[]{:S(2)}) copy-start(bf16[8,8,144,128]{3,2,1,0:T(8,128)(2,1)} %get-tuple-element.15) | copy-start | bytes 7077892
  10.9 5.7 %copy-start.9 = (bf16[512,256]{1,0:T(8,128)(2,1)S(1)}, bf16[512,256]{1,0:T(8,128)(2,1)}, u32[]{:S(2)}) copy-start(bf16[512,256]{1,0:T(8,128)(2,1)} %refs_5_.4) | copy-start | bytes 786436
  10.9 5.7 %copy-start.10 = (s32[8,8,6]{1,0,2:T(8,128)S(1)}, s32[8,8,6]{1,0,2:T(8,128)}, u32[]{:S(2)}) copy-start(s32[8,8,6]{1,0,2:T(8,128)} %param.17) | copy-start | bytes 4612
  10.9 26.2 %collective-permute-start.3 = (bf16[1200,128]{1,0:T(8,128)(2,1)}, bf16[1200,128]{1,0:T(8,128)(2,1)S(1)}, u32[]{:S(2)}, u32[]{:S(2)}) collective-permute-start(bf16[1200,128]{1,0:T(8,128)(2,1)} %get-tuple-element.19), channel_id=1, source_target_pairs={{8,16},{16,8},{24,0},{0,24},{9,17},{17,9},{25,1},{1,25},{10,18},{1... | collective-permute-start | bytes 921608 | tf_op jit(solution)/shard_map/ppermute | solution.py:532
  13.5 23.6 %collective-permute-start.5 = (bf16[384,128]{1,0:T(8,128)(2,1)S(1)}, bf16[384,128]{1,0:T(8,128)(2,1)S(1)}, u32[]{:S(2)}, u32[]{:S(2)}) collective-permute-start(bf16[384,128]{1,0:T(8,128)(2,1)S(1)} %get-tuple-element.21), channel_id=1, source_target_pairs={{0,8},{8,0},{16,24},{24,16},{1,9},{9,1},{17,25},{25,17},{2,10},{10... | collective-permute-start | bytes 294920 | tf_op jit(solution)/shard_map/ppermute | solution.py:532
  14.3 22.9 %collective-permute-start.6 = (bf16[384,128]{1,0:T(8,128)(2,1)S(1)}, bf16[384,128]{1,0:T(8,128)(2,1)S(1)}, u32[]{:S(2)}, u32[]{:S(2)}) collective-permute-start(bf16[384,128]{1,0:T(8,128)(2,1)S(1)} %get-tuple-element.22), channel_id=1, source_target_pairs={{8,16},{16,8},{24,0},{0,24},{9,17},{17,9},{25,1},{1,25},{10,18},{1... | collective-permute-start | bytes 294920 | tf_op jit(solution)/shard_map/ppermute | solution.py:532
  16.7 20.5 %copy-start.12 = (s32[28]{0:T(128)S(1)}, s32[28]{0:T(128)}, u32[]{:S(2)}) copy-start(s32[28]{0:T(128)} %constant.5.clone.refs_0_) | copy-start | bytes 340
  37.1 36.1 %copy-start.1 = (bf16[8,8,3,128]{3,1,2,0:T(8,128)(2,1)S(1)}, bf16[8,8,3,128]{3,1,2,0:T(8,128)(2,1)}, u32[]{:S(2)}) copy-start(bf16[8,8,3,128]{3,1,2,0:T(8,128)(2,1)} %param.14) | copy-start | bytes 147460
  37.1 36.0 %copy-start.5 = (f32[1,1,7,128]{3,1,2,0:T(1,128)S(1)}, f32[1,1,7,128]{3,1,2,0:T(1,128)}, u32[]{:S(2)}) copy-start(f32[1,1,7,128]{3,1,2,0:T(1,128)} %param.20) | copy-start | bytes 10756
  37.1 36.0 %copy-start.6 = (f32[1,1,6,128]{3,1,2,0:T(1,128)S(1)}, f32[1,1,6,128]{3,1,2,0:T(1,128)}, u32[]{:S(2)}) copy-start(f32[1,1,6,128]{3,1,2,0:T(1,128)} %param.21) | copy-start | bytes 9220
  37.1 36.0 %copy-start.7 = (f32[1,1,4,128]{3,2,1,0:T(4,128)S(1)}, f32[1,1,4,128]{3,2,1,0:T(4,128)}, u32[]{:S(2)}) copy-start(f32[1,1,4,128]{3,2,1,0:T(4,128)} %refs_5_.5) | copy-start | bytes 6148
  56.7 1.2 %collective-permute-start.7 = (f32[3,8,128]{2,1,0:T(8,128)S(1)}, f32[3,8,128]{2,1,0:T(8,128)S(1)}, u32[]{:S(2)}, u32[]{:S(2)}) collective-permute-start(f32[3,8,128]{2,1,0:T(8,128)S(1)} %get-tuple-element.24), channel_id=1, source_target_pairs={{0,1},{1,0},{2,3},{3,2},{4,5},{5,4},{6,7},{7,6},{8,9},{9,8},{10,11... | collective-permute-start | bytes 36872 | tf_op jit(solution)/shard_map/ppermute | solution.py:532
  58.0 4.2 %collective-permute-start.8 = (f32[2,3,8,128]{3,2,1,0:T(8,128)S(1)}, f32[2,3,8,128]{3,2,1,0:T(8,128)S(1)}, u32[]{:S(2)}, u32[]{:S(2)}) collective-permute-start(f32[2,3,8,128]{3,2,1,0:T(8,128)S(1)} %pad_maximum_fusion.2), channel_id=1, source_target_pairs={{1,2},{2,1},{3,4},{4,3},{5,6},{6,5},{7,0},{0,7},{9,10},{10,9},{11,... | collective-permute-start | bytes 73736 | tf_op jit(solution)/shard_map/ppermute | solution.py:532
  62.1 1.2 %collective-permute-start.9 = (f32[3,8,128]{2,1,0:T(8,128)S(1)}, f32[3,8,128]{2,1,0:T(8,128)S(1)}, u32[]{:S(2)}, u32[]{:S(2)}) collective-permute-start(f32[3,8,128]{2,1,0:T(8,128)S(1)} %get-tuple-element.33), channel_id=1, source_target_pairs={{0,1},{1,0},{2,3},{3,2},{4,5},{5,4},{6,7},{7,6},{8,9},{9,8},{10,11... | collective-permute-start | bytes 36872 | tf_op jit(solution)/shard_map/ppermute | solution.py:532
  63.3 4.0 %collective-permute-start.10 = (f32[3,3,8,128]{3,2,1,0:T(8,128)S(1)}, f32[3,3,8,128]{3,2,1,0:T(8,128)S(1)}, u32[]{:S(2)}, u32[]{:S(2)}) collective-permute-start(f32[3,3,8,128]{3,2,1,0:T(8,128)S(1)} %pad_maximum_fusion.refs_0_), channel_id=1, source_target_pairs={{0,8},{8,0},{16,24},{24,16},{1,9},{9,1},{17,25},{25,17},{2,10},{10... | collective-permute-start | bytes 110600 | tf_op jit(solution)/shard_map/ppermute | solution.py:532
  67.3 5.8 %collective-permute-start.11 = (f32[3,3,8,128]{3,2,1,0:T(8,128)S(1)}, f32[3,3,8,128]{3,2,1,0:T(8,128)S(1)}, u32[]{:S(2)}, u32[]{:S(2)}) collective-permute-start(f32[3,3,8,128]{3,2,1,0:T(8,128)S(1)} %pad_maximum_fusion.1), channel_id=1, source_target_pairs={{8,16},{16,8},{24,0},{0,24},{9,17},{17,9},{25,1},{1,25},{10,18},{1... | collective-permute-start | bytes 110600 | tf_op jit(solution)/shard_map/ppermute | solution.py:532
  (2 other events, 11.5 us)
